TPU v7x, 32 devices: a whole 2x2x4 slice. The times are simulated.
32 devices in a mesh: grp: 2 (over y), row: 4 (over x, core), col: 4 (over z).
Axes of the slice: x: 2, y: 2, z: 4, core: 2. Of those that a mesh axis runs over, the one named last changes fastest.
Arguments:
- left_factors: bfloat16 [8, 48, 32, 128], P(('grp', 'row'), 'col'), parts along dimension 0, may hold values from -6 to 6
- right_factors: bfloat16 [8, 48, 32, 128], P(('grp', 'col'), 'row'), parts along dimension 0, may hold values from -6 to 6
- out_weight: bfloat16 [1024, 128], replicated, may hold values from -2 to 2
- out_bias: float32 [128], replicated, may hold values from -4 to 4
- pair_grad: bfloat16 [384, 192, 128], P(('grp', 'row'), 'col'), parts along dimension 0, may hold values from -6 to 6
Outputs:
- pair_update: bfloat16 [384, 192, 128], P(('grp', 'row'), 'col'), parts along dimension 0
- grad_left: float32 [8, 48, 32, 128], P(('grp', 'row'), 'col'), parts along dimension 0
- grad_right: float32 [8, 48, 32, 128], P(('grp', 'col'), 'row'), parts along dimension 0
- grad_weight: float32 [2048, 128], P('grp'), parts along dimension 0
There are 2 independent parts, one for each index of `grp`. A program takes and returns all parts, laid end to end along the dimension named above; an argument that names none is the same for every part. Nothing has to cross between parts.
All inputs are finite; a program needn't handle non-finite values.
Results may differ from a plain program's by a relative error of at most 0.004.
Values may be sent and summed in bfloat16 or wider, within the bound.
No kernel may reach another device: no remote copies, remote signals or barrier semaphores. Data moves between devices by JAX's collectives and lax.ppermute only.
A program may use at most 64 MiB of HBM per device.

v0:
```python
import jax
import jax.numpy as jnp
from jax import lax
from jax.sharding import PartitionSpec as P


def on_device(left_factors, right_factors, out_weight, out_bias, pair_grad):
    gathered_left = lax.all_gather(left_factors, "col", axis=1, tiled=True)[0]
    gathered_right = lax.all_gather(right_factors, "row", axis=1, tiled=True)[0]
    row_count, chan_count, sample_count = gathered_left.shape
    col_count = gathered_right.shape[0]
    out_width = out_weight.shape[1]
    blk_rows = 16
    blk_count = row_count // blk_rows
    inv_samples = 1.0 / sample_count
    left_blocks = gathered_left.reshape(blk_count, blk_rows, chan_count, sample_count)
    grad_blocks = pair_grad.reshape(blk_count, blk_rows, col_count, out_width)

    def advance(carried, inputs):
        weight_acc, right_acc = carried
        left_blk, grad_blk = inputs
        outer_mean = jnp.einsum(
            "ics,jes->ijce", left_blk, gathered_right, preferred_element_type=jnp.float32
        )
        outer_mean = (
            (outer_mean * inv_samples)
            .astype(jnp.bfloat16)
            .reshape(blk_rows, col_count, chan_count * chan_count)
        )
        pair_blk = jnp.einsum(
            "ijk,kh->ijh", outer_mean, out_weight, preferred_element_type=jnp.float32
        )
        pair_blk = (pair_blk + out_bias).astype(jnp.bfloat16)
        weight_acc = weight_acc + jnp.einsum(
            "ijk,ijh->kh", outer_mean, grad_blk, preferred_element_type=jnp.float32
        )
        outer_grad = jnp.einsum(
            "ijh,kh->ijk", grad_blk, out_weight, preferred_element_type=jnp.float32
        )
        outer_grad = outer_grad.astype(jnp.bfloat16).reshape(
            blk_rows, col_count, chan_count, chan_count
        )
        left_part = (
            jnp.einsum(
                "ijce,jes->ics", outer_grad, gathered_right, preferred_element_type=jnp.float32
            )
            * inv_samples
        )
        right_acc = (
            right_acc
            + jnp.einsum("ijce,ics->jes", outer_grad, left_blk, preferred_element_type=jnp.float32)
            * inv_samples
        )
        return ((weight_acc, right_acc), (pair_blk, left_part))

    start = (
        jnp.zeros((chan_count * chan_count, out_width), jnp.float32),
        jnp.zeros((col_count, chan_count, sample_count), jnp.float32),
    )
    (weight_acc, right_acc), (pair_blocks, left_parts) = lax.scan(
        advance, start, (left_blocks, grad_blocks)
    )
    pair_update = pair_blocks.reshape(row_count, col_count, out_width)
    left_sum = left_parts.reshape(1, row_count, chan_count, sample_count)
    right_sum = right_acc.reshape(1, col_count, chan_count, sample_count)
    left_total = lax.psum(left_sum, "col")
    right_total = lax.psum(right_sum, "row")
    left_piece = row_count // lax.axis_size("col")
    right_piece = col_count // lax.axis_size("row")
    grad_left = lax.dynamic_slice_in_dim(
        left_total, lax.axis_index("col") * left_piece, left_piece, 1
    )
    grad_right = lax.dynamic_slice_in_dim(
        right_total, lax.axis_index("row") * right_piece, right_piece, 1
    )
    weight_sum = lax.psum(weight_acc, ("row", "col"))
    grad_weight = weight_sum / jnp.float32(row_count * lax.axis_size("row"))
    return (pair_update, grad_left, grad_right, grad_weight)


def solution(mesh):
    return jax.shard_map(
        on_device,
        mesh=mesh,
        in_specs=(
            P(("grp", "row"), "col", None, None),
            P(("grp", "col"), "row", None, None),
            P(),
            P(),
            P(("grp", "row"), "col", None),
        ),
        out_specs=(
            P(("grp", "row"), "col", None),
            P(("grp", "row"), "col", None, None),
            P(("grp", "col"), "row", None, None),
            P("grp", None),
        ),
        check_vma=False,
    )
```

profile of v0, /device:TPU:0, one launch (start us, length us, event | category | flops | bytes accessed | tf_op | source)
XLA Modules:
  0.0 346.2 jit_solution(6067962147962505410)
XLA Ops:
  7.2 16.4 %all_gather.6 = bf16[1,48,32,128]{3,2,0,1:T(8,128)(2,1)S(1)} all-gather(bf16[1,12,32,128]{3,2,0,1:T(8,128)(2,1)} %bitcast.108), channel_id=1, replica_groups=mesh['grp'=2,'row'=4,'col'=4] {'col'}, dimensions={1}, use_global_device_ids=true | all-gather | bytes 491520 | tf_op jit(solution)/shard_map/all_gather | solution.py:8
  23.7 6.7 %all_gather.7 = bf16[1,48,32,128]{3,2,0,1:T(8,128)(2,1)S(1)} all-gather(bf16[1,12,32,128]{3,2,0,1:T(8,128)(2,1)} %bitcast.109), channel_id=1, replica_groups=mesh['grp'=2,'row'=4,'col'=4] {'row'}, dimensions={1}, use_global_device_ids=true | all-gather | bytes 491520 | tf_op jit(solution)/shard_map/all_gather | solution.py:9
  30.4 131.6 %while.17 = (s32[]{:T(128)}, f32[1024,128]{1,0:T(8,128)S(1)}, f32[48,32,128]{2,1,0:T(8,128)}, bf16[3,16,48,128]{3,2,1,0:T(8,128)(2,1)}, f32[3,16,32,128]{3,2,1,0...) while((s32[]{:T(128)}, f32[1024,128]{1,0:T(8,128)S(1)}, ...), condition=%wide.region_1.2_spmd.clone, body=%wide.region_0.1_spmd.clone.sunk | while | flops 1211432960 | bytes 43322212 | solution.py:60
  30.4 3.3 fusion.60
  33.7 12.5 %copy.31 = bf16[16,48,32,32]{3,2,1,0:T(8,128)(2,1)} copy(bf16[16,48,32,32]{1,2,3,0:T(8,128)(2,1)} %fusion.60) | data formatting | bytes 3145728 | tf_op jit(solution)/shard_map/while/body/eval_jaxpr/convert_element_type | solution.py:27
  46.1 8.8 %reshape.42 = bf16[16,48,1024]{2,1,0:T(8,128)(2,1)S(1)} reshape(bf16[16,48,32,32]{3,2,1,0:T(8,128)(2,1)} %copy.31) | data formatting | bytes 3145728 | tf_op jit(solution)/shard_map/while/body/eval_jaxpr/reshape | solution.py:28
  59.0 6.1 %reshape.43 = bf16[16,48,32,32]{3,2,1,0:T(8,128)(2,1)} reshape(bf16[16,48,1024]{2,1,0:T(8,128)(2,1)S(1)} %convolution_convert_fusion.2) | data formatting | bytes 3145728 | tf_op jit(solution)/shard_map/while/body/eval_jaxpr/reshape | solution.py:40
  65.1 5.6 %fusion.62 = f32[48,32,128]{2,1,0:T(8,128)} fusion(bf16[16,48,32,32]{3,2,1,0:T(8,128)(2,1)} %reshape.43, f32[48,32,128]{2,1,0:T(8,128)} %get-tuple-element.191, pred[]{:T(512)S(6)} %compare.3, bf16[3,16,32,128]{3,2,1,0:T(8,128)(2,1)} %copy-done.2, s32[]{:T(128)S(6)} %copy.39), kind=kOutput, calls=%fused_computation.5.clone.1 | convolution fusion | flops 201916416 | bytes 7995397 | tf_op jit(solution)/shard_map/while/body/eval_jaxpr/ijce,ics->jes/dot_general | solution.py:51
  72.0 2.0 fusion.64
  74.1 3.3 fusion.60
  77.4 12.5 %copy.31 = bf16[16,48,32,32]{3,2,1,0:T(8,128)(2,1)} copy(bf16[16,48,32,32]{1,2,3,0:T(8,128)(2,1)} %fusion.60) | data formatting | bytes 3145728 | tf_op jit(solution)/shard_map/while/body/eval_jaxpr/convert_element_type | solution.py:27
  89.9 8.8 %reshape.42 = bf16[16,48,1024]{2,1,0:T(8,128)(2,1)S(1)} reshape(bf16[16,48,32,32]{3,2,1,0:T(8,128)(2,1)} %copy.31) | data formatting | bytes 3145728 | tf_op jit(solution)/shard_map/while/body/eval_jaxpr/reshape | solution.py:28
  102.7 6.1 %reshape.43 = bf16[16,48,32,32]{3,2,1,0:T(8,128)(2,1)} reshape(bf16[16,48,1024]{2,1,0:T(8,128)(2,1)S(1)} %convolution_convert_fusion.2) | data formatting | bytes 3145728 | tf_op jit(solution)/shard_map/while/body/eval_jaxpr/reshape | solution.py:40
  108.9 5.8 %fusion.62 = f32[48,32,128]{2,1,0:T(8,128)} fusion(bf16[16,48,32,32]{3,2,1,0:T(8,128)(2,1)} %reshape.43, f32[48,32,128]{2,1,0:T(8,128)} %get-tuple-element.191, pred[]{:T(512)S(6)} %compare.3, bf16[3,16,32,128]{3,2,1,0:T(8,128)(2,1)} %copy-done.2, s32[]{:T(128)S(6)} %copy.39), kind=kOutput, calls=%fused_computation.5.clone.1 | convolution fusion | flops 201916416 | bytes 7995397 | tf_op jit(solution)/shard_map/while/body/eval_jaxpr/ijce,ics->jes/dot_general | solution.py:51
  116.0 2.0 fusion.64
  118.0 3.3 fusion.60
  121.3 12.5 %copy.31 = bf16[16,48,32,32]{3,2,1,0:T(8,128)(2,1)} copy(bf16[16,48,32,32]{1,2,3,0:T(8,128)(2,1)} %fusion.60) | data formatting | bytes 3145728 | tf_op jit(solution)/shard_map/while/body/eval_jaxpr/convert_element_type | solution.py:27
  133.8 8.8 %reshape.42 = bf16[16,48,1024]{2,1,0:T(8,128)(2,1)S(1)} reshape(bf16[16,48,32,32]{3,2,1,0:T(8,128)(2,1)} %copy.31) | data formatting | bytes 3145728 | tf_op jit(solution)/shard_map/while/body/eval_jaxpr/reshape | solution.py:28
  146.6 6.1 %reshape.43 = bf16[16,48,32,32]{3,2,1,0:T(8,128)(2,1)} reshape(bf16[16,48,1024]{2,1,0:T(8,128)(2,1)S(1)} %convolution_convert_fusion.2) | data formatting | bytes 3145728 | tf_op jit(solution)/shard_map/while/body/eval_jaxpr/reshape | solution.py:40
  152.8 5.8 %fusion.62 = f32[48,32,128]{2,1,0:T(8,128)} fusion(bf16[16,48,32,32]{3,2,1,0:T(8,128)(2,1)} %reshape.43, f32[48,32,128]{2,1,0:T(8,128)} %get-tuple-element.191, pred[]{:T(512)S(6)} %compare.3, bf16[3,16,32,128]{3,2,1,0:T(8,128)(2,1)} %copy-done.2, s32[]{:T(128)S(6)} %copy.39), kind=kOutput, calls=%fused_computation.5.clone.1 | convolution fusion | flops 201916416 | bytes 7995397 | tf_op jit(solution)/shard_map/while/body/eval_jaxpr/ijce,ics->jes/dot_general | solution.py:51
  159.9 2.0 fusion.64
  164.2 90.2 %all-reduce.8.cloned.1.call-done = f32[1024,128]{1,0:T(8,128)} async-done(((f32[1024,128]{1,0:T(8,128)}), f32[1024,128]{1,0:T(8,128)}) %all-reduce.8.cloned.1.call-update) | async-done | bytes 524304 | tf_op jit(solution)/shard_map/psum | solution.py:76
  256.3 35.6 %all-reduce.6.cloned.1.call-done = f32[1,48,32,128]{3,2,1,0:T(8,128)} async-done(((f32[1,48,32,128]{3,2,1,0:T(8,128)}), f32[1,48,32,128]{3,2,1,0:T(8,128)}) %all-reduce.6.cloned.1.call-update) | async-done | bytes 786448 | tf_op jit(solution)/shard_map/psum | solution.py:67
  293.6 44.5 %all-reduce.4.cloned.1.call-done = f32[1,48,32,128]{3,2,1,0:T(8,128)} async-done(((f32[1,48,32,128]{3,2,1,0:T(8,128)}), f32[1,48,32,128]{3,2,1,0:T(8,128)}) %all-reduce.4.cloned.1.call-update) | async-done | bytes 786448 | tf_op jit(solution)/shard_map/psum | solution.py:66
  (66 shorter events, 23.5 us)
Async XLA Ops:
  7.2 247.3 %all-reduce.8.cloned.1.call-start = ((), (), s32[]{:S(2)}) async-start(), calls=%async_computation.2 | async-start | bytes 1048576 | tf_op jit(solution)/shard_map/psum | solution.py:76
  30.4 3.3 copy-start.2
  56.6 0.8 copy-start.4
  65.1 5.6 %copy-start.1 = (bf16[1024,128]{1,0:T(8,128)(2,1)S(1)}, bf16[1024,128]{1,0:T(8,128)(2,1)}, u32[]{:S(2)}) copy-start(bf16[1024,128]{1,0:T(8,128)(2,1)} %get-tuple-element.209) | copy-start | bytes 786436 | tf_op jit(solution)/shard_map/while
  65.1 5.6 %copy-start.7 = (f32[128]{0:T(128)S(1)}, f32[128]{0:T(128)}, u32[]{:S(2)}) copy-start(f32[128]{0:T(128)} %get-tuple-element.210) | copy-start | bytes 1540 | tf_op jit(solution)/shard_map/while
  65.1 6.9 %copy-start = (bf16[16,48,32,32]{3,2,1,0:T(8,128)(2,1)S(1)}, bf16[16,48,32,32]{3,2,1,0:T(8,128)(2,1)}, u32[]{:S(2)}) copy-start(bf16[16,48,32,32]{3,2,1,0:T(8,128)(2,1)} %reshape.43) | copy-start | bytes 4718596 | tf_op jit(solution)/shard_map/while
  72.0 2.0 copy-start.3
  72.0 2.0 copy-start.5
  74.1 3.3 copy-start.2
  100.3 0.8 copy-start.4
  108.9 5.8 %copy-start.1 = (bf16[1024,128]{1,0:T(8,128)(2,1)S(1)}, bf16[1024,128]{1,0:T(8,128)(2,1)}, u32[]{:S(2)}) copy-start(bf16[1024,128]{1,0:T(8,128)(2,1)} %get-tuple-element.209) | copy-start | bytes 786436 | tf_op jit(solution)/shard_map/while
  108.9 5.8 %copy-start.7 = (f32[128]{0:T(128)S(1)}, f32[128]{0:T(128)}, u32[]{:S(2)}) copy-start(f32[128]{0:T(128)} %get-tuple-element.210) | copy-start | bytes 1540 | tf_op jit(solution)/shard_map/while
  108.9 7.1 %copy-start = (bf16[16,48,32,32]{3,2,1,0:T(8,128)(2,1)S(1)}, bf16[16,48,32,32]{3,2,1,0:T(8,128)(2,1)}, u32[]{:S(2)}) copy-start(bf16[16,48,32,32]{3,2,1,0:T(8,128)(2,1)} %reshape.43) | copy-start | bytes 4718596 | tf_op jit(solution)/shard_map/while
  116.0 2.0 copy-start.3
  116.0 2.0 copy-start.5
  118.0 3.3 copy-start.2
  144.2 0.8 copy-start.4
  152.8 5.8 %copy-start.1 = (bf16[1024,128]{1,0:T(8,128)(2,1)S(1)}, bf16[1024,128]{1,0:T(8,128)(2,1)}, u32[]{:S(2)}) copy-start(bf16[1024,128]{1,0:T(8,128)(2,1)} %get-tuple-element.209) | copy-start | bytes 786436 | tf_op jit(solution)/shard_map/while
  152.8 5.8 %copy-start.7 = (f32[128]{0:T(128)S(1)}, f32[128]{0:T(128)}, u32[]{:S(2)}) copy-start(f32[128]{0:T(128)} %get-tuple-element.210) | copy-start | bytes 1540 | tf_op jit(solution)/shard_map/while
  152.8 7.1 %copy-start = (bf16[16,48,32,32]{3,2,1,0:T(8,128)(2,1)S(1)}, bf16[16,48,32,32]{3,2,1,0:T(8,128)(2,1)}, u32[]{:S(2)}) copy-start(bf16[16,48,32,32]{3,2,1,0:T(8,128)(2,1)} %reshape.43) | copy-start | bytes 4718596 | tf_op jit(solution)/shard_map/while
  159.9 2.0 copy-start.3
  159.9 2.0 copy-start.5
  162.7 129.2 %all-reduce.6.cloned.1.call-start = ((), (), s32[]{:S(2)}) async-start(), calls=%async_computation.1 | async-start | bytes 1572864 | tf_op jit(solution)/shard_map/psum | solution.py:67
  163.5 174.6 %all-reduce.4.cloned.1.call-start = ((), (), s32[]{:S(2)}) async-start(), calls=%async_computation | async-start | bytes 1572864 | tf_op jit(solution)/shard_map/psum | solution.py:66
  (1 other events, 0.8 us)
Sparse Core Ops, SparseCore 0:
  162.9 91.5 all-reduce.7
  256.8 35.0 all-reduce.5
  294.3 43.6 all-reduce.3
where the time goes:
time: 348 us; the launch traced here: 346 us
  waiting for transfers between devices  172 us (49%)
  local copies, waits for them, and re-layouts  88.5 us (25%)
  matrix products  46.9 us (13%)
  blocking collectives  23.1 us (7%)
  between operations  13.8 us (4%)
    psum x1, waiting for transfers between devices, on_device(): weight_sum = lax.psum(weight_acc, ('row', 'col'))  90.2 us
    psum x1, waiting for transfers between devices, on_device(): left_total = lax.psum(left_sum, 'col')  44.5 us
    convert_element_type x3, local copies, waits for them, and re-layouts, advance(): outer_mean = (outer_mean * inv_samples).astype(jnp.bfloat16).reshape(blk_...  37.4 us
    psum x1, waiting for transfers between devices, on_device(): right_total = lax.psum(right_sum, 'row')  35.6 us
    reshape x3, local copies, waits for them, and re-layouts, advance(): outer_mean = (outer_mean * inv_samples).astype(jnp.bfloat16).reshape(blk_...  26.3 us
    reshape x3, local copies, waits for them, and re-layouts, advance(): outer_grad.astype(jnp.bfloat16)  18.4 us
    dot_general x3, matrix products, advance(): jnp.einsum('ijce,ics->jes', outer_grad, left_blk, preferred_element_type=...  17.2 us
    all_gather x1, blocking collectives, on_device(): gathered_left = lax.all_gather(left_factors, 'col', axis=1, tiled=True)[0]  16.4 us
  transfers between devices with their start and end apart: 3, of which 3 were waited for; matrix products, arithmetic and copies ran while one was open for 1% of the time, Pallas kernels for 0%

commit v1 on v0

v1 whole, which is shorter than its diff:
```python
import jax
import jax.numpy as jnp
from jax import lax
from jax.experimental import pallas as pl
from jax.experimental.pallas import tpu as pltpu
from jax.sharding import PartitionSpec as P

BF = jnp.bfloat16
F32 = jnp.float32
VMEM = pl.BlockSpec(memory_space=pltpu.VMEM)
LANES = 128


def dot_nt(x, y):
    return lax.dot_general(x, y, (((1,), (1,)), ((), ())), preferred_element_type=F32)


def dot_tn(x, y):
    return lax.dot_general(x, y, (((0,), (0,)), ((), ())), preferred_element_type=F32)


def dot_nn(x, y):
    return lax.dot_general(x, y, (((1,), (0,)), ((), ())), preferred_element_type=F32)


def swap01(x):
    return jnp.swapaxes(x.astype(F32), 0, 1).astype(x.dtype)


def xor_groups(x, a, chan):
    n = x.shape[0] // (4 * chan)
    x4 = x.reshape(n, 4, chan, x.shape[-1])
    return jnp.concatenate([x4[:, p ^ a][:, None] for p in range(4)], axis=1).reshape(x.shape)


def lane_masks(rows, chan):
    group = lax.broadcasted_iota(jnp.int32, (rows, LANES), 1) // chan
    return (group % 2) == 1, (group // 2) == 1


def trade(xs, masks):
    low, high = masks
    u = [jnp.where(low, xs[a ^ 1], xs[a]) for a in range(4)]
    return [jnp.where(high, u[b ^ 2], u[b]) for b in range(4)]


def assemble(scratch, parts, axis, axis_size):
    me = lax.axis_index(axis)
    piece = parts[0].shape[0]
    for k in range(axis_size):
        scratch[pl.ds((me ^ k) * piece, piece)] = parts[k][...]


def hand_out(total, pieces, axis, axis_size):
    me = lax.axis_index(axis)
    piece = pieces[0].shape[0]
    for k in range(axis_size):
        pieces[k][...] = total[pl.ds((me ^ k) * piece, piece)].astype(pieces[k].dtype)


def call(kernel, outs, scratch, name, *operands):
    single = not isinstance(outs, (list, tuple))
    return pl.pallas_call(
        kernel,
        out_shape=outs,
        in_specs=[VMEM] * len(operands),
        out_specs=VMEM if single else [VMEM] * len(outs),
        scratch_shapes=list(scratch),
        compiler_params=pltpu.CompilerParams(vmem_limit_bytes=40 * 1024 * 1024),
        name=name,
    )(*operands)


def send_xor(pieces, axis, axis_size):
    return [pieces[0]] + [
        lax.ppermute(pieces[k], axis, [(d, d ^ k) for d in range(axis_size)])
        for k in range(1, axis_size)
    ]


def on_device(left_factors, right_factors, out_weight, out_bias, pair_grad):
    n_row = lax.axis_size("row")
    n_col = lax.axis_size("col")
    left, right = left_factors[0], right_factors[0]
    left_piece, chan, samples = left.shape
    right_piece = right.shape[0]
    rows, cols, width = pair_grad.shape
    pairs = chan * chan
    row4, chan4 = rows // 4, chan // 4
    inv_samples = 1.0 / samples
    struct = jax.ShapeDtypeStruct
    weight3 = out_weight.reshape(chan, chan, width)
    grad4 = pair_grad.reshape(row4, 4, cols, width)

    right_parts = send_xor([right] * n_row, "row", n_row)
    left_parts = send_xor([left] * n_col, "col", n_col)

    wide = 2 * LANES

    def outer_grad_kernel(grad_ref, weight_ref, z_ref, tmp):
        w = swap01(weight_ref[...]).reshape(pairs, width)
        masks = lane_masks(cols, chan)
        for blk in range(pairs // wide):
            for b in range(4):
                tmp[blk, b] = dot_nt(
                    grad_ref[:, b].reshape(row4 * cols, width),
                    xor_groups(w, b, chan)[blk * wide : (blk + 1) * wide],
                ).astype(BF)
            for n in range(row4):
                for h in range(2):
                    ys = trade(
                        [
                            tmp[blk, b, n * cols : (n + 1) * cols, h * LANES : (h + 1) * LANES]
                            for b in range(4)
                        ],
                        masks,
                    )
                    for a in range(4):
                        z_ref[2 * blk + h, a, :, n * LANES : (n + 1) * LANES] = ys[a]

    z = call(
        outer_grad_kernel,
        struct((chan4, 4, cols, rows * chan), BF),
        [pltpu.VMEM((pairs // wide, 4, row4 * cols, wide), BF)],
        "outer_grad",
        grad4,
        weight3,
    )

    def left_kernel(z_ref, *refs):
        b_refs, pieces, whole, total = refs[:n_row], refs[n_row : n_row + n_col], refs[-2], refs[-1]
        assemble(whole, b_refs, "row", n_row)
        be = swap01(whole[...]).reshape(chan4, 4, cols, samples)
        acc = None
        for a in range(4):
            d = dot_tn(
                z_ref[:, a].reshape(chan4 * cols, rows * chan),
                be[:, a].reshape(chan4 * cols, samples),
            )
            d = xor_groups(d, a, chan)
            acc = d if acc is None else acc + d
        total[...] = (acc * inv_samples).reshape(rows, chan, samples)
        hand_out(total, pieces, "col", n_col)

    left_pieces = call(
        left_kernel,
        [struct((left_piece, chan, samples), BF)] * n_col,
        [pltpu.VMEM((cols, chan, samples), BF), pltpu.VMEM((rows, chan, samples), F32)],
        "left_grad",
        z,
        *right_parts,
    )
    left_got = send_xor(left_pieces, "col", n_col)

    weight_piece = pairs // n_row

    def outer_mean_kernel(grad_ref, *refs):
        a_refs, b_refs = refs[:n_col], refs[n_col : n_col + n_row]
        y_ref = refs[n_col + n_row]
        pieces = refs[n_col + n_row + 1 : n_col + 2 * n_row + 1]
        a_whole, b_whole, tmp, total = refs[-4:]
        assemble(a_whole, a_refs, "col", n_col)
        assemble(b_whole, b_refs, "row", n_row)
        be = swap01(b_whole[...]).reshape(chan4, 4, cols, samples)
        am = a_whole[...].reshape(rows * chan, samples)
        masks = lane_masks(cols, chan)
        for blk in range(rows * chan // wide):
            for a in range(4):
                tmp[blk, a] = dot_nt(
                    be[:, a].reshape(chan4 * cols, samples),
                    xor_groups(am, a, chan)[blk * wide : (blk + 1) * wide],
                ).astype(BF)
            for e in range(chan4):
                for h in range(2):
                    ys = trade(
                        [
                            tmp[blk, a, e * cols : (e + 1) * cols, h * LANES : (h + 1) * LANES]
                            for a in range(4)
                        ],
                        masks,
                    )
                    for b in range(4):
                        y_ref[2 * blk + h, b, :, e * LANES : (e + 1) * LANES] = ys[b]
        acc = None
        for b in range(4):
            d = dot_tn(
                y_ref[:, b].reshape(row4 * cols, pairs),
                grad_ref[:, b].reshape(row4 * cols, width),
            )
            d = xor_groups(d, b, chan)
            acc = d if acc is None else acc + d
        acc = (acc * (inv_samples / (rows * n_row))).reshape(chan, chan, width)
        total[...] = jnp.swapaxes(acc, 0, 1).reshape(pairs, width)
        hand_out(total, pieces, "row", n_row)

    y, *weight_pieces = call(
        outer_mean_kernel,
        [struct((row4, 4, cols, pairs), BF)] + [struct((weight_piece, width), BF)] * n_row,
        [
            pltpu.VMEM((rows, chan, samples), BF),
            pltpu.VMEM((cols, chan, samples), BF),
            pltpu.VMEM((rows * chan // wide, 4, chan4 * cols, wide), BF),
            pltpu.VMEM((pairs, width), F32),
        ],
        "outer_mean",
        grad4,
        *left_parts,
        *right_parts,
    )
    weight_got = send_xor(weight_pieces, "row", n_row)

    def right_kernel(z_ref, *refs):
        a_refs, pieces, whole, total = refs[:n_col], refs[n_col : n_col + n_row], refs[-2], refs[-1]
        assemble(whole, a_refs, "col", n_col)
        am = whole[...].reshape(rows * chan, samples)
        for a in range(4):
            d = dot_nn(z_ref[:, a].reshape(chan4 * cols, rows * chan), xor_groups(am, a, chan))
            total[:, a] = d.reshape(chan4, cols, samples)
        d = jnp.swapaxes(total[...].reshape(chan, cols, samples), 0, 1) * inv_samples
        me = lax.axis_index("row")
        wholes = d.astype(BF)
        whole2 = refs[-3]
        whole2[...] = wholes
        for k in range(n_row):
            pieces[k][...] = whole2[pl.ds((me ^ k) * right_piece, right_piece)]

    right_pieces = call(
        right_kernel,
        [struct((right_piece, chan, samples), BF)] * n_row,
        [
            pltpu.VMEM((cols, chan, samples), BF),
            pltpu.VMEM((rows, chan, samples), BF),
            pltpu.VMEM((chan4, 4, cols, samples), F32),
        ],
        "right_grad",
        z,
        *left_parts,
    )
    right_got = send_xor(right_pieces, "row", n_row)

    def pair_kernel(y_ref, weight_ref, bias_ref, p_ref):
        w = swap01(weight_ref[...]).reshape(pairs, width)
        for b in range(4):
            d = dot_nn(y_ref[:, b].reshape(row4 * cols, pairs), xor_groups(w, b, chan))
            p_ref[:, b] = (d * inv_samples + bias_ref[...]).reshape(row4, cols, width).astype(BF)

    pair_update = call(
        pair_kernel,
        struct((row4, 4, cols, width), BF),
        [],
        "pair_update",
        y,
        weight3,
        out_bias.reshape(1, width),
    ).reshape(rows, cols, width)

    def add_up(parts):
        total = parts[0].astype(F32)
        for part in parts[1:]:
            total = total + part.astype(F32)
        return total

    weight_row = add_up(weight_got)
    col_me = lax.axis_index("col")
    row_me = lax.axis_index("row")
    fine = weight_piece // n_col
    weight_fine = [
        lax.dynamic_slice_in_dim(weight_row, (col_me ^ k) * fine, fine, 0) for k in range(n_col)
    ]
    weight_sum = add_up(send_xor(weight_fine, "col", n_col))
    col_parts = send_xor([weight_sum] * n_col, "col", n_col)
    mine = jnp.zeros((n_col, fine, width), F32)
    for k in range(n_col):
        mine = lax.dynamic_update_slice_in_dim(mine, col_parts[k][None], col_me ^ k, 0)
    mine = mine.reshape(weight_piece, width).astype(BF)
    row_parts = send_xor([mine] * n_row, "row", n_row)
    grad_weight = jnp.zeros((n_row, weight_piece, width), F32)
    for k in range(n_row):
        grad_weight = lax.dynamic_update_slice_in_dim(
            grad_weight, row_parts[k][None].astype(F32), row_me ^ k, 0
        )
    grad_weight = grad_weight.reshape(pairs, width)
    grad_left = add_up(left_got)[None]
    grad_right = add_up(right_got)[None]
    return (pair_update, grad_left, grad_right, grad_weight)


def solution(mesh):
    return jax.shard_map(
        on_device,
        mesh=mesh,
        in_specs=(
            P(("grp", "row"), "col", None, None),
            P(("grp", "col"), "row", None, None),
            P(),
            P(),
            P(("grp", "row"), "col", None),
        ),
        out_specs=(
            P(("grp", "row"), "col", None),
            P(("grp", "row"), "col", None, None),
            P(("grp", "col"), "row", None, None),
            P("grp", None),
        ),
        check_vma=False,
    )
```

time: 348 us -> 73.8 us (0.21)
  waiting for transfers between devices: 172 us -> 18.1 us
  local copies, waits for them, and re-layouts: 88.5 us -> 14.7 us
  matrix products: 46.9 us -> 0 us
  starting transfers between devices: 0.12 us -> 26.8 us
  blocking collectives: 23.1 us -> 0 us
  between operations: 13.8 us -> 0.83 us
  Pallas kernels: 0 us -> 11.4 us
    psum x3 -> x0, waiting for transfers between devices: 170 us -> none  [the longest x1 90.2 us: on_device(): weight_sum = lax.psum(weight_acc, ('row', 'col'))]
    dot_general x18 -> x0, matrix products: 46.9 us -> none  [the longest x3 17.2 us: advance(): jnp.einsum('ijce,ics->jes', outer_grad, left_blk, preferred_element_type=...]
    reshape x6 -> x0, local copies, waits for them, and re-layouts: 44.7 us -> none  [the longest x3 26.3 us: advance(): outer_mean = (outer_mean * inv_samples).astype(jnp.bfloat16).reshape(blk_...]
    convert_element_type x3 -> x0, local copies, waits for them, and re-layouts: 37.4 us -> none  [advance(): outer_mean = (outer_mean * inv_samples).astype(jnp.bfloat16).reshape(blk_...]
    ppermute x0 -> x24, starting transfers between devices: none -> 26.8 us  [send_xor(): lax.ppermute(pieces[k], axis, [(d, d ^ k) for d in range(axis_size)])]
    all_gather x2 -> x0, blocking collectives: 23.1 us -> none  [the longest x1 16.4 us: on_device(): gathered_left = lax.all_gather(left_factors, 'col', axis=1, tiled=True)[0]]
    ppermute x0 -> x24, waiting for transfers between devices: none -> 18.1 us  [send_xor(): lax.ppermute(pieces[k], axis, [(d, d ^ k) for d in range(axis_size)])]
    unnamed x2 -> x30, local copies, waits for them, and re-layouts: 0.79 us -> 14.6 us
  transfers between devices with their start and end apart: 3 -> 24, of which waited for: 3 -> 7; matrix products, arithmetic and copies ran while one was open for 1% -> 2% of each run, Pallas kernels for 0% -> 10%
where the time goes in v1:
time: 73.8 us; the launch traced here: 73.4 us
  starting transfers between devices  26.8 us (36%)
  waiting for transfers between devices  18.1 us (25%)
  local copies, waits for them, and re-layouts  14.7 us (20%)
  Pallas kernels  11.4 us (15%)
  other arithmetic  1.57 us (2%)
  between operations  0.83 us (1%)
    ppermute x24, starting transfers between devices, send_xor(): lax.ppermute(pieces[k], axis, [(d, d ^ k) for d in range(axis_size)])  26.8 us
    ppermute x24, waiting for transfers between devices, send_xor(): lax.ppermute(pieces[k], axis, [(d, d ^ k) for d in range(axis_size)])  18.1 us
    unnamed x30, local copies, waits for them, and re-layouts  14.6 us
    pallas_call x5, Pallas kernels, call(): pl.pallas_call(kernel, out_shape=outs, in_specs=[VMEM] * len(operands), o...  11.4 us
  transfers between devices with their start and end apart: 24, of which 7 were waited for; matrix products, arithmetic and copies ran while one was open for 2% of the time, Pallas kernels for 10%

profile of v1, /device:TPU:0, one launch (start us, length us, event | category | flops | bytes accessed | tf_op | source)
XLA Modules:
  0.0 73.4 jit_solution(3996451084408299369)
XLA Ops:
  0.6 3.1 %collective-permute-start = (bf16[12,32,128]{2,1,0:T(8,128)(2,1)}, bf16[12,32,128]{2,1,0:T(8,128)(2,1)S(1)}, u32[]{:S(2)}, u32[]{:S(2)}) collective-permute-start(bf16[12,32,128]{2,1,0:T(8,128)(2,1)} %bitcast.42), channel_id=1, source_target_pairs={{0,1},{1,0},{2,3},{3,2},{4,5},{5,4},{6,7},{7,6},{8,9},{9,8},{10,11... | collective-permute-start | bytes 294920 | tf_op jit(solution)/shard_map/ppermute | solution.py:76
  3.7 2.6 %collective-permute-start.1 = (bf16[12,32,128]{2,1,0:T(8,128)(2,1)}, bf16[12,32,128]{2,1,0:T(8,128)(2,1)S(1)}, u32[]{:S(2)}, u32[]{:S(2)}) collective-permute-start(bf16[12,32,128]{2,1,0:T(8,128)(2,1)} %bitcast.43), channel_id=1, source_target_pairs={{0,2},{1,3},{2,0},{3,1},{4,6},{5,7},{6,4},{7,5},{8,10},{9,11},{10,... | collective-permute-start | bytes 294920 | tf_op jit(solution)/shard_map/ppermute | solution.py:76
  6.3 1.7 %collective-permute-start.4 = (bf16[12,32,128]{2,1,0:T(8,128)(2,1)}, bf16[12,32,128]{2,1,0:T(8,128)(2,1)S(1)}, u32[]{:S(2)}, u32[]{:S(2)}) collective-permute-start(bf16[12,32,128]{2,1,0:T(8,128)(2,1)} %bitcast.38), channel_id=1, source_target_pairs={{0,8},{4,12},{8,0},{12,4},{1,9},{5,13},{9,1},{13,5},{2,10},{6,14},... | collective-permute-start | bytes 294920 | tf_op jit(solution)/shard_map/ppermute | solution.py:76
  8.2 6.2 %collective-permute-done.1.refs_2_ = bf16[12,32,128]{2,1,0:T(8,128)(2,1)S(1)} collective-permute-done((bf16[12,32,128]{2,1,0:T(8,128)(2,1)}, bf16[12,32,128]{2,1,0:T(8,128)(2,1)S(1)}, u32[]{:S(2)}, u32[]{:S(2)}) %collective-permute-start.1) | collective-permute-done | bytes 98336 | tf_op jit(solution)/shard_map/ppermute | solution.py:76
  17.2 4.1 %outer_mean.1 = (bf16[12,4,48,1024]{3,2,1,0:T(8,128)(2,1)S(1)}, bf16[256,128]{1,0:T(8,128)(2,1)S(1)}, bf16[256,128]{1,0:T(8,128)(2,1)S(1)}, bf16[256,128]{1,0:T(8,128)(2,1)S(1)}, bf16[256,128]{1,0:T(8,128)(2,1)S(1)}) custom-call(bf16[12,4,48,128]{3,2,1,0:T(8,128)(2,1)S(1)} %bitcast.33, bf16[12,32,128]{2,1,0:T(8,128)(2,1)S(1)} %bitcast.45, ...), custom_call_target="tpu_custom_call" | custom-call | tf_op jit(solution)/shard_map/outer_mean/pallas_call | solution.py:63
  21.3 2.1 %copy-done.3 = bf16[12,4,48,1024]{3,2,1,0:T(8,128)(2,1)} copy-done((bf16[12,4,48,1024]{3,2,1,0:T(8,128)(2,1)}, bf16[12,4,48,1024]{3,2,1,0:T(8,128)(2,1)S(1)}, u32[]{:S(2)}) %copy-start.3) | copy-done | bytes 4718616
  25.3 2.5 %collective-permute-done.14 = bf16[256,128]{1,0:T(8,128)(2,1)S(1)} collective-permute-done((bf16[256,128]{1,0:T(8,128)(2,1)S(1)}, bf16[256,128]{1,0:T(8,128)(2,1)S(1)}, u32[]{:S(2)}, u32[]{:S(2)}) %collective-permute-start.14) | collective-permute-done | bytes 65568 | tf_op jit(solution)/shard_map/ppermute | solution.py:76
  27.8 1.4 %collective-permute-done.13 = bf16[256,128]{1,0:T(8,128)(2,1)S(1)} collective-permute-done((bf16[256,128]{1,0:T(8,128)(2,1)S(1)}, bf16[256,128]{1,0:T(8,128)(2,1)S(1)}, u32[]{:S(2)}, u32[]{:S(2)}) %collective-permute-start.13) | collective-permute-done | bytes 65568 | tf_op jit(solution)/shard_map/ppermute | solution.py:76
  29.3 2.9 %collective-permute-start.17 = (f32[64,128]{1,0:T(8,128)S(1)}, f32[64,128]{1,0:T(8,128)S(1)}, u32[]{:S(2)}, u32[]{:S(2)}) collective-permute-start(f32[64,128]{1,0:T(8,128)S(1)} %get-tuple-element.33), channel_id=1, source_target_pairs={{0,3},{1,2},{2,1},{3,0},{4,7},{5,6},{6,5},{7,4},{8,11},{9,10},{10,... | collective-permute-start | bytes 98312 | tf_op jit(solution)/shard_map/ppermute | solution.py:76
  32.5 1.3 %collective-permute-start.15 = (f32[64,128]{1,0:T(8,128)S(1)}, f32[64,128]{1,0:T(8,128)S(1)}, u32[]{:S(2)}, u32[]{:S(2)}) collective-permute-start(f32[64,128]{1,0:T(8,128)S(1)} %get-tuple-element.32), channel_id=1, source_target_pairs={{0,1},{1,0},{2,3},{3,2},{4,5},{5,4},{6,7},{7,6},{8,9},{9,8},{10,11... | collective-permute-start | bytes 98312 | tf_op jit(solution)/shard_map/ppermute | solution.py:76
  35.8 2.0 %outer_grad.1.z_ref = bf16[8,4,48,1536]{3,2,1,0:T(8,128)(2,1)S(1)} custom-call(bf16[12,4,48,128]{3,2,1,0:T(8,128)(2,1)S(1)} %bitcast.34, bf16[32,32,128]{2,1,0:T(8,128)(2,1)S(1)} %bitcast.35), custom_call_target="tpu_custom_call" | custom-call | tf_op jit(solution)/shard_map/outer_grad/pallas_call | solution.py:63
  37.8 2.1 %copy-done = bf16[8,4,48,1536]{3,2,1,0:T(8,128)(2,1)} copy-done((bf16[8,4,48,1536]{3,2,1,0:T(8,128)(2,1)}, bf16[8,4,48,1536]{3,2,1,0:T(8,128)(2,1)S(1)}, u32[]{:S(2)}) %copy-start) | copy-done | bytes 4718616
  40.0 2.3 %copy-done.1 = bf16[8,4,48,1536]{3,2,1,0:T(8,128)(2,1)S(1)} copy-done((bf16[8,4,48,1536]{3,2,1,0:T(8,128)(2,1)S(1)}, bf16[8,4,48,1536]{3,2,1,0:T(8,128)(2,1)}, u32[]{:S(2)}) %copy-start.1) | copy-done | bytes 4718616
  42.3 1.6 %left_grad.1 = (bf16[12,32,128]{2,1,0:T(8,128)(2,1)S(1)}, bf16[12,32,128]{2,1,0:T(8,128)(2,1)S(1)}, bf16[12,32,128]{2,1,0:T(8,128)(2,1)S(1)}, bf16[12,32,128]{2,1,0:T(8,128)(2,1)S(1)}) custom-call(bf16[8,4,48,1536]{3,2,1,0:T(8,128)(2,1)S(1)} %copy-done.1, bf16[12,32,128]{2,1,0:T(8,128)(2,1)S(1)} %bitcast.41, ...), custom_call_target="tpu_custom_call" | custom-call | tf_op jit(solution)/shard_map/left_grad/pallas_call | solution.py:63
  43.9 3.0 %collective-permute-start.8 = (bf16[12,32,128]{2,1,0:T(8,128)(2,1)S(1)}, bf16[12,32,128]{2,1,0:T(8,128)(2,1)S(1)}, u32[]{:S(2)}, u32[]{:S(2)}) collective-permute-start(bf16[12,32,128]{2,1,0:T(8,128)(2,1)S(1)} %get-tuple-element.21), channel_id=1, source_target_pairs={{0,3},{1,2},{2,1},{3,0},{4,7},{5,6},{6,5},{7,4},{8,11},{9,10},{10,... | collective-permute-start | bytes 294920 | tf_op jit(solution)/shard_map/ppermute | solution.py:76
  46.9 2.3 %copy-done.4 = bf16[12,4,48,1024]{3,2,1,0:T(8,128)(2,1)S(1)} copy-done((bf16[12,4,48,1024]{3,2,1,0:T(8,128)(2,1)S(1)}, bf16[12,4,48,1024]{3,2,1,0:T(8,128)(2,1)}, u32[]{:S(2)}) %copy-start.4) | copy-done | bytes 4718616
  49.2 2.2 %pair_update.1 = bf16[12,4,48,128]{3,2,1,0:T(8,128)(2,1)} custom-call(bf16[12,4,48,1024]{3,2,1,0:T(8,128)(2,1)S(1)} %copy-done.4, bf16[32,32,128]{2,1,0:T(8,128)(2,1)S(1)} %bitcast.36, f32[1,128]{1,0:T(1,128)S(1)} %bitcast.47), custom_call_target="tpu_custom_call" | custom-call | tf_op jit(solution)/shard_map/pair_update/pallas_call | solution.py:63
  51.5 1.5 %right_grad.1 = (bf16[12,32,128]{2,1,0:T(8,128)(2,1)S(1)}, bf16[12,32,128]{2,1,0:T(8,128)(2,1)S(1)}, bf16[12,32,128]{2,1,0:T(8,128)(2,1)S(1)}, bf16[12,32,128]{2,1,0:T(8,128)(2,1)S(1)}) custom-call(bf16[8,4,48,1536]{3,2,1,0:T(8,128)(2,1)S(1)} %copy-done.2, bf16[12,32,128]{2,1,0:T(8,128)(2,1)S(1)} %bitcast.46, ...), custom_call_target="tpu_custom_call" | custom-call | tf_op jit(solution)/shard_map/right_grad/pallas_call | solution.py:63
  53.0 1.5 %collective-permute-start.6 = (bf16[12,32,128]{2,1,0:T(8,128)(2,1)S(1)}, bf16[12,32,128]{2,1,0:T(8,128)(2,1)S(1)}, u32[]{:S(2)}, u32[]{:S(2)}) collective-permute-start(bf16[12,32,128]{2,1,0:T(8,128)(2,1)S(1)} %get-tuple-element.19), channel_id=1, source_target_pairs={{0,1},{1,0},{2,3},{3,2},{4,5},{5,4},{6,7},{7,6},{8,9},{9,8},{10,11... | collective-permute-start | bytes 294920 | tf_op jit(solution)/shard_map/ppermute | solution.py:76
  54.5 1.5 %collective-permute-start.10 = (bf16[12,32,128]{2,1,0:T(8,128)(2,1)S(1)}, bf16[12,32,128]{2,1,0:T(8,128)(2,1)S(1)}, u32[]{:S(2)}, u32[]{:S(2)}) collective-permute-start(bf16[12,32,128]{2,1,0:T(8,128)(2,1)S(1)} %get-tuple-element.24), channel_id=1, source_target_pairs={{0,8},{4,12},{8,0},{12,4},{1,9},{5,13},{9,1},{13,5},{2,10},{6,14},... | collective-permute-start | bytes 294920 | tf_op jit(solution)/shard_map/ppermute | solution.py:76
  57.7 2.9 %collective-permute-start.19 = (bf16[64,128]{1,0:T(8,128)(2,1)S(1)}, bf16[64,128]{1,0:T(8,128)(2,1)S(1)}, u32[]{:S(2)}, u32[]{:S(2)}) collective-permute-start(bf16[64,128]{1,0:T(8,128)(2,1)S(1)} %get-tuple-element.31), channel_id=1, source_target_pairs={{0,2},{1,3},{2,0},{3,1},{4,6},{5,7},{6,4},{7,5},{8,10},{9,11},{10,... | collective-permute-start | bytes 49160 | tf_op jit(solution)/shard_map/ppermute | solution.py:76
  63.2 3.6 %collective-permute-done.20 = bf16[64,128]{1,0:T(8,128)(2,1)S(1)} collective-permute-done((bf16[64,128]{1,0:T(8,128)(2,1)S(1)}, bf16[64,128]{1,0:T(8,128)(2,1)S(1)}, u32[]{:S(2)}, u32[]{:S(2)}) %collective-permute-start.20) | collective-permute-done | bytes 16416 | tf_op jit(solution)/shard_map/ppermute | solution.py:76
  66.9 1.6 %collective-permute-start.22 = (bf16[256,128]{1,0:T(8,128)(2,1)S(1)}, bf16[256,128]{1,0:T(8,128)(2,1)S(1)}, u32[]{:S(2)}, u32[]{:S(2)}) collective-permute-start(bf16[256,128]{1,0:T(8,128)(2,1)S(1)} %bitcast.51), channel_id=1, source_target_pairs={{0,8},{4,12},{8,0},{12,4},{1,9},{5,13},{9,1},{13,5},{2,10},{6,14},... | collective-permute-start | bytes 196616 | tf_op jit(solution)/shard_map/ppermute | solution.py:76
  68.8 2.6 %collective-permute-done.22 = bf16[256,128]{1,0:T(8,128)(2,1)S(1)} collective-permute-done((bf16[256,128]{1,0:T(8,128)(2,1)S(1)}, bf16[256,128]{1,0:T(8,128)(2,1)S(1)}, u32[]{:S(2)}, u32[]{:S(2)}) %collective-permute-start.22) | collective-permute-done | bytes 65568 | tf_op jit(solution)/shard_map/ppermute | solution.py:76
  (73 shorter events, 13.8 us)
Async XLA Ops:
  0.6 7.4 %collective-permute-start = (bf16[12,32,128]{2,1,0:T(8,128)(2,1)}, bf16[12,32,128]{2,1,0:T(8,128)(2,1)S(1)}, u32[]{:S(2)}, u32[]{:S(2)}) collective-permute-start(bf16[12,32,128]{2,1,0:T(8,128)(2,1)} %bitcast.42), channel_id=1, source_target_pairs={{0,1},{1,0},{2,3},{3,2},{4,5},{5,4},{6,7},{7,6},{8,9},{9,8},{10,11... | collective-permute-start | bytes 294920 | tf_op jit(solution)/shard_map/ppermute | solution.py:76
  3.7 10.6 %collective-permute-start.1 = (bf16[12,32,128]{2,1,0:T(8,128)(2,1)}, bf16[12,32,128]{2,1,0:T(8,128)(2,1)S(1)}, u32[]{:S(2)}, u32[]{:S(2)}) collective-permute-start(bf16[12,32,128]{2,1,0:T(8,128)(2,1)} %bitcast.43), channel_id=1, source_target_pairs={{0,2},{1,3},{2,0},{3,1},{4,6},{5,7},{6,4},{7,5},{8,10},{9,11},{10,... | collective-permute-start | bytes 294920 | tf_op jit(solution)/shard_map/ppermute | solution.py:76
  6.3 8.1 %collective-permute-start.2 = (bf16[12,32,128]{2,1,0:T(8,128)(2,1)}, bf16[12,32,128]{2,1,0:T(8,128)(2,1)S(1)}, u32[]{:S(2)}, u32[]{:S(2)}) collective-permute-start(bf16[12,32,128]{2,1,0:T(8,128)(2,1)} %bitcast.44), channel_id=1, source_target_pairs={{0,3},{1,2},{2,1},{3,0},{4,7},{5,6},{6,5},{7,4},{8,11},{9,10},{10,... | collective-permute-start | bytes 294920 | tf_op jit(solution)/shard_map/ppermute | solution.py:76
  6.3 8.1 %collective-permute-start.3 = (bf16[12,32,128]{2,1,0:T(8,128)(2,1)}, bf16[12,32,128]{2,1,0:T(8,128)(2,1)S(1)}, u32[]{:S(2)}, u32[]{:S(2)}) collective-permute-start(bf16[12,32,128]{2,1,0:T(8,128)(2,1)} %bitcast.37), channel_id=1, source_target_pairs={{0,4},{4,0},{8,12},{12,8},{1,5},{5,1},{9,13},{13,9},{2,6},{6,2},{1... | collective-permute-start | bytes 294920 | tf_op jit(solution)/shard_map/ppermute | solution.py:76
  6.3 8.1 %collective-permute-start.4 = (bf16[12,32,128]{2,1,0:T(8,128)(2,1)}, bf16[12,32,128]{2,1,0:T(8,128)(2,1)S(1)}, u32[]{:S(2)}, u32[]{:S(2)}) collective-permute-start(bf16[12,32,128]{2,1,0:T(8,128)(2,1)} %bitcast.38), channel_id=1, source_target_pairs={{0,8},{4,12},{8,0},{12,4},{1,9},{5,13},{9,1},{13,5},{2,10},{6,14},... | collective-permute-start | bytes 294920 | tf_op jit(solution)/shard_map/ppermute | solution.py:76
  8.0 6.4 %collective-permute-start.5 = (bf16[12,32,128]{2,1,0:T(8,128)(2,1)}, bf16[12,32,128]{2,1,0:T(8,128)(2,1)S(1)}, u32[]{:S(2)}, u32[]{:S(2)}) collective-permute-start(bf16[12,32,128]{2,1,0:T(8,128)(2,1)} %bitcast.39), channel_id=1, source_target_pairs={{0,12},{4,8},{8,4},{12,0},{1,13},{5,9},{9,5},{13,1},{2,14},{6,10},... | collective-permute-start | bytes 294920 | tf_op jit(solution)/shard_map/ppermute | solution.py:76
  23.5 4.3 %collective-permute-start.14 = (bf16[256,128]{1,0:T(8,128)(2,1)S(1)}, bf16[256,128]{1,0:T(8,128)(2,1)S(1)}, u32[]{:S(2)}, u32[]{:S(2)}) collective-permute-start(bf16[256,128]{1,0:T(8,128)(2,1)S(1)} %get-tuple-element.29), channel_id=1, source_target_pairs={{0,12},{4,8},{8,4},{12,0},{1,13},{5,9},{9,5},{13,1},{2,14},{6,10},... | collective-permute-start | bytes 196616 | tf_op jit(solution)/shard_map/ppermute | solution.py:76
  24.4 4.9 %collective-permute-start.13 = (bf16[256,128]{1,0:T(8,128)(2,1)S(1)}, bf16[256,128]{1,0:T(8,128)(2,1)S(1)}, u32[]{:S(2)}, u32[]{:S(2)}) collective-permute-start(bf16[256,128]{1,0:T(8,128)(2,1)S(1)} %get-tuple-element.28), channel_id=1, source_target_pairs={{0,8},{4,12},{8,0},{12,4},{1,9},{5,13},{9,1},{13,5},{2,10},{6,14},... | collective-permute-start | bytes 196616 | tf_op jit(solution)/shard_map/ppermute | solution.py:76
  25.0 4.3 %collective-permute-start.12 = (bf16[256,128]{1,0:T(8,128)(2,1)S(1)}, bf16[256,128]{1,0:T(8,128)(2,1)S(1)}, u32[]{:S(2)}, u32[]{:S(2)}) collective-permute-start(bf16[256,128]{1,0:T(8,128)(2,1)S(1)} %get-tuple-element.27), channel_id=1, source_target_pairs={{0,4},{4,0},{8,12},{12,8},{1,5},{5,1},{9,13},{13,9},{2,6},{6,2},{1... | collective-permute-start | bytes 196616 | tf_op jit(solution)/shard_map/ppermute | solution.py:76
  29.3 23.7 %collective-permute-start.17 = (f32[64,128]{1,0:T(8,128)S(1)}, f32[64,128]{1,0:T(8,128)S(1)}, u32[]{:S(2)}, u32[]{:S(2)}) collective-permute-start(f32[64,128]{1,0:T(8,128)S(1)} %get-tuple-element.33), channel_id=1, source_target_pairs={{0,3},{1,2},{2,1},{3,0},{4,7},{5,6},{6,5},{7,4},{8,11},{9,10},{10,... | collective-permute-start | bytes 98312 | tf_op jit(solution)/shard_map/ppermute | solution.py:76
  32.3 22.3 %collective-permute-start.16 = (f32[64,128]{1,0:T(8,128)S(1)}, f32[64,128]{1,0:T(8,128)S(1)}, u32[]{:S(2)}, u32[]{:S(2)}) collective-permute-start(f32[64,128]{1,0:T(8,128)S(1)} %get-tuple-element.34), channel_id=1, source_target_pairs={{0,2},{1,3},{2,0},{3,1},{4,6},{5,7},{6,4},{7,5},{8,10},{9,11},{10,... | collective-permute-start | bytes 98312 | tf_op jit(solution)/shard_map/ppermute | solution.py:76
  32.5 22.1 %collective-permute-start.15 = (f32[64,128]{1,0:T(8,128)S(1)}, f32[64,128]{1,0:T(8,128)S(1)}, u32[]{:S(2)}, u32[]{:S(2)}) collective-permute-start(f32[64,128]{1,0:T(8,128)S(1)} %get-tuple-element.32), channel_id=1, source_target_pairs={{0,1},{1,0},{2,3},{3,2},{4,5},{5,4},{6,7},{7,6},{8,9},{9,8},{10,11... | collective-permute-start | bytes 98312 | tf_op jit(solution)/shard_map/ppermute | solution.py:76
  43.9 12.2 %collective-permute-start.8 = (bf16[12,32,128]{2,1,0:T(8,128)(2,1)S(1)}, bf16[12,32,128]{2,1,0:T(8,128)(2,1)S(1)}, u32[]{:S(2)}, u32[]{:S(2)}) collective-permute-start(bf16[12,32,128]{2,1,0:T(8,128)(2,1)S(1)} %get-tuple-element.21), channel_id=1, source_target_pairs={{0,3},{1,2},{2,1},{3,0},{4,7},{5,6},{6,5},{7,4},{8,11},{9,10},{10,... | collective-permute-start | bytes 294920 | tf_op jit(solution)/shard_map/ppermute | solution.py:76
  46.9 9.6 %collective-permute-start.7 = (bf16[12,32,128]{2,1,0:T(8,128)(2,1)S(1)}, bf16[12,32,128]{2,1,0:T(8,128)(2,1)S(1)}, u32[]{:S(2)}, u32[]{:S(2)}) collective-permute-start(bf16[12,32,128]{2,1,0:T(8,128)(2,1)S(1)} %get-tuple-element.20), channel_id=1, source_target_pairs={{0,2},{1,3},{2,0},{3,1},{4,6},{5,7},{6,4},{7,5},{8,10},{9,11},{10,... | collective-permute-start | bytes 294920 | tf_op jit(solution)/shard_map/ppermute | solution.py:76
  53.0 4.7 %collective-permute-start.6 = (bf16[12,32,128]{2,1,0:T(8,128)(2,1)S(1)}, bf16[12,32,128]{2,1,0:T(8,128)(2,1)S(1)}, u32[]{:S(2)}, u32[]{:S(2)}) collective-permute-start(bf16[12,32,128]{2,1,0:T(8,128)(2,1)S(1)} %get-tuple-element.19), channel_id=1, source_target_pairs={{0,1},{1,0},{2,3},{3,2},{4,5},{5,4},{6,7},{7,6},{8,9},{9,8},{10,11... | collective-permute-start | bytes 294920 | tf_op jit(solution)/shard_map/ppermute | solution.py:76
  54.5 6.8 %collective-permute-start.11 = (bf16[12,32,128]{2,1,0:T(8,128)(2,1)S(1)}, bf16[12,32,128]{2,1,0:T(8,128)(2,1)S(1)}, u32[]{:S(2)}, u32[]{:S(2)}) collective-permute-start(bf16[12,32,128]{2,1,0:T(8,128)(2,1)S(1)} %get-tuple-element.25), channel_id=1, source_target_pairs={{0,12},{4,8},{8,4},{12,0},{1,13},{5,9},{9,5},{13,1},{2,14},{6,10},... | collective-permute-start | bytes 294920 | tf_op jit(solution)/shard_map/ppermute | solution.py:76
  54.5 7.9 %collective-permute-start.10 = (bf16[12,32,128]{2,1,0:T(8,128)(2,1)S(1)}, bf16[12,32,128]{2,1,0:T(8,128)(2,1)S(1)}, u32[]{:S(2)}, u32[]{:S(2)}) collective-permute-start(bf16[12,32,128]{2,1,0:T(8,128)(2,1)S(1)} %get-tuple-element.24), channel_id=1, source_target_pairs={{0,8},{4,12},{8,0},{12,4},{1,9},{5,13},{9,1},{13,5},{2,10},{6,14},... | collective-permute-start | bytes 294920 | tf_op jit(solution)/shard_map/ppermute | solution.py:76
  56.1 6.4 %collective-permute-start.9 = (bf16[12,32,128]{2,1,0:T(8,128)(2,1)S(1)}, bf16[12,32,128]{2,1,0:T(8,128)(2,1)S(1)}, u32[]{:S(2)}, u32[]{:S(2)}) collective-permute-start(bf16[12,32,128]{2,1,0:T(8,128)(2,1)S(1)} %get-tuple-element.23), channel_id=1, source_target_pairs={{0,4},{4,0},{8,12},{12,8},{1,5},{5,1},{9,13},{13,9},{2,6},{6,2},{1... | collective-permute-start | bytes 294920 | tf_op jit(solution)/shard_map/ppermute | solution.py:76
  56.5 6.7 %collective-permute-start.18 = (bf16[64,128]{1,0:T(8,128)(2,1)S(1)}, bf16[64,128]{1,0:T(8,128)(2,1)S(1)}, u32[]{:S(2)}, u32[]{:S(2)}) collective-permute-start(bf16[64,128]{1,0:T(8,128)(2,1)S(1)} %get-tuple-element.31), channel_id=1, source_target_pairs={{0,1},{1,0},{2,3},{3,2},{4,5},{5,4},{6,7},{7,6},{8,9},{9,8},{10,11... | collective-permute-start | bytes 49160 | tf_op jit(solution)/shard_map/ppermute | solution.py:76
  57.7 5.5 %collective-permute-start.19 = (bf16[64,128]{1,0:T(8,128)(2,1)S(1)}, bf16[64,128]{1,0:T(8,128)(2,1)S(1)}, u32[]{:S(2)}, u32[]{:S(2)}) collective-permute-start(bf16[64,128]{1,0:T(8,128)(2,1)S(1)} %get-tuple-element.31), channel_id=1, source_target_pairs={{0,2},{1,3},{2,0},{3,1},{4,6},{5,7},{6,4},{7,5},{8,10},{9,11},{10,... | collective-permute-start | bytes 49160 | tf_op jit(solution)/shard_map/ppermute | solution.py:76
  61.3 5.5 %collective-permute-start.20 = (bf16[64,128]{1,0:T(8,128)(2,1)S(1)}, bf16[64,128]{1,0:T(8,128)(2,1)S(1)}, u32[]{:S(2)}, u32[]{:S(2)}) collective-permute-start(bf16[64,128]{1,0:T(8,128)(2,1)S(1)} %get-tuple-element.31), channel_id=1, source_target_pairs={{0,3},{1,2},{2,1},{3,0},{4,7},{5,6},{6,5},{7,4},{8,11},{9,10},{10,... | collective-permute-start | bytes 49160 | tf_op jit(solution)/shard_map/ppermute | solution.py:76
  66.9 1.9 %collective-permute-start.21 = (bf16[256,128]{1,0:T(8,128)(2,1)S(1)}, bf16[256,128]{1,0:T(8,128)(2,1)S(1)}, u32[]{:S(2)}, u32[]{:S(2)}) collective-permute-start(bf16[256,128]{1,0:T(8,128)(2,1)S(1)} %bitcast.50), channel_id=1, source_target_pairs={{0,4},{4,0},{8,12},{12,8},{1,5},{5,1},{9,13},{13,9},{2,6},{6,2},{1... | collective-permute-start | bytes 196616 | tf_op jit(solution)/shard_map/ppermute | solution.py:76
  66.9 4.5 %collective-permute-start.22 = (bf16[256,128]{1,0:T(8,128)(2,1)S(1)}, bf16[256,128]{1,0:T(8,128)(2,1)S(1)}, u32[]{:S(2)}, u32[]{:S(2)}) collective-permute-start(bf16[256,128]{1,0:T(8,128)(2,1)S(1)} %bitcast.51), channel_id=1, source_target_pairs={{0,8},{4,12},{8,0},{12,4},{1,9},{5,13},{9,1},{13,5},{2,10},{6,14},... | collective-permute-start | bytes 196616 | tf_op jit(solution)/shard_map/ppermute | solution.py:76
  68.4 4.1 %collective-permute-start.23 = (bf16[256,128]{1,0:T(8,128)(2,1)S(1)}, bf16[256,128]{1,0:T(8,128)(2,1)S(1)}, u32[]{:S(2)}, u32[]{:S(2)}) collective-permute-start(bf16[256,128]{1,0:T(8,128)(2,1)S(1)} %bitcast.52), channel_id=1, source_target_pairs={{0,12},{4,8},{8,4},{12,0},{1,13},{5,9},{9,5},{13,1},{2,14},{6,10},... | collective-permute-start | bytes 196616 | tf_op jit(solution)/shard_map/ppermute | solution.py:76
  (15 other events, 77.8 us)

commit v2 on v1

--- a/solution.py
+++ b/solution.py
@@ -58,7 +58,15 @@
         pieces[k][...] = total[pl.ds((me ^ k) * piece, piece)].astype(pieces[k].dtype)
 
 
-def call(kernel, outs, scratch, name, *operands):
+def hand_out_halves(total, keep, send, axis, axis_size):
+    me = lax.axis_index(axis)
+    piece = keep.shape[1]
+    for k in range(axis_size):
+        out = send if k % 2 else keep
+        out[k // 2] = total[pl.ds((me ^ k) * piece, piece)].astype(out.dtype)
+
+
+def call(kernel, outs, scratch, name, flops, *operands):
     single = not isinstance(outs, (list, tuple))
     return pl.pallas_call(
         kernel,
@@ -66,16 +74,42 @@
         in_specs=[VMEM] * len(operands),
         out_specs=VMEM if single else [VMEM] * len(outs),
         scratch_shapes=list(scratch),
-        compiler_params=pltpu.CompilerParams(vmem_limit_bytes=40 * 1024 * 1024),
+        compiler_params=pltpu.CompilerParams(vmem_limit_bytes=24 * 1024 * 1024),
+        cost_estimate=pl.CostEstimate(flops=flops, bytes_accessed=2**20, transcendentals=0),
         name=name,
     )(*operands)
 
 
-def send_xor(pieces, axis, axis_size):
-    return [pieces[0]] + [
-        lax.ppermute(pieces[k], axis, [(d, d ^ k) for d in range(axis_size)])
-        for k in range(1, axis_size)
-    ]
+def swap(x, axis, k):
+    n = lax.axis_size(axis)
+    return lax.ppermute(x, axis, [(d, d ^ k) for d in range(n)])
+
+
+def after(x, *earlier):
+    return lax.optimization_barrier((x, earlier))[0]
+
+
+def bits_of(n):
+    return [1 << s for s in range(n.bit_length() - 1)]
+
+
+def gather_halves(own, axis, n):
+    parts = {0: own}
+    for bit in reversed(bits_of(n)):
+        for k in sorted(parts):
+            parts[k ^ bit] = swap(parts[k], axis, bit)
+    return [parts[k] for k in range(n)]
+
+
+def gather_direct(own, axis, n):
+    return [own] + [swap(own, axis, k) for k in range(1, n)]
+
+
+def tree_sum(parts):
+    parts = [part.astype(F32) for part in parts]
+    while len(parts) > 1:
+        parts = [parts[i] + parts[i + 1] for i in range(0, len(parts), 2)]
+    return parts[0]
 
 
 def on_device(left_factors, right_factors, out_weight, out_bias, pair_grad):
@@ -88,14 +122,16 @@
     pairs = chan * chan
     row4, chan4 = rows // 4, chan // 4
     inv_samples = 1.0 / samples
+    flops = 2 * rows * cols * pairs * width
+    wide = 2 * LANES
+    half = n_row // 2
+    weight_piece = pairs // n_row
     struct = jax.ShapeDtypeStruct
     weight3 = out_weight.reshape(chan, chan, width)
     grad4 = pair_grad.reshape(row4, 4, cols, width)
 
-    right_parts = send_xor([right] * n_row, "row", n_row)
-    left_parts = send_xor([left] * n_col, "col", n_col)
-
-    wide = 2 * LANES
+    right_parts = gather_halves(right, "row", n_row)
+    left_parts = gather_direct(left, "col", n_col)
 
     def outer_grad_kernel(grad_ref, weight_ref, z_ref, tmp):
         w = swap01(weight_ref[...]).reshape(pairs, width)
@@ -123,6 +159,7 @@
         struct((chan4, 4, cols, rows * chan), BF),
         [pltpu.VMEM((pairs // wide, 4, row4 * cols, wide), BF)],
         "outer_grad",
+        flops,
         grad4,
         weight3,
     )
@@ -147,17 +184,15 @@
         [struct((left_piece, chan, samples), BF)] * n_col,
         [pltpu.VMEM((cols, chan, samples), BF), pltpu.VMEM((rows, chan, samples), F32)],
         "left_grad",
+        flops,
         z,
         *right_parts,
     )
-    left_got = send_xor(left_pieces, "col", n_col)
-
-    weight_piece = pairs // n_row
+    left_parts[-1] = after(left_parts[-1], *left_pieces)
 
     def outer_mean_kernel(grad_ref, *refs):
         a_refs, b_refs = refs[:n_col], refs[n_col : n_col + n_row]
-        y_ref = refs[n_col + n_row]
-        pieces = refs[n_col + n_row + 1 : n_col + 2 * n_row + 1]
+        y_ref, keep, send = refs[n_col + n_row : n_col + n_row + 3]
         a_whole, b_whole, tmp, total = refs[-4:]
         assemble(a_whole, a_refs, "col", n_col)
         assemble(b_whole, b_refs, "row", n_row)
@@ -191,11 +226,15 @@
             acc = d if acc is None else acc + d
         acc = (acc * (inv_samples / (rows * n_row))).reshape(chan, chan, width)
         total[...] = jnp.swapaxes(acc, 0, 1).reshape(pairs, width)
-        hand_out(total, pieces, "row", n_row)
-
-    y, *weight_pieces = call(
+        hand_out_halves(total, keep, send, "row", n_row)
+
+    y, weight_keep, weight_send = call(
         outer_mean_kernel,
-        [struct((row4, 4, cols, pairs), BF)] + [struct((weight_piece, width), BF)] * n_row,
+        [
+            struct((row4, 4, cols, pairs), BF),
+            struct((half, weight_piece, width), F32),
+            struct((half, weight_piece, width), BF),
+        ],
         [
             pltpu.VMEM((rows, chan, samples), BF),
             pltpu.VMEM((cols, chan, samples), BF),
@@ -203,40 +242,89 @@
             pltpu.VMEM((pairs, width), F32),
         ],
         "outer_mean",
+        2 * flops,
         grad4,
         *left_parts,
         *right_parts,
     )
-    weight_got = send_xor(weight_pieces, "row", n_row)
 
     def right_kernel(z_ref, *refs):
-        a_refs, pieces, whole, total = refs[:n_col], refs[n_col : n_col + n_row], refs[-2], refs[-1]
+        a_refs, (keep, send) = refs[:n_col], refs[n_col : n_col + 2]
+        whole, total, turned = refs[-3:]
         assemble(whole, a_refs, "col", n_col)
         am = whole[...].reshape(rows * chan, samples)
         for a in range(4):
             d = dot_nn(z_ref[:, a].reshape(chan4 * cols, rows * chan), xor_groups(am, a, chan))
             total[:, a] = d.reshape(chan4, cols, samples)
-        d = jnp.swapaxes(total[...].reshape(chan, cols, samples), 0, 1) * inv_samples
-        me = lax.axis_index("row")
-        wholes = d.astype(BF)
-        whole2 = refs[-3]
-        whole2[...] = wholes
-        for k in range(n_row):
-            pieces[k][...] = whole2[pl.ds((me ^ k) * right_piece, right_piece)]
-
-    right_pieces = call(
+        turned[...] = jnp.swapaxes(total[...].reshape(chan, cols, samples), 0, 1) * inv_samples
+        hand_out_halves(turned, keep, send, "row", n_row)
+
+    right_keep, right_send = call(
         right_kernel,
-        [struct((right_piece, chan, samples), BF)] * n_row,
         [
-            pltpu.VMEM((cols, chan, samples), BF),
+            struct((half, right_piece, chan, samples), F32),
+            struct((half, right_piece, chan, samples), BF),
+        ],
+        [
             pltpu.VMEM((rows, chan, samples), BF),
             pltpu.VMEM((chan4, 4, cols, samples), F32),
+            pltpu.VMEM((cols, chan, samples), F32),
         ],
         "right_grad",
-        z,
+        flops,
+        after(z, weight_send),
         *left_parts,
     )
-    right_got = send_xor(right_pieces, "row", n_row)
+
+    def halve_kernel(w_keep, w_got, r_keep, r_got, w_next, w_send, r_next, r_send):
+        n = w_keep.shape[0]
+        for k in range(n):
+            w_out, r_out = (w_send, r_send) if k % 2 else (w_next, r_next)
+            w_out[k // 2] = (w_keep[k] + w_got[k].astype(F32)).astype(w_out.dtype)
+            r_out[k // 2] = (r_keep[k] + r_got[k].astype(F32)).astype(r_out.dtype)
+
+    for bit in bits_of(n_row)[:-1]:
+        weight_got = swap(weight_send, "row", bit)
+        right_got = swap(right_send, "row", bit)
+        half = half // 2
+        weight_keep, weight_send, right_keep, right_send = call(
+            halve_kernel,
+            [
+                struct((half, weight_piece, width), F32),
+                struct((half, weight_piece, width), BF),
+                struct((half, right_piece, chan, samples), F32),
+                struct((half, right_piece, chan, samples), BF),
+            ],
+            [],
+            "halve_row_%d" % bit,
+            2**20,
+            weight_keep,
+            weight_got,
+            right_keep,
+            right_got,
+        )
+
+    weight_got = swap(weight_send, "row", n_row // 2)
+    right_got = swap(right_send, "row", n_row // 2)
+    left_pieces = [after(piece, weight_send) for piece in left_pieces]
+    left_got = [left_pieces[0]] + [swap(left_pieces[k], "col", k) for k in range(1, n_col)]
+
+    def last_kernel(w_keep, w_got, r_keep, r_got, w_out, r_out):
+        w_out[...] = (w_keep[0] + w_got[0].astype(F32)).astype(w_out.dtype)
+        r_out[...] = r_keep[...] + r_got[...].astype(F32)
+
+    weight_own, grad_right = call(
+        last_kernel,
+        [struct((weight_piece, width), BF), struct((1, right_piece, chan, samples), F32)],
+        [],
+        "halve_row_last",
+        2**20,
+        weight_keep,
+        weight_got,
+        right_keep,
+        right_got,
+    )
+    weight_cols = gather_direct(weight_own, "col", n_col)
 
     def pair_kernel(y_ref, weight_ref, bias_ref, p_ref):
         w = swap01(weight_ref[...]).reshape(pairs, width)
@@ -249,40 +337,31 @@
         struct((row4, 4, cols, width), BF),
         [],
         "pair_update",
-        y,
+        flops,
+        after(y, weight_own),
         weight3,
         out_bias.reshape(1, width),
-    ).reshape(rows, cols, width)
-
-    def add_up(parts):
-        total = parts[0].astype(F32)
-        for part in parts[1:]:
-            total = total + part.astype(F32)
-        return total
-
-    weight_row = add_up(weight_got)
-    col_me = lax.axis_index("col")
-    row_me = lax.axis_index("row")
-    fine = weight_piece // n_col
-    weight_fine = [
-        lax.dynamic_slice_in_dim(weight_row, (col_me ^ k) * fine, fine, 0) for k in range(n_col)
-    ]
-    weight_sum = add_up(send_xor(weight_fine, "col", n_col))
-    col_parts = send_xor([weight_sum] * n_col, "col", n_col)
-    mine = jnp.zeros((n_col, fine, width), F32)
-    for k in range(n_col):
-        mine = lax.dynamic_update_slice_in_dim(mine, col_parts[k][None], col_me ^ k, 0)
-    mine = mine.reshape(weight_piece, width).astype(BF)
-    row_parts = send_xor([mine] * n_row, "row", n_row)
-    grad_weight = jnp.zeros((n_row, weight_piece, width), F32)
-    for k in range(n_row):
-        grad_weight = lax.dynamic_update_slice_in_dim(
-            grad_weight, row_parts[k][None].astype(F32), row_me ^ k, 0
-        )
-    grad_weight = grad_weight.reshape(pairs, width)
-    grad_left = add_up(left_got)[None]
-    grad_right = add_up(right_got)[None]
-    return (pair_update, grad_left, grad_right, grad_weight)
+    )
+    grad_left = tree_sum(left_got)[None]
+    weight_cols[-1] = after(weight_cols[-1], pair_update, grad_left)
+
+    def col_sum_kernel(*refs):
+        refs[-1][...] = tree_sum([ref[...] for ref in refs[:-1]]).astype(BF)
+
+    weight_sum = call(
+        col_sum_kernel, struct((weight_piece, width), BF), [], "weight_col_sum", 2**20, *weight_cols
+    )
+    weight_rows = gather_halves(weight_sum, "row", n_row)
+
+    def place_kernel(*refs):
+        me = lax.axis_index("row")
+        for k in range(n_row):
+            refs[-1][pl.ds((me ^ k) * weight_piece, weight_piece)] = refs[k][...].astype(F32)
+
+    grad_weight = call(
+        place_kernel, struct((pairs, width), F32), [], "weight_place", 2**20, *weight_rows
+    )
+    return (pair_update.reshape(rows, cols, width), grad_left, grad_right, grad_weight)
 
 
 def solution(mesh):

time: 73.8 us -> 53.1 us (0.72)
  local copies, waits for them, and re-layouts: 14.7 us -> 2.04 us
  starting transfers between devices: 26.8 us -> 19.5 us
  Pallas kernels: 11.4 us -> 13.1 us
  waiting for transfers between devices: 18.1 us -> 16.8 us
  other arithmetic: 1.57 us -> 0.73 us
    unnamed x30 -> x14, local copies, waits for them, and re-layouts: 14.6 us -> 2.04 us
    ppermute x24 -> x19, starting transfers between devices: 26.8 us -> 19.5 us  [swap(): return lax.ppermute(x, axis, [(d, d ^ k) for d in range(n)])]
    pallas_call x5 -> x9, Pallas kernels: 11.4 us -> 13.1 us  [call(): pl.pallas_call(kernel, out_shape=outs, in_specs=[VMEM] * len(operands), o...]
    ppermute x24 -> x19, waiting for transfers between devices: 18.1 us -> 16.8 us  [swap(): return lax.ppermute(x, axis, [(d, d ^ k) for d in range(n)])]
  transfers between devices with their start and end apart: 24 -> 19, of which waited for: 7 -> 7; matrix products, arithmetic and copies ran while one was open for 2% -> 1% of each run, Pallas kernels for 10% -> 12%
where the time goes in v2:
time: 53.1 us; the launch traced here: 52.9 us
  starting transfers between devices  19.5 us (37%)
  waiting for transfers between devices  16.8 us (32%)
  Pallas kernels  13.1 us (25%)
  local copies, waits for them, and re-layouts  2.04 us (4%)
  between operations  0.75 us (1%)
  other arithmetic  0.73 us (1%)
    ppermute x19, starting transfers between devices, swap(): return lax.ppermute(x, axis, [(d, d ^ k) for d in range(n)])  19.5 us
    ppermute x19, waiting for transfers between devices, swap(): return lax.ppermute(x, axis, [(d, d ^ k) for d in range(n)])  16.8 us
    pallas_call x9, Pallas kernels, call(): pl.pallas_call(kernel, out_shape=outs, in_specs=[VMEM] * len(operands), o...  13.1 us
    unnamed x14, local copies, waits for them, and re-layouts  2.04 us
  transfers between devices with their start and end apart: 19, of which 7 were waited for; matrix products, arithmetic and copies ran while one was open for 1% of the time, Pallas kernels for 12%

profile of v2, /device:TPU:0, one launch (start us, length us, event | category | flops | bytes accessed | tf_op | source)
XLA Modules:
  0.0 52.9 jit_solution(777218604341984400)
XLA Ops:
  0.6 3.0 %collective-permute-start.4 = (bf16[12,32,128]{2,1,0:T(8,128)(2,1)}, bf16[12,32,128]{2,1,0:T(8,128)(2,1)S(1)}, u32[]{:S(2)}, u32[]{:S(2)}) collective-permute-start(bf16[12,32,128]{2,1,0:T(8,128)(2,1)} %bitcast.12), channel_id=1, source_target_pairs={{0,8},{4,12},{8,0},{12,4},{1,9},{5,13},{9,1},{13,5},{2,10},{6,14},... | collective-permute-start | bytes 294920 | tf_op jit(solution)/shard_map/ppermute | solution.py:85
  3.6 3.0 %collective-permute-done.4.refs_2_.refs_6_ = bf16[12,32,128]{2,1,0:T(8,128)(2,1)S(1)} collective-permute-done((bf16[12,32,128]{2,1,0:T(8,128)(2,1)}, bf16[12,32,128]{2,1,0:T(8,128)(2,1)S(1)}, u32[]{:S(2)}, u32[]{:S(2)}) %collective-permute-start.4) | collective-permute-done | bytes 98336 | tf_op jit(solution)/shard_map/ppermute | solution.py:85
  6.6 3.9 %collective-permute-start.2 = (bf16[12,32,128]{2,1,0:T(8,128)(2,1)}, bf16[12,32,128]{2,1,0:T(8,128)(2,1)S(1)}, u32[]{:S(2)}, u32[]{:S(2)}) collective-permute-start(bf16[12,32,128]{2,1,0:T(8,128)(2,1)} %bitcast.16), channel_id=1, source_target_pairs={{0,3},{1,2},{2,1},{3,0},{4,7},{5,6},{6,5},{7,4},{8,11},{9,10},{10,... | collective-permute-start | bytes 294920 | tf_op jit(solution)/shard_map/ppermute | solution.py:85
  11.1 0.9 %copy-done = bf16[1024,128]{1,0:T(8,128)(2,1)S(1)} copy-done((bf16[1024,128]{1,0:T(8,128)(2,1)S(1)}, bf16[1024,128]{1,0:T(8,128)(2,1)}, u32[]{:S(2)}) %copy-start) | copy-done | bytes 262168
  12.1 1.1 %copy-done.2 = bf16[48,48,128]{2,1,0:T(8,128)(2,1)S(1)} copy-done((bf16[48,48,128]{2,1,0:T(8,128)(2,1)S(1)}, bf16[48,48,128]{2,1,0:T(8,128)(2,1)}, u32[]{:S(2)}) %copy-start.2) | copy-done | bytes 589848
  13.2 2.0 %outer_grad.1.z_ref = bf16[8,4,48,1536]{3,2,1,0:T(8,128)(2,1)S(1)} custom-call(bf16[12,4,48,128]{3,2,1,0:T(8,128)(2,1)S(1)} %bitcast.10, bf16[32,32,128]{2,1,0:T(8,128)(2,1)S(1)} %bitcast.8), custom_call_target="tpu_custom_call" | custom-call | flops 603979776 | bytes 1048576 | tf_op jit(solution)/shard_map/outer_grad/pallas_call | solution.py:71
  15.2 1.6 %left_grad.1 = (bf16[12,32,128]{2,1,0:T(8,128)(2,1)S(1)}, bf16[12,32,128]{2,1,0:T(8,128)(2,1)S(1)}, bf16[12,32,128]{2,1,0:T(8,128)(2,1)S(1)}, bf16[12,32,128]{2,1,0:T(8,128)(2,1)S(1)}) custom-call(bf16[8,4,48,1536]{3,2,1,0:T(8,128)(2,1)S(1)} %outer_grad.1.z_ref, bf16[12,32,128]{2,1,0:T(8,128)(2,1)S(1)} %bitcast.14, ...), custom_call_target="tpu_custom_call" | custom-call | flops 603979776 | bytes 1048576 | tf_op jit(solution)/shard_map/left_grad/pallas_call | solution.py:71
  16.8 2.9 %collective-permute-done.1.refs_2_ = bf16[12,32,128]{2,1,0:T(8,128)(2,1)S(1)} collective-permute-done((bf16[12,32,128]{2,1,0:T(8,128)(2,1)}, bf16[12,32,128]{2,1,0:T(8,128)(2,1)S(1)}, u32[]{:S(2)}, u32[]{:S(2)}) %collective-permute-start.1) | collective-permute-done | bytes 98336 | tf_op jit(solution)/shard_map/ppermute | solution.py:85
  19.7 4.1 %outer_mean.1 = (bf16[12,4,48,1024]{3,2,1,0:T(8,128)(2,1)S(1)}, f32[2,256,128]{2,1,0:T(8,128)S(1)}, bf16[2,256,128]{2,1,0:T(8,128)(2,1)S(1)}) custom-call(bf16[12,4,48,128]{3,2,1,0:T(8,128)(2,1)S(1)} %bitcast.11, bf16[12,32,128]{2,1,0:T(8,128)(2,1)S(1)} %bitcast.19, bf16[12,32,128]{2,1,0:T(8,128)(2,1)S(1)} %collective-permute-done.refs_1_, ...), custom_call_target="tpu_custom_call" | custom-call | flops 1207959552 | bytes 1048576 | tf_op jit(solution)/shard_map/outer_mean/pallas_call | solution.py:71
  23.8 1.5 %right_grad.1 = (f32[2,12,32,128]{3,2,1,0:T(8,128)S(1)}, bf16[2,12,32,128]{3,2,1,0:T(8,128)(2,1)S(1)}) custom-call(bf16[8,4,48,1536]{3,2,1,0:T(8,128)(2,1)S(1)} %outer_grad.1.z_ref, bf16[12,32,128]{2,1,0:T(8,128)(2,1)S(1)} %bitcast.20, bf16[12,32,128]{2,1,0:T(8,128)(2,1)S(1)} %collective-permute-done.refs_1_, ...), custom_call_target="tpu_custom_call" | custom-call | flops 603979776 | bytes 1048576 | tf_op jit(solution)/shard_map/right_grad/pallas_call | solution.py:71
  26.0 1.1 %collective-permute-done.6.w_got = bf16[2,256,128]{2,1,0:T(8,128)(2,1)S(1)} collective-permute-done((bf16[2,256,128]{2,1,0:T(8,128)(2,1)S(1)}, bf16[2,256,128]{2,1,0:T(8,128)(2,1)S(1)}, u32[]{:S(2)}, u32[]{:S(2)}) %collective-permute-start.6) | collective-permute-done | bytes 131104 | tf_op jit(solution)/shard_map/ppermute | solution.py:85
  27.1 1.5 %collective-permute-start.9 = (bf16[1,12,32,128]{3,2,1,0:T(8,128)(2,1)S(1)}, bf16[1,12,32,128]{3,2,1,0:T(8,128)(2,1)S(1)}, u32[]{:S(2)}, u32[]{:S(2)}) collective-permute-start(bf16[1,12,32,128]{3,2,1,0:T(8,128)(2,1)S(1)} %get-tuple-element.41), channel_id=1, source_target_pairs={{0,8},{4,12},{8,0},{12,4},{1,9},{5,13},{9,1},{13,5},{2,10},{6,14},... | collective-permute-start | bytes 294920 | tf_op jit(solution)/shard_map/ppermute | solution.py:85
  29.2 2.5 %collective-permute-start.11 = (bf16[12,32,128]{2,1,0:T(8,128)(2,1)S(1)}, bf16[12,32,128]{2,1,0:T(8,128)(2,1)S(1)}, u32[]{:S(2)}, u32[]{:S(2)}) collective-permute-start(bf16[12,32,128]{2,1,0:T(8,128)(2,1)S(1)} %get-tuple-element.46), channel_id=1, source_target_pairs={{0,2},{1,3},{2,0},{3,1},{4,6},{5,7},{6,4},{7,5},{8,10},{9,11},{10,... | collective-permute-start | bytes 294920 | tf_op jit(solution)/shard_map/ppermute | solution.py:85
  31.7 1.3 %collective-permute-start.12 = (bf16[12,32,128]{2,1,0:T(8,128)(2,1)S(1)}, bf16[12,32,128]{2,1,0:T(8,128)(2,1)S(1)}, u32[]{:S(2)}, u32[]{:S(2)}) collective-permute-start(bf16[12,32,128]{2,1,0:T(8,128)(2,1)S(1)} %get-tuple-element.47), channel_id=1, source_target_pairs={{0,3},{1,2},{2,1},{3,0},{4,7},{5,6},{6,5},{7,4},{8,11},{9,10},{10,... | collective-permute-start | bytes 294920 | tf_op jit(solution)/shard_map/ppermute | solution.py:85
  33.6 3.7 %collective-permute-done.8.w_got = bf16[1,256,128]{2,1,0:T(8,128)(2,1)S(1)} collective-permute-done((bf16[1,256,128]{2,1,0:T(8,128)(2,1)S(1)}, bf16[1,256,128]{2,1,0:T(8,128)(2,1)S(1)}, u32[]{:S(2)}, u32[]{:S(2)}) %collective-permute-start.8) | collective-permute-done | bytes 65568 | tf_op jit(solution)/shard_map/ppermute | solution.py:85
  37.3 0.7 %halve_row_last.1 = (bf16[256,128]{1,0:T(8,128)(2,1)S(1)}, f32[1,12,32,128]{3,2,1,0:T(8,128)}) custom-call(f32[1,256,128]{2,1,0:T(8,128)S(1)} %get-tuple-element.38.w_keep, bf16[1,256,128]{2,1,0:T(8,128)(2,1)S(1)} %collective-permute-done.8.w_got, f32[1,12,32,128]{3,2,1,0:T(8,128)S(1)} %get-tuple-element.40.r_keep, ...), custom_call_target="tpu_custom_call" | custom-call | flops 1048576 | bytes 1048576 | tf_op jit(solution)/shard_map/halve_row_last/pallas_call | solution.py:71
  38.0 2.5 %collective-permute-start.15 = (bf16[256,128]{1,0:T(8,128)(2,1)S(1)}, bf16[256,128]{1,0:T(8,128)(2,1)S(1)}, u32[]{:S(2)}, u32[]{:S(2)}) collective-permute-start(bf16[256,128]{1,0:T(8,128)(2,1)S(1)} %get-tuple-element.42.refs_0_), channel_id=1, source_target_pairs={{0,3},{1,2},{2,1},{3,0},{4,7},{5,6},{6,5},{7,4},{8,11},{9,10},{10,... | collective-permute-start | bytes 196616 | tf_op jit(solution)/shard_map/ppermute | solution.py:85
  40.5 1.9 %collective-permute-start.13 = (bf16[256,128]{1,0:T(8,128)(2,1)S(1)}, bf16[256,128]{1,0:T(8,128)(2,1)S(1)}, u32[]{:S(2)}, u32[]{:S(2)}) collective-permute-start(bf16[256,128]{1,0:T(8,128)(2,1)S(1)} %get-tuple-element.42.refs_0_), channel_id=1, source_target_pairs={{0,1},{1,0},{2,3},{3,2},{4,5},{5,4},{6,7},{7,6},{8,9},{9,8},{10,11... | collective-permute-start | bytes 196616 | tf_op jit(solution)/shard_map/ppermute | solution.py:85
  42.4 0.7 %add_bitcast_fusion = f32[1,12,32,128]{3,2,1,0:T(8,128)} fusion(bf16[12,32,128]{2,1,0:T(8,128)(2,1)S(1)} %collective-permute-done.12, bf16[12,32,128]{2,1,0:T(8,128)(2,1)S(1)} %collective-permute-done.11, bf16[12,32,128]{2,1,0:T(8,128)(2,1)S(1)} %collective-permute-done.10, bf16[12,32,128]{2,1,0:T(8,128)(2,1)S(1)} %get-tuple-element.44), kind=kLoop, calls=%fused_computation | loop fusion | flops 344064 | bytes 589824 | tf_op jit(solution)/shard_map/broadcast_in_dim | solution.py:345
  43.2 2.2 %pair_update.1 = bf16[12,4,48,128]{3,2,1,0:T(8,128)(2,1)} custom-call(bf16[12,4,48,1024]{3,2,1,0:T(8,128)(2,1)S(1)} %get-tuple-element.43.y_ref, bf16[32,32,128]{2,1,0:T(8,128)(2,1)S(1)} %bitcast.9, f32[1,128]{1,0:T(1,128)S(1)} %bitcast.21), custom_call_target="tpu_custom_call" | custom-call | flops 603979776 | bytes 1048576 | tf_op jit(solution)/shard_map/pair_update/pallas_call | solution.py:71
  45.4 1.1 %collective-permute-done.14.refs_2_ = bf16[256,128]{1,0:T(8,128)(2,1)S(1)} collective-permute-done((bf16[256,128]{1,0:T(8,128)(2,1)S(1)}, bf16[256,128]{1,0:T(8,128)(2,1)S(1)}, u32[]{:S(2)}, u32[]{:S(2)}) %collective-permute-start.14) | collective-permute-done | bytes 65568 | tf_op jit(solution)/shard_map/ppermute | solution.py:85
  47.1 3.7 %collective-permute-done.17.refs_2_ = bf16[256,128]{1,0:T(8,128)(2,1)S(1)} collective-permute-done((bf16[256,128]{1,0:T(8,128)(2,1)S(1)}, bf16[256,128]{1,0:T(8,128)(2,1)S(1)}, u32[]{:S(2)}, u32[]{:S(2)}) %collective-permute-start.17) | collective-permute-done | bytes 65568 | tf_op jit(solution)/shard_map/ppermute | solution.py:85
  50.8 1.2 %collective-permute-done.18.refs_3_ = bf16[256,128]{1,0:T(8,128)(2,1)S(1)} collective-permute-done((bf16[256,128]{1,0:T(8,128)(2,1)S(1)}, bf16[256,128]{1,0:T(8,128)(2,1)S(1)}, u32[]{:S(2)}, u32[]{:S(2)}) %collective-permute-start.18) | collective-permute-done | bytes 65568 | tf_op jit(solution)/shard_map/ppermute | solution.py:85
  52.1 0.8 %weight_place.1 = f32[1024,128]{1,0:T(8,128)} custom-call(bf16[256,128]{1,0:T(8,128)(2,1)S(1)} %weight_col_sum.1.refs_0_, bf16[256,128]{1,0:T(8,128)(2,1)S(1)} %collective-permute-done.16.refs_1_, bf16[256,128]{1,0:T(8,128)(2,1)S(1)} %collective-permute-done.17.refs_2_, bf16[256,128]{1,0:T(8,128)(2,1)S(1)} %collective-permute-done.18.refs_3_), custom_call_target="tpu_custom_call" | custom-call | flops 1048576 | bytes 1048576 | tf_op jit(solution)/shard_map/weight_place/pallas_call | solution.py:71
  (38 shorter events, 3.0 us)
Async XLA Ops:
  0.6 6.0 %collective-permute-start.4 = (bf16[12,32,128]{2,1,0:T(8,128)(2,1)}, bf16[12,32,128]{2,1,0:T(8,128)(2,1)S(1)}, u32[]{:S(2)}, u32[]{:S(2)}) collective-permute-start(bf16[12,32,128]{2,1,0:T(8,128)(2,1)} %bitcast.12), channel_id=1, source_target_pairs={{0,8},{4,12},{8,0},{12,4},{1,9},{5,13},{9,1},{13,5},{2,10},{6,14},... | collective-permute-start | bytes 294920 | tf_op jit(solution)/shard_map/ppermute | solution.py:85
  3.6 11.5 %collective-permute-start.3 = (bf16[12,32,128]{2,1,0:T(8,128)(2,1)}, bf16[12,32,128]{2,1,0:T(8,128)(2,1)S(1)}, u32[]{:S(2)}, u32[]{:S(2)}) collective-permute-start(bf16[12,32,128]{2,1,0:T(8,128)(2,1)} %bitcast.13), channel_id=1, source_target_pairs={{0,4},{4,0},{8,12},{12,8},{1,5},{5,1},{9,13},{13,9},{2,6},{6,2},{1... | collective-permute-start | bytes 294920 | tf_op jit(solution)/shard_map/ppermute | solution.py:85
  6.6 8.5 %collective-permute-start.5 = (bf16[12,32,128]{2,1,0:T(8,128)(2,1)S(1)}, bf16[12,32,128]{2,1,0:T(8,128)(2,1)S(1)}, u32[]{:S(2)}, u32[]{:S(2)}) collective-permute-start(bf16[12,32,128]{2,1,0:T(8,128)(2,1)S(1)} %collective-permute-done.4.refs_2_.refs_6_), channel_id=1, source_target_pairs={{0,4},{4,0},{8,12},{12,8},{1,5},{5,1},{9,13},{13,9},{2,6},{6,2},{1... | collective-permute-start | bytes 294920 | tf_op jit(solution)/shard_map/ppermute | solution.py:85
  6.6 10.1 %collective-permute-start.2 = (bf16[12,32,128]{2,1,0:T(8,128)(2,1)}, bf16[12,32,128]{2,1,0:T(8,128)(2,1)S(1)}, u32[]{:S(2)}, u32[]{:S(2)}) collective-permute-start(bf16[12,32,128]{2,1,0:T(8,128)(2,1)} %bitcast.16), channel_id=1, source_target_pairs={{0,3},{1,2},{2,1},{3,0},{4,7},{5,6},{6,5},{7,4},{8,11},{9,10},{10,... | collective-permute-start | bytes 294920 | tf_op jit(solution)/shard_map/ppermute | solution.py:85
  10.6 9.1 %collective-permute-start.1 = (bf16[12,32,128]{2,1,0:T(8,128)(2,1)}, bf16[12,32,128]{2,1,0:T(8,128)(2,1)S(1)}, u32[]{:S(2)}, u32[]{:S(2)}) collective-permute-start(bf16[12,32,128]{2,1,0:T(8,128)(2,1)} %bitcast.17), channel_id=1, source_target_pairs={{0,2},{1,3},{2,0},{3,1},{4,6},{5,7},{6,4},{7,5},{8,10},{9,11},{10,... | collective-permute-start | bytes 294920 | tf_op jit(solution)/shard_map/ppermute | solution.py:85
  10.6 9.1 %collective-permute-start = (bf16[12,32,128]{2,1,0:T(8,128)(2,1)}, bf16[12,32,128]{2,1,0:T(8,128)(2,1)S(1)}, u32[]{:S(2)}, u32[]{:S(2)}) collective-permute-start(bf16[12,32,128]{2,1,0:T(8,128)(2,1)} %bitcast.18), channel_id=1, source_target_pairs={{0,1},{1,0},{2,3},{3,2},{4,5},{5,4},{6,7},{7,6},{8,9},{9,8},{10,11... | collective-permute-start | bytes 294920 | tf_op jit(solution)/shard_map/ppermute | solution.py:85
  13.2 2.0 %copy-start.4 = (bf16[1,12,32,128]{3,2,1,0:T(8,128)(2,1)S(1)}, bf16[1,12,32,128]{3,2,1,0:T(8,128)(2,1)}, u32[]{:S(2)}) copy-start(bf16[1,12,32,128]{3,2,1,0:T(8,128)(2,1)} %param.6) | copy-start | bytes 294916
  13.2 6.6 %copy-start.3 = (bf16[48,48,128]{2,1,0:T(8,128)(2,1)S(1)}, bf16[48,48,128]{2,1,0:T(8,128)(2,1)}, u32[]{:S(2)}) copy-start(bf16[48,48,128]{2,1,0:T(8,128)(2,1)} %param.9) | copy-start | bytes 1769476
  13.2 6.6 %copy-start.5 = (bf16[1,12,32,128]{3,2,1,0:T(8,128)(2,1)S(1)}, bf16[1,12,32,128]{3,2,1,0:T(8,128)(2,1)}, u32[]{:S(2)}) copy-start(bf16[1,12,32,128]{3,2,1,0:T(8,128)(2,1)} %param.5) | copy-start | bytes 294916
  16.8 26.4 %copy-start.1 = (bf16[1024,128]{1,0:T(8,128)(2,1)S(1)}, bf16[1024,128]{1,0:T(8,128)(2,1)}, u32[]{:S(2)}) copy-start(bf16[1024,128]{1,0:T(8,128)(2,1)} %param.7) | copy-start | bytes 786436
  16.8 26.4 %copy-start.6 = (f32[128]{0:T(128)S(1)}, f32[128]{0:T(128)}, u32[]{:S(2)}) copy-start(f32[128]{0:T(128)} %param.8) | copy-start | bytes 1540
  25.4 1.7 %collective-permute-start.7 = (bf16[2,12,32,128]{3,2,1,0:T(8,128)(2,1)S(1)}, bf16[2,12,32,128]{3,2,1,0:T(8,128)(2,1)S(1)}, u32[]{:S(2)}, u32[]{:S(2)}) collective-permute-start(bf16[2,12,32,128]{3,2,1,0:T(8,128)(2,1)S(1)} %get-tuple-element.37), channel_id=1, source_target_pairs={{0,4},{4,0},{8,12},{12,8},{1,5},{5,1},{9,13},{13,9},{2,6},{6,2},{1... | collective-permute-start | bytes 589832 | tf_op jit(solution)/shard_map/ppermute | solution.py:85
  25.5 1.6 %collective-permute-start.6 = (bf16[2,256,128]{2,1,0:T(8,128)(2,1)S(1)}, bf16[2,256,128]{2,1,0:T(8,128)(2,1)S(1)}, u32[]{:S(2)}, u32[]{:S(2)}) collective-permute-start(bf16[2,256,128]{2,1,0:T(8,128)(2,1)S(1)} %get-tuple-element.34), channel_id=1, source_target_pairs={{0,4},{4,0},{8,12},{12,8},{1,5},{5,1},{9,13},{13,9},{2,6},{6,2},{1... | collective-permute-start | bytes 393224 | tf_op jit(solution)/shard_map/ppermute | solution.py:85
  27.1 10.2 %collective-permute-start.9 = (bf16[1,12,32,128]{3,2,1,0:T(8,128)(2,1)S(1)}, bf16[1,12,32,128]{3,2,1,0:T(8,128)(2,1)S(1)}, u32[]{:S(2)}, u32[]{:S(2)}) collective-permute-start(bf16[1,12,32,128]{3,2,1,0:T(8,128)(2,1)S(1)} %get-tuple-element.41), channel_id=1, source_target_pairs={{0,8},{4,12},{8,0},{12,4},{1,9},{5,13},{9,1},{13,5},{2,10},{6,14},... | collective-permute-start | bytes 294920 | tf_op jit(solution)/shard_map/ppermute | solution.py:85
  28.7 11.8 %collective-permute-start.10 = (bf16[12,32,128]{2,1,0:T(8,128)(2,1)S(1)}, bf16[12,32,128]{2,1,0:T(8,128)(2,1)S(1)}, u32[]{:S(2)}, u32[]{:S(2)}) collective-permute-start(bf16[12,32,128]{2,1,0:T(8,128)(2,1)S(1)} %get-tuple-element.45), channel_id=1, source_target_pairs={{0,1},{1,0},{2,3},{3,2},{4,5},{5,4},{6,7},{7,6},{8,9},{9,8},{10,11... | collective-permute-start | bytes 294920 | tf_op jit(solution)/shard_map/ppermute | solution.py:85
  29.2 13.2 %collective-permute-start.11 = (bf16[12,32,128]{2,1,0:T(8,128)(2,1)S(1)}, bf16[12,32,128]{2,1,0:T(8,128)(2,1)S(1)}, u32[]{:S(2)}, u32[]{:S(2)}) collective-permute-start(bf16[12,32,128]{2,1,0:T(8,128)(2,1)S(1)} %get-tuple-element.46), channel_id=1, source_target_pairs={{0,2},{1,3},{2,0},{3,1},{4,6},{5,7},{6,4},{7,5},{8,10},{9,11},{10,... | collective-permute-start | bytes 294920 | tf_op jit(solution)/shard_map/ppermute | solution.py:85
  31.7 10.7 %collective-permute-start.12 = (bf16[12,32,128]{2,1,0:T(8,128)(2,1)S(1)}, bf16[12,32,128]{2,1,0:T(8,128)(2,1)S(1)}, u32[]{:S(2)}, u32[]{:S(2)}) collective-permute-start(bf16[12,32,128]{2,1,0:T(8,128)(2,1)S(1)} %get-tuple-element.47), channel_id=1, source_target_pairs={{0,3},{1,2},{2,1},{3,0},{4,7},{5,6},{6,5},{7,4},{8,11},{9,10},{10,... | collective-permute-start | bytes 294920 | tf_op jit(solution)/shard_map/ppermute | solution.py:85
  33.1 4.3 %collective-permute-start.8 = (bf16[1,256,128]{2,1,0:T(8,128)(2,1)S(1)}, bf16[1,256,128]{2,1,0:T(8,128)(2,1)S(1)}, u32[]{:S(2)}, u32[]{:S(2)}) collective-permute-start(bf16[1,256,128]{2,1,0:T(8,128)(2,1)S(1)} %get-tuple-element.39), channel_id=1, source_target_pairs={{0,8},{4,12},{8,0},{12,4},{1,9},{5,13},{9,1},{13,5},{2,10},{6,14},... | collective-permute-start | bytes 196616 | tf_op jit(solution)/shard_map/ppermute | solution.py:85
  38.0 7.4 %collective-permute-start.15 = (bf16[256,128]{1,0:T(8,128)(2,1)S(1)}, bf16[256,128]{1,0:T(8,128)(2,1)S(1)}, u32[]{:S(2)}, u32[]{:S(2)}) collective-permute-start(bf16[256,128]{1,0:T(8,128)(2,1)S(1)} %get-tuple-element.42.refs_0_), channel_id=1, source_target_pairs={{0,3},{1,2},{2,1},{3,0},{4,7},{5,6},{6,5},{7,4},{8,11},{9,10},{10,... | collective-permute-start | bytes 196616 | tf_op jit(solution)/shard_map/ppermute | solution.py:85
  40.5 5.9 %collective-permute-start.14 = (bf16[256,128]{1,0:T(8,128)(2,1)S(1)}, bf16[256,128]{1,0:T(8,128)(2,1)S(1)}, u32[]{:S(2)}, u32[]{:S(2)}) collective-permute-start(bf16[256,128]{1,0:T(8,128)(2,1)S(1)} %get-tuple-element.42.refs_0_), channel_id=1, source_target_pairs={{0,2},{1,3},{2,0},{3,1},{4,6},{5,7},{6,4},{7,5},{8,10},{9,11},{10,... | collective-permute-start | bytes 196616 | tf_op jit(solution)/shard_map/ppermute | solution.py:85
  40.5 5.9 %collective-permute-start.13 = (bf16[256,128]{1,0:T(8,128)(2,1)S(1)}, bf16[256,128]{1,0:T(8,128)(2,1)S(1)}, u32[]{:S(2)}, u32[]{:S(2)}) collective-permute-start(bf16[256,128]{1,0:T(8,128)(2,1)S(1)} %get-tuple-element.42.refs_0_), channel_id=1, source_target_pairs={{0,1},{1,0},{2,3},{3,2},{4,5},{5,4},{6,7},{7,6},{8,9},{9,8},{10,11... | collective-permute-start | bytes 196616 | tf_op jit(solution)/shard_map/ppermute | solution.py:85
  46.5 4.3 %collective-permute-start.17 = (bf16[256,128]{1,0:T(8,128)(2,1)S(1)}, bf16[256,128]{1,0:T(8,128)(2,1)S(1)}, u32[]{:S(2)}, u32[]{:S(2)}) collective-permute-start(bf16[256,128]{1,0:T(8,128)(2,1)S(1)} %weight_col_sum.1.refs_0_), channel_id=1, source_target_pairs={{0,8},{4,12},{8,0},{12,4},{1,9},{5,13},{9,1},{13,5},{2,10},{6,14},... | collective-permute-start | bytes 196616 | tf_op jit(solution)/shard_map/ppermute | solution.py:85
  47.1 3.7 %collective-permute-start.16 = (bf16[256,128]{1,0:T(8,128)(2,1)S(1)}, bf16[256,128]{1,0:T(8,128)(2,1)S(1)}, u32[]{:S(2)}, u32[]{:S(2)}) collective-permute-start(bf16[256,128]{1,0:T(8,128)(2,1)S(1)} %weight_col_sum.1.refs_0_), channel_id=1, source_target_pairs={{0,4},{4,0},{8,12},{12,8},{1,5},{5,1},{9,13},{13,9},{2,6},{6,2},{1... | collective-permute-start | bytes 196616 | tf_op jit(solution)/shard_map/ppermute | solution.py:85
  50.8 1.3 %collective-permute-start.18 = (bf16[256,128]{1,0:T(8,128)(2,1)S(1)}, bf16[256,128]{1,0:T(8,128)(2,1)S(1)}, u32[]{:S(2)}, u32[]{:S(2)}) collective-permute-start(bf16[256,128]{1,0:T(8,128)(2,1)S(1)} %collective-permute-done.17.refs_2_), channel_id=1, source_target_pairs={{0,4},{4,0},{8,12},{12,8},{1,5},{5,1},{9,13},{13,9},{2,6},{6,2},{1... | collective-permute-start | bytes 196616 | tf_op jit(solution)/shard_map/ppermute | solution.py:85
  (2 other events, 2.0 us)

commit v3 on v0

v3 whole, which is shorter than its diff:
```python
import jax
import jax.numpy as jnp
from jax import lax
from jax.experimental import pallas as pl
from jax.experimental.pallas import tpu as pltpu
from jax.sharding import PartitionSpec as P

BF = jnp.bfloat16
F32 = jnp.float32
VMEM = pl.BlockSpec(memory_space=pltpu.VMEM)
LANES = 128


def dot_nt(x, y):
    return lax.dot_general(x, y, (((1,), (1,)), ((), ())), preferred_element_type=F32)


def dot_tn(x, y):
    return lax.dot_general(x, y, (((0,), (0,)), ((), ())), preferred_element_type=F32)


def dot_nn(x, y):
    return lax.dot_general(x, y, (((1,), (0,)), ((), ())), preferred_element_type=F32)


def swap01(x):
    return jnp.swapaxes(x.astype(F32), 0, 1).astype(x.dtype)


def xor_groups(x, a, chan):
    n = x.shape[0] // (4 * chan)
    x4 = x.reshape(n, 4, chan, x.shape[-1])
    return jnp.concatenate([x4[:, p ^ a][:, None] for p in range(4)], axis=1).reshape(x.shape)


def lane_masks(rows, chan):
    group = lax.broadcasted_iota(jnp.int32, (rows, LANES), 1) // chan
    return (group % 2) == 1, (group // 2) == 1


def trade(xs, masks):
    low, high = masks
    u = [jnp.where(low, xs[a ^ 1], xs[a]) for a in range(4)]
    return [jnp.where(high, u[b ^ 2], u[b]) for b in range(4)]


def assemble(scratch, parts, first, me):
    piece = parts[0].shape[0]
    count = scratch.shape[0] // piece
    for k, part in enumerate(parts):
        scratch[pl.ds(((me ^ (first + k)) % count) * piece, piece)] = part[...]


def call(kernel, outs, scratch, name, *operands, cost=1, hbm_in=(), hbm_out=()):
    hbm = pl.BlockSpec(memory_space=pltpu.HBM)
    return pl.pallas_call(
        kernel,
        out_shape=outs,
        in_specs=[hbm if i in hbm_in else VMEM for i in range(len(operands))],
        out_specs=[hbm if i in hbm_out else VMEM for i in range(len(outs))],
        scratch_shapes=list(scratch),
        compiler_params=pltpu.CompilerParams(vmem_limit_bytes=24 * 1024 * 1024),
        cost_estimate=pl.CostEstimate(flops=cost * 2**30, bytes_accessed=2**16, transcendentals=0),
        name=name,
    )(*operands)


def hand_out_halves(total, keep, send, me):
    piece = keep.shape[1]
    for k in range(total.shape[0] // piece):
        out = send if k % 2 else keep
        out[k // 2] = total[pl.ds((me ^ k) * piece, piece)].astype(out.dtype)


def swap(x, axis, k):
    n = lax.axis_size(axis)
    return lax.ppermute(x, axis, [(d, d ^ k) for d in range(n)])


def swap_all(pieces, axis):
    return [pieces[0]] + [swap(pieces[k], axis, k) for k in range(1, len(pieces))]


def bits_of(n):
    return [1 << s for s in range(n.bit_length() - 1)]


def gather_halves(own, axis):
    n = lax.axis_size(axis)
    parts = {0: own}
    for bit in reversed(bits_of(n)):
        for k in sorted(parts):
            parts[k ^ bit] = swap(parts[k], axis, bit)
    return [parts[k] for k in range(n)]


def after(x, *earlier):
    return lax.optimization_barrier((x, earlier))[0]


def tree_sum(parts):
    parts = [part.astype(F32) for part in parts]
    while len(parts) > 1:
        parts = [parts[i] + parts[i + 1] for i in range(0, len(parts), 2)]
    return parts[0]


def on_device(left_factors, right_factors, out_weight, out_bias, pair_grad):
    n_row = lax.axis_size("row")
    n_col = lax.axis_size("col")
    left, right = left_factors[0], right_factors[0]
    left_piece, chan, samples = left.shape
    right_piece = right.shape[0]
    rows, cols, width = pair_grad.shape
    pairs = chan * chan
    row4, chan4 = rows // 4, chan // 4
    half4 = row4 // 2
    near, half = n_col // 2, n_row // 2
    inv_samples = 1.0 / samples
    wide = 2 * LANES
    weight_piece = pairs // n_row
    struct = jax.ShapeDtypeStruct
    weight3 = out_weight.reshape(chan, chan, width)
    grad4 = pair_grad.reshape(row4, 4, cols, width)

    left_parts = gather_halves(left, "col")
    right_parts = gather_halves(right, "row")

    def stage_kernel(grad_hbm, weight_hbm, left_hbm, right_hbm, grad, weight_e, left, right, *scr):
        weight, sems = scr
        copies = [
            pltpu.make_async_copy(source, target, sems.at[i])
            for i, (source, target) in enumerate(
                [(weight_hbm, weight), (left_hbm, left), (right_hbm, right), (grad_hbm, grad)]
            )
        ]
        for copy in copies:
            copy.start()
        copies[0].wait()
        weight_e[...] = swap01(weight[...]).reshape(pairs, width)
        for copy in copies[1:]:
            copy.wait()

    grad_vmem, weight_e, left_parts[0], right_parts[0] = call(
        stage_kernel,
        [
            struct(grad4.shape, BF),
            struct((pairs, width), BF),
            struct(left.shape, BF),
            struct(right.shape, BF),
        ],
        [pltpu.VMEM(weight3.shape, BF), pltpu.SemaphoreType.DMA((4,))],
        "stage",
        *[pltpu.with_memory_space_constraint(x, pltpu.HBM) for x in (grad4, weight3, left, right)],
        hbm_in=(0, 1, 2, 3),
    )

    def outer_mean(a_whole, be, grad_ref, y_ref, tmp, group, masks):
        am = a_whole[...].reshape(rows * chan // 2, samples)
        for blk in range(rows * chan // 2 // wide):
            for a in range(4):
                tmp[blk, a] = dot_nt(
                    be[:, a].reshape(chan4 * cols, samples),
                    xor_groups(am, a, chan)[blk * wide : (blk + 1) * wide],
                ).astype(BF)
            for e in range(chan4):
                for h in range(2):
                    ys = trade(
                        [
                            tmp[blk, a, e * cols : (e + 1) * cols, h * LANES : (h + 1) * LANES]
                            for a in range(4)
                        ],
                        masks,
                    )
                    for b in range(4):
                        y_ref[2 * blk + h, b, :, e * LANES : (e + 1) * LANES] = ys[b]
        acc = None
        for b in range(4):
            d = dot_tn(
                y_ref[:, b].reshape(half4 * cols, pairs),
                grad_ref[pl.ds(group * half4, half4), b].reshape(half4 * cols, width),
            )
            d = xor_groups(d, b, chan)
            acc = d if acc is None else acc + d
        return acc

    mean_scratch = [
        pltpu.VMEM((rows // 2, chan, samples), BF),
        pltpu.VMEM((rows * chan // 2 // wide, 4, chan4 * cols, wide), BF),
    ]

    def near_kernel(grad_ref, *refs):
        a_refs, b_refs = refs[:near], refs[near : near + n_row]
        y_ref, weight_ref, be_ref, a_whole, tmp, b_whole = refs[near + n_row :]
        me = lax.axis_index("col")
        assemble(a_whole, a_refs, 0, me)
        assemble(b_whole, b_refs, 0, lax.axis_index("row"))
        be = swap01(b_whole[...]).reshape(chan4, 4, cols, samples)
        be_ref[...] = be
        weight_ref[...] = outer_mean(
            a_whole, be, grad_ref, y_ref, tmp, me // near, lane_masks(cols, chan)
        )

    y_struct = struct((half4, 4, cols, pairs), BF)
    y_near, weight_near, right_e = call(
        near_kernel,
        [y_struct, struct((pairs, width), F32), struct((chan4, 4, cols, samples), BF)],
        mean_scratch + [pltpu.VMEM((cols, chan, samples), BF)],
        "outer_mean_near",
        grad_vmem,
        *left_parts[:near],
        *right_parts,
    )

    def far_kernel(grad_ref, be_ref, near_ref, *refs):
        a_refs, y_ref = refs[:near], refs[near]
        keep, send, a_whole, tmp, total = refs[near + 1 :]
        me = lax.axis_index("col")
        assemble(a_whole, a_refs, near, me)
        acc = outer_mean(
            a_whole, be_ref, grad_ref, y_ref, tmp, 1 - me // near, lane_masks(cols, chan)
        )
        acc = (acc + near_ref[...]) * (inv_samples / (rows * n_row))
        total[...] = jnp.swapaxes(acc.reshape(chan, chan, width), 0, 1).reshape(pairs, width)
        hand_out_halves(total, keep, send, lax.axis_index("row"))

    y_far, weight_keep, weight_send = call(
        far_kernel,
        [y_struct] + [struct((half, weight_piece, width), dtype) for dtype in (F32, BF)],
        mean_scratch + [pltpu.VMEM((pairs, width), F32)],
        "outer_mean_far",
        grad_vmem,
        right_e,
        weight_near,
        *left_parts[near:],
    )
    def outer_grad_kernel(grad_ref, weight_ref, z_ref, tmp):
        w = weight_ref[...]
        masks = lane_masks(cols, chan)
        for blk in range(pairs // wide):
            for b in range(4):
                tmp[blk, b] = dot_nt(
                    grad_ref[:, b].reshape(row4 * cols, width),
                    xor_groups(w, b, chan)[blk * wide : (blk + 1) * wide],
                ).astype(BF)
            for n in range(row4):
                for h in range(2):
                    ys = trade(
                        [
                            tmp[blk, b, n * cols : (n + 1) * cols, h * LANES : (h + 1) * LANES]
                            for b in range(4)
                        ],
                        masks,
                    )
                    for a in range(4):
                        z_ref[2 * blk + h, a, :, n * LANES : (n + 1) * LANES] = ys[a]

    (z,) = call(
        outer_grad_kernel,
        [struct((chan4, 4, cols, rows * chan), BF)],
        [pltpu.VMEM((pairs // wide, 4, row4 * cols, wide), BF)],
        "outer_grad",
        after(grad_vmem, weight_send),
        weight_e,
        cost=4,
    )

    def halve_kernel(keep, got, next_keep, next_send):
        for k in range(keep.shape[0]):
            out = next_send if k % 2 else next_keep
            out[k // 2] = (keep[k] + got[k].astype(F32)).astype(out.dtype)

    def halve(keep, got, name):
        shape = (keep.shape[0] // 2,) + keep.shape[1:]
        return call(
            halve_kernel, [struct(shape, dtype) for dtype in (F32, BF)], [], name, keep, got
        )

    for bit in bits_of(n_row)[:-1]:
        weight_got = after(swap(weight_send, "row", bit), z)
        weight_keep, weight_send = halve(weight_keep, weight_got, "weight_halve_%d" % bit)

    def left_kernel(z_ref, be_ref, keep, send, total):
        acc = None
        for a in range(4):
            d = dot_tn(
                z_ref[:, a].reshape(chan4 * cols, rows * chan),
                be_ref[:, a].reshape(chan4 * cols, samples),
            )
            d = xor_groups(d, a, chan)
            acc = d if acc is None else acc + d
        total[...] = (acc * inv_samples).reshape(rows, chan, samples)
        hand_out_halves(total, keep, send, lax.axis_index("col"))

    left_keep, left_send = call(
        left_kernel,
        [struct((near, left_piece, chan, samples), dtype) for dtype in (F32, BF)],
        [pltpu.VMEM((rows, chan, samples), F32)],
        "left_grad",
        after(z, weight_send),
        right_e,
        cost=3,
    )

    def right_kernel(z_ref, *refs):
        a_refs, (keep, send, whole, total, turned) = refs[:n_col], refs[n_col:]
        assemble(whole, a_refs, 0, lax.axis_index("col"))
        am = whole[...].reshape(rows * chan, samples)
        for a in range(4):
            d = dot_nn(z_ref[:, a].reshape(chan4 * cols, rows * chan), xor_groups(am, a, chan))
            total[:, a] = d.reshape(chan4, cols, samples)
        turned[...] = jnp.swapaxes(total[...].reshape(chan, cols, samples), 0, 1) * inv_samples
        hand_out_halves(turned, keep, send, lax.axis_index("row"))

    right_keep, right_send = call(
        right_kernel,
        [struct((half, right_piece, chan, samples), dtype) for dtype in (F32, BF)],
        [
            pltpu.VMEM((rows, chan, samples), BF),
            pltpu.VMEM((chan4, 4, cols, samples), F32),
            pltpu.VMEM((cols, chan, samples), F32),
        ],
        "right_grad",
        after(z, left_send),
        *left_parts,
        cost=3,
    )

    def last_kernel(keep, got, out):
        out[...] = (keep[0] + got[0].astype(F32)).astype(BF)

    (weight_own,) = call(
        last_kernel,
        [struct((weight_piece, width), BF)],
        [],
        "weight_row_sum",
        weight_keep,
        after(swap(weight_send, "row", half), right_send),
    )
    col_got = swap_all([weight_own] * n_col, "col")

    for bit in bits_of(n_col)[:-1]:
        left_got = after(swap(left_send, "col", bit), weight_own)
        left_keep, left_send = halve(left_keep, left_got, "left_halve_%d" % bit)
    left_got = swap(left_send, "col", near)

    for bit in bits_of(n_row)[:-1]:
        right_got = after(swap(right_send, "row", bit), left_send)
        right_keep, right_send = halve(right_keep, right_got, "right_halve_%d" % bit)
    right_got = swap(right_send, "row", half)


    def pair_kernel(near_ref, far_ref, weight_ref, bias_ref, p_hbm, p_ref, sem):
        me = lax.axis_index("col")
        copies = []
        for part, y_ref in enumerate((near_ref, far_ref)):
            group = part ^ (me // near)
            for b in range(4):
                d = dot_nn(
                    y_ref[:, b].reshape(half4 * cols, pairs), xor_groups(weight_ref[...], b, chan)
                )
                d = d * inv_samples + bias_ref[...]
                p_ref[part, :, b] = d.reshape(half4, cols, width).astype(BF)
            copies.append(
                pltpu.make_async_copy(
                    p_ref.at[part], p_hbm.at[pl.ds(group * half4, half4)], sem.at[part]
                )
            )
            copies[-1].start()
        for copy in copies:
            copy.wait()

    (pair_update,) = call(
        pair_kernel,
        [struct((row4, 4, cols, width), BF)],
        [pltpu.VMEM((2, half4, 4, cols, width), BF), pltpu.SemaphoreType.DMA((2,))],
        "pair_update",
        after(y_near, right_send, left_send),
        y_far,
        weight_e,
        out_bias.reshape(1, width),
        cost=16,
        hbm_out=(0,),
    )


    def col_sum_kernel(*refs):
        refs[-1][...] = tree_sum([ref[...] for ref in refs[:-1]]).astype(BF)

    (weight_sum,) = call(
        col_sum_kernel, [struct((weight_piece, width), BF)], [], "weight_col_sum", *col_got[:-1], after(col_got[-1], pair_update)
    )
    weight_rows = swap_all([weight_sum] * n_row, "row")

    def totals_kernel(l_keep, l_got, r_keep, r_got, l_out, r_out):
        l_out[...] = l_keep[...] + l_got[...].astype(F32)
        r_out[...] = r_keep[...] + r_got[...].astype(F32)

    grad_left, grad_right = call(
        totals_kernel,
        [
            struct((1, left_piece, chan, samples), F32),
            struct((1, right_piece, chan, samples), F32),
        ],
        [],
        "left_right_totals",
        after(left_keep, weight_sum),
        left_got,
        right_keep,
        right_got,
    )

    def place_kernel(*refs):
        me = lax.axis_index("row")
        for k in range(n_row):
            refs[-1][pl.ds((me ^ k) * weight_piece, weight_piece)] = refs[k][...].astype(F32)

    weight_rows[-1] = after(weight_rows[-1], grad_right)
    (grad_weight,) = call(
        place_kernel, [struct((pairs, width), F32)], [], "weight_place", *weight_rows
    )
    return (pair_update.reshape(rows, cols, width), grad_left, grad_right, grad_weight)


def solution(mesh):
    return jax.shard_map(
        on_device,
        mesh=mesh,
        in_specs=(
            P(("grp", "row"), "col", None, None),
            P(("grp", "col"), "row", None, None),
            P(),
            P(),
            P(("grp", "row"), "col", None),
        ),
        out_specs=(
            P(("grp", "row"), "col", None),
            P(("grp", "row"), "col", None, None),
            P(("grp", "col"), "row", None, None),
            P("grp", None),
        ),
        check_vma=False,
    )
```

time: 348 us -> 42.7 us (0.12)
  waiting for transfers between devices: 172 us -> 6.06 us
  local copies, waits for them, and re-layouts: 88.5 us -> 0.01 us
  matrix products: 46.9 us -> 0 us
  blocking collectives: 23.1 us -> 0 us
  starting transfers between devices: 0.12 us -> 20.9 us
  Pallas kernels: 0 us -> 14.8 us
  between operations: 13.8 us -> 0.79 us
    psum x3 -> x0, waiting for transfers between devices: 170 us -> none  [the longest x1 90.2 us: on_device(): weight_sum = lax.psum(weight_acc, ('row', 'col'))]
    dot_general x18 -> x0, matrix products: 46.9 us -> none  [the longest x3 17.2 us: advance(): jnp.einsum('ijce,ics->jes', outer_grad, left_blk, preferred_element_type=...]
    reshape x6 -> x0, local copies, waits for them, and re-layouts: 44.7 us -> none  [the longest x3 26.3 us: advance(): outer_mean = (outer_mean * inv_samples).astype(jnp.bfloat16).reshape(blk_...]
    convert_element_type x3 -> x0, local copies, waits for them, and re-layouts: 37.4 us -> none  [advance(): outer_mean = (outer_mean * inv_samples).astype(jnp.bfloat16).reshape(blk_...]
    all_gather x2 -> x0, blocking collectives: 23.1 us -> none  [the longest x1 16.4 us: on_device(): gathered_left = lax.all_gather(left_factors, 'col', axis=1, tiled=True)[0]]
    ppermute x0 -> x18, starting transfers between devices: none -> 20.9 us  [swap(): return lax.ppermute(x, axis, [(d, d ^ k) for d in range(n)])]
    pallas_call x0 -> x14, Pallas kernels: none -> 14.8 us  [call(): pl.pallas_call(kernel, out_shape=outs, in_specs=[hbm if i in hbm_in else...]
    ppermute x0 -> x18, waiting for transfers between devices: none -> 6.06 us  [swap(): return lax.ppermute(x, axis, [(d, d ^ k) for d in range(n)])]
  transfers between devices with their start and end apart: 3 -> 18, of which waited for: 3 -> 5; matrix products, arithmetic and copies ran while one was open for 1% -> 0% of each run, Pallas kernels for 0% -> 27%
where the time goes in v3:
time: 42.7 us; the launch traced here: 42.5 us
  starting transfers between devices  20.9 us (49%)
  Pallas kernels  14.8 us (35%)
  waiting for transfers between devices  6.06 us (14%)
  between operations  0.79 us (2%)
    ppermute x18, starting transfers between devices, swap(): return lax.ppermute(x, axis, [(d, d ^ k) for d in range(n)])  20.9 us
    pallas_call x14, Pallas kernels, call(): pl.pallas_call(kernel, out_shape=outs, in_specs=[hbm if i in hbm_in else...  14.8 us
    ppermute x18, waiting for transfers between devices, swap(): return lax.ppermute(x, axis, [(d, d ^ k) for d in range(n)])  6.06 us
  transfers between devices with their start and end apart: 18, of which 5 were waited for; matrix products, arithmetic and copies ran while one was open for 0% of the time, Pallas kernels for 27%

profile of v3, /device:TPU:0, one launch (start us, length us, event | category | flops | bytes accessed | tf_op | source)
XLA Modules:
  0.0 42.5 jit_solution(1828184258585390411)
XLA Ops:
  0.6 3.0 %collective-permute-start.2 = (bf16[12,32,128]{2,1,0:T(8,128)(2,1)}, bf16[12,32,128]{2,1,0:T(8,128)(2,1)S(1)}, u32[]{:S(2)}, u32[]{:S(2)}) collective-permute-start(bf16[12,32,128]{2,1,0:T(8,128)(2,1)} %bitcast.12), channel_id=1, source_target_pairs={{0,8},{4,12},{8,0},{12,4},{1,9},{5,13},{9,1},{13,5},{2,10},{6,14},... | collective-permute-start | bytes 294920 | tf_op jit(solution)/shard_map/ppermute | solution.py:77
  3.6 2.6 %collective-permute-start.4 = (bf16[12,32,128]{2,1,0:T(8,128)(2,1)}, bf16[12,32,128]{2,1,0:T(8,128)(2,1)S(1)}, u32[]{:S(2)}, u32[]{:S(2)}) collective-permute-start(bf16[12,32,128]{2,1,0:T(8,128)(2,1)} %bitcast.9), channel_id=1, source_target_pairs={{0,2},{1,3},{2,0},{3,1},{4,6},{5,7},{6,4},{7,5},{8,10},{9,11},{10,... | collective-permute-start | bytes 294920 | tf_op jit(solution)/shard_map/ppermute | solution.py:77
  6.2 1.6 %collective-permute-start = (bf16[12,32,128]{2,1,0:T(8,128)(2,1)}, bf16[12,32,128]{2,1,0:T(8,128)(2,1)S(1)}, u32[]{:S(2)}, u32[]{:S(2)}) collective-permute-start(bf16[12,32,128]{2,1,0:T(8,128)(2,1)} %bitcast.10), channel_id=1, source_target_pairs={{0,1},{1,0},{2,3},{3,2},{4,5},{5,4},{6,7},{7,6},{8,9},{9,8},{10,11... | collective-permute-start | bytes 294920 | tf_op jit(solution)/shard_map/ppermute | solution.py:77
  7.8 0.5 %collective-permute-start.3 = (bf16[12,32,128]{2,1,0:T(8,128)(2,1)S(1)}, bf16[12,32,128]{2,1,0:T(8,128)(2,1)S(1)}, u32[]{:S(2)}, u32[]{:S(2)}) collective-permute-start(bf16[12,32,128]{2,1,0:T(8,128)(2,1)S(1)} %collective-permute-done.2.refs_4_), channel_id=1, source_target_pairs={{0,4},{4,0},{8,12},{12,8},{1,5},{5,1},{9,13},{13,9},{2,6},{6,2},{1... | collective-permute-start | bytes 294920 | tf_op jit(solution)/shard_map/ppermute | solution.py:77
  8.3 1.3 %stage.1 = (bf16[12,4,48,128]{3,2,1,0:T(8,128)(2,1)S(1)}, bf16[1024,128]{1,0:T(8,128)(2,1)S(1)}, bf16[12,32,128]{2,1,0:T(8,128)(2,1)S(1)}, bf16[12,32,128]{2,1,0:T(8,128)(2,1)S(1)}) custom-call(bf16[12,4,48,128]{3,2,1,0:T(8,128)(2,1)} %bitcast.7, bf16[32,32,128]{2,1,0:T(8,128)(2,1)} %bitcast.8, bf16[12,32,128]{2,1,0:T(8,128)(2,1)} %bitcast.11, ...), custom_call_target="tpu_custom_call" | custom-call | flops 1073741824 | bytes 65536 | tf_op jit(solution)/shard_map/stage/pallas_call | solution.py:56
  9.6 1.5 %collective-permute-done.4.refs_0_.refs_2_ = bf16[12,32,128]{2,1,0:T(8,128)(2,1)S(1)} collective-permute-done((bf16[12,32,128]{2,1,0:T(8,128)(2,1)}, bf16[12,32,128]{2,1,0:T(8,128)(2,1)S(1)}, u32[]{:S(2)}, u32[]{:S(2)}) %collective-permute-start.4) | collective-permute-done | bytes 98336 | tf_op jit(solution)/shard_map/ppermute | solution.py:77
  11.1 0.8 %collective-permute-start.5 = (bf16[12,32,128]{2,1,0:T(8,128)(2,1)S(1)}, bf16[12,32,128]{2,1,0:T(8,128)(2,1)S(1)}, u32[]{:S(2)}, u32[]{:S(2)}) collective-permute-start(bf16[12,32,128]{2,1,0:T(8,128)(2,1)S(1)} %collective-permute-done.4.refs_0_.refs_2_), channel_id=1, source_target_pairs={{0,1},{1,0},{2,3},{3,2},{4,5},{5,4},{6,7},{7,6},{8,9},{9,8},{10,11... | collective-permute-start | bytes 294920 | tf_op jit(solution)/shard_map/ppermute | solution.py:77
  11.9 2.3 %outer_mean_near.1 = (bf16[6,4,48,1024]{3,2,1,0:T(8,128)(2,1)S(1)}, f32[1024,128]{1,0:T(8,128)S(1)}, bf16[8,4,48,128]{3,2,1,0:T(8,128)(2,1)S(1)}) custom-call(bf16[12,4,48,128]{3,2,1,0:T(8,128)(2,1)S(1)} %get-tuple-element.44.grad_ref, bf16[12,32,128]{2,1,0:T(8,128)(2,1)S(1)} %get-tuple-element.38.refs_0_, ...), custom_call_target="tpu_custom_call" | custom-call | flops 1073741824 | bytes 65536 | tf_op jit(solution)/shard_map/outer_mean_near/pallas_call | solution.py:56
  14.2 1.5 %collective-permute-done.5.refs_1_.refs_3_ = bf16[12,32,128]{2,1,0:T(8,128)(2,1)S(1)} collective-permute-done((bf16[12,32,128]{2,1,0:T(8,128)(2,1)S(1)}, bf16[12,32,128]{2,1,0:T(8,128)(2,1)S(1)}, u32[]{:S(2)}, u32[]{:S(2)}) %collective-permute-start.5) | collective-permute-done | bytes 98336 | tf_op jit(solution)/shard_map/ppermute | solution.py:77
  15.7 2.3 %outer_mean_far.1 = (bf16[6,4,48,1024]{3,2,1,0:T(8,128)(2,1)S(1)}, f32[2,256,128]{2,1,0:T(8,128)S(1)}, bf16[2,256,128]{2,1,0:T(8,128)(2,1)S(1)}) custom-call(bf16[12,4,48,128]{3,2,1,0:T(8,128)(2,1)S(1)} %get-tuple-element.44.grad_ref, bf16[8,4,48,128]{3,2,1,0:T(8,128)(2,1)S(1)} %get-tuple-element.41.be_ref, f32[1024,128]{1,0:T(8,128)S(1)} %get-tuple-element.42.near_ref, ...), custom_call_target="tpu_custom_call" | custom-call | flops 1073741824 | bytes 65536 | tf_op jit(solution)/shard_map/outer_mean_far/pallas_call | solution.py:56
  18.1 2.0 %outer_grad.1.z_ref = bf16[8,4,48,1536]{3,2,1,0:T(8,128)(2,1)S(1)} custom-call(bf16[12,4,48,128]{3,2,1,0:T(8,128)(2,1)S(1)} %get-tuple-element.44.grad_ref, bf16[1024,128]{1,0:T(8,128)(2,1)S(1)} %get-tuple-element.45.weight_ref), custom_call_target="tpu_custom_call" | custom-call | flops 4294967296 | bytes 65536 | tf_op jit(solution)/shard_map/outer_grad/pallas_call | solution.py:56
  20.3 1.5 %left_grad.1 = (f32[2,12,32,128]{3,2,1,0:T(8,128)S(1)}, bf16[2,12,32,128]{3,2,1,0:T(8,128)(2,1)S(1)}) custom-call(bf16[8,4,48,1536]{3,2,1,0:T(8,128)(2,1)S(1)} %outer_grad.1.z_ref, bf16[8,4,48,128]{3,2,1,0:T(8,128)(2,1)S(1)} %get-tuple-element.41.be_ref), custom_call_target="tpu_custom_call" | custom-call | flops 3221225472 | bytes 65536 | tf_op jit(solution)/shard_map/left_grad/pallas_call | solution.py:56
  21.8 1.3 %collective-permute-start.8 = (bf16[2,12,32,128]{3,2,1,0:T(8,128)(2,1)S(1)}, bf16[2,12,32,128]{3,2,1,0:T(8,128)(2,1)S(1)}, u32[]{:S(2)}, u32[]{:S(2)}) collective-permute-start(bf16[2,12,32,128]{3,2,1,0:T(8,128)(2,1)S(1)} %get-tuple-element.50), channel_id=1, source_target_pairs={{0,1},{1,0},{2,3},{3,2},{4,5},{5,4},{6,7},{7,6},{8,9},{9,8},{10,11... | collective-permute-start | bytes 589832 | tf_op jit(solution)/shard_map/ppermute | solution.py:77
  23.1 1.5 %right_grad.1 = (f32[2,12,32,128]{3,2,1,0:T(8,128)S(1)}, bf16[2,12,32,128]{3,2,1,0:T(8,128)(2,1)S(1)}) custom-call(bf16[8,4,48,1536]{3,2,1,0:T(8,128)(2,1)S(1)} %outer_grad.1.z_ref, bf16[12,32,128]{2,1,0:T(8,128)(2,1)S(1)} %get-tuple-element.38.refs_0_, bf16[12,32,128]{2,1,0:T(8,128)(2,1)S(1)} %collective-permute-done.refs_1_, ...), custom_call_target="tpu_custom_call" | custom-call | flops 3221225472 | bytes 65536 | tf_op jit(solution)/shard_map/right_grad/pallas_call | solution.py:56
  24.8 3.5 %collective-permute-start.12 = (bf16[256,128]{1,0:T(8,128)(2,1)S(1)}, bf16[256,128]{1,0:T(8,128)(2,1)S(1)}, u32[]{:S(2)}, u32[]{:S(2)}) collective-permute-start(bf16[256,128]{1,0:T(8,128)(2,1)S(1)} %weight_row_sum.1.refs_0_), channel_id=1, source_target_pairs={{0,3},{1,2},{2,1},{3,0},{4,7},{5,6},{6,5},{7,4},{8,11},{9,10},{10,... | collective-permute-start | bytes 196616 | tf_op jit(solution)/shard_map/ppermute | solution.py:77
  28.3 0.9 %collective-permute-start.10 = (bf16[256,128]{1,0:T(8,128)(2,1)S(1)}, bf16[256,128]{1,0:T(8,128)(2,1)S(1)}, u32[]{:S(2)}, u32[]{:S(2)}) collective-permute-start(bf16[256,128]{1,0:T(8,128)(2,1)S(1)} %weight_row_sum.1.refs_0_), channel_id=1, source_target_pairs={{0,1},{1,0},{2,3},{3,2},{4,5},{5,4},{6,7},{7,6},{8,9},{9,8},{10,11... | collective-permute-start | bytes 196616 | tf_op jit(solution)/shard_map/ppermute | solution.py:77
  29.3 2.9 %collective-permute-start.13 = (bf16[1,12,32,128]{3,2,1,0:T(8,128)(2,1)S(1)}, bf16[1,12,32,128]{3,2,1,0:T(8,128)(2,1)S(1)}, u32[]{:S(2)}, u32[]{:S(2)}) collective-permute-start(bf16[1,12,32,128]{3,2,1,0:T(8,128)(2,1)S(1)} %get-tuple-element.58), channel_id=1, source_target_pairs={{0,2},{1,3},{2,0},{3,1},{4,6},{5,7},{6,4},{7,5},{8,10},{9,11},{10,... | collective-permute-start | bytes 294920 | tf_op jit(solution)/shard_map/ppermute | solution.py:77
  32.2 1.6 %collective-permute-start.14 = (bf16[1,12,32,128]{3,2,1,0:T(8,128)(2,1)S(1)}, bf16[1,12,32,128]{3,2,1,0:T(8,128)(2,1)S(1)}, u32[]{:S(2)}, u32[]{:S(2)}) collective-permute-start(bf16[1,12,32,128]{3,2,1,0:T(8,128)(2,1)S(1)} %get-tuple-element.60), channel_id=1, source_target_pairs={{0,8},{4,12},{8,0},{12,4},{1,9},{5,13},{9,1},{13,5},{2,10},{6,14},... | collective-permute-start | bytes 294920 | tf_op jit(solution)/shard_map/ppermute | solution.py:77
  33.8 2.1 %pair_update.1 = bf16[12,4,48,128]{3,2,1,0:T(8,128)(2,1)} custom-call(bf16[6,4,48,1024]{3,2,1,0:T(8,128)(2,1)S(1)} %get-tuple-element.61.near_ref, bf16[6,4,48,1024]{3,2,1,0:T(8,128)(2,1)S(1)} %get-tuple-element.62.far_ref, bf16[1024,128]{1,0:T(8,128)(2,1)S(1)} %get-tuple-element.45.weight_ref, f32[1,128]{1,0:T(1,128)S(1)} %bitcast.6), custom_call_target="tpu_custom_call" | custom-call | flops 17179869184 | bytes 65536 | tf_op jit(solution)/shard_map/pair_update/pallas_call | solution.py:56
  36.3 1.2 %collective-permute-start.16 = (bf16[256,128]{1,0:T(8,128)(2,1)S(1)}, bf16[256,128]{1,0:T(8,128)(2,1)S(1)}, u32[]{:S(2)}, u32[]{:S(2)}) collective-permute-start(bf16[256,128]{1,0:T(8,128)(2,1)S(1)} %weight_col_sum.1.refs_0_), channel_id=1, source_target_pairs={{0,8},{4,12},{8,0},{12,4},{1,9},{5,13},{9,1},{13,5},{2,10},{6,14},... | collective-permute-start | bytes 196616 | tf_op jit(solution)/shard_map/ppermute | solution.py:77
  37.9 1.5 %collective-permute-done.13.l_got = bf16[1,12,32,128]{3,2,1,0:T(8,128)(2,1)S(1)} collective-permute-done((bf16[1,12,32,128]{3,2,1,0:T(8,128)(2,1)S(1)}, bf16[1,12,32,128]{3,2,1,0:T(8,128)(2,1)S(1)}, u32[]{:S(2)}, u32[]{:S(2)}) %collective-permute-start.13) | collective-permute-done | bytes 98336 | tf_op jit(solution)/shard_map/ppermute | solution.py:77
  39.5 0.8 %left_right_totals.1 = (f32[1,12,32,128]{3,2,1,0:T(8,128)}, f32[1,12,32,128]{3,2,1,0:T(8,128)}) custom-call(f32[1,12,32,128]{3,2,1,0:T(8,128)S(1)} %get-tuple-element.65.l_keep, bf16[1,12,32,128]{3,2,1,0:T(8,128)(2,1)S(1)} %collective-permute-done.13.l_got, f32[1,12,32,128]{3,2,1,0:T(8,128)S(1)} %get-tuple-element.66.r_keep, ...), custom_call_target="tpu_custom_call" | custom-call | flops 1073741824 | bytes 65536 | tf_op jit(solution)/shard_map/left_right_totals/pallas_call | solution.py:56
  40.4 1.2 %collective-permute-done.16.refs_2_ = bf16[256,128]{1,0:T(8,128)(2,1)S(1)} collective-permute-done((bf16[256,128]{1,0:T(8,128)(2,1)S(1)}, bf16[256,128]{1,0:T(8,128)(2,1)S(1)}, u32[]{:S(2)}, u32[]{:S(2)}) %collective-permute-start.16) | collective-permute-done | bytes 65568 | tf_op jit(solution)/shard_map/ppermute | solution.py:77
  41.7 0.8 %weight_place.1 = f32[1024,128]{1,0:T(8,128)} custom-call(bf16[256,128]{1,0:T(8,128)(2,1)S(1)} %weight_col_sum.1.refs_0_, bf16[256,128]{1,0:T(8,128)(2,1)S(1)} %collective-permute-done.15.refs_1_, bf16[256,128]{1,0:T(8,128)(2,1)S(1)} %collective-permute-done.16.refs_2_, bf16[256,128]{1,0:T(8,128)(2,1)S(1)} %collective-permute-done.17.refs_3_), custom_call_target="tpu_custom_call" | custom-call | flops 1073741824 | bytes 65536 | tf_op jit(solution)/shard_map/weight_place/pallas_call | solution.py:56
  (28 shorter events, 1.5 us)
Async XLA Ops:
  0.6 7.2 %collective-permute-start.2 = (bf16[12,32,128]{2,1,0:T(8,128)(2,1)}, bf16[12,32,128]{2,1,0:T(8,128)(2,1)S(1)}, u32[]{:S(2)}, u32[]{:S(2)}) collective-permute-start(bf16[12,32,128]{2,1,0:T(8,128)(2,1)} %bitcast.12), channel_id=1, source_target_pairs={{0,8},{4,12},{8,0},{12,4},{1,9},{5,13},{9,1},{13,5},{2,10},{6,14},... | collective-permute-start | bytes 294920 | tf_op jit(solution)/shard_map/ppermute | solution.py:77
  3.6 7.5 %collective-permute-start.4 = (bf16[12,32,128]{2,1,0:T(8,128)(2,1)}, bf16[12,32,128]{2,1,0:T(8,128)(2,1)S(1)}, u32[]{:S(2)}, u32[]{:S(2)}) collective-permute-start(bf16[12,32,128]{2,1,0:T(8,128)(2,1)} %bitcast.9), channel_id=1, source_target_pairs={{0,2},{1,3},{2,0},{3,1},{4,6},{5,7},{6,4},{7,5},{8,10},{9,11},{10,... | collective-permute-start | bytes 294920 | tf_op jit(solution)/shard_map/ppermute | solution.py:77
  6.2 5.7 %collective-permute-start = (bf16[12,32,128]{2,1,0:T(8,128)(2,1)}, bf16[12,32,128]{2,1,0:T(8,128)(2,1)S(1)}, u32[]{:S(2)}, u32[]{:S(2)}) collective-permute-start(bf16[12,32,128]{2,1,0:T(8,128)(2,1)} %bitcast.10), channel_id=1, source_target_pairs={{0,1},{1,0},{2,3},{3,2},{4,5},{5,4},{6,7},{7,6},{8,9},{9,8},{10,11... | collective-permute-start | bytes 294920 | tf_op jit(solution)/shard_map/ppermute | solution.py:77
  7.8 4.1 %collective-permute-start.1 = (bf16[12,32,128]{2,1,0:T(8,128)(2,1)}, bf16[12,32,128]{2,1,0:T(8,128)(2,1)S(1)}, u32[]{:S(2)}, u32[]{:S(2)}) collective-permute-start(bf16[12,32,128]{2,1,0:T(8,128)(2,1)} %bitcast.13), channel_id=1, source_target_pairs={{0,4},{4,0},{8,12},{12,8},{1,5},{5,1},{9,13},{13,9},{2,6},{6,2},{1... | collective-permute-start | bytes 294920 | tf_op jit(solution)/shard_map/ppermute | solution.py:77
  7.8 4.1 %collective-permute-start.3 = (bf16[12,32,128]{2,1,0:T(8,128)(2,1)S(1)}, bf16[12,32,128]{2,1,0:T(8,128)(2,1)S(1)}, u32[]{:S(2)}, u32[]{:S(2)}) collective-permute-start(bf16[12,32,128]{2,1,0:T(8,128)(2,1)S(1)} %collective-permute-done.2.refs_4_), channel_id=1, source_target_pairs={{0,4},{4,0},{8,12},{12,8},{1,5},{5,1},{9,13},{13,9},{2,6},{6,2},{1... | collective-permute-start | bytes 294920 | tf_op jit(solution)/shard_map/ppermute | solution.py:77
  11.1 4.6 %collective-permute-start.5 = (bf16[12,32,128]{2,1,0:T(8,128)(2,1)S(1)}, bf16[12,32,128]{2,1,0:T(8,128)(2,1)S(1)}, u32[]{:S(2)}, u32[]{:S(2)}) collective-permute-start(bf16[12,32,128]{2,1,0:T(8,128)(2,1)S(1)} %collective-permute-done.4.refs_0_.refs_2_), channel_id=1, source_target_pairs={{0,1},{1,0},{2,3},{3,2},{4,5},{5,4},{6,7},{7,6},{8,9},{9,8},{10,11... | collective-permute-start | bytes 294920 | tf_op jit(solution)/shard_map/ppermute | solution.py:77
  18.0 2.1 %collective-permute-start.6 = (bf16[2,256,128]{2,1,0:T(8,128)(2,1)S(1)}, bf16[2,256,128]{2,1,0:T(8,128)(2,1)S(1)}, u32[]{:S(2)}, u32[]{:S(2)}) collective-permute-start(bf16[2,256,128]{2,1,0:T(8,128)(2,1)S(1)} %get-tuple-element.43), channel_id=1, source_target_pairs={{0,4},{4,0},{8,12},{12,8},{1,5},{5,1},{9,13},{13,9},{2,6},{6,2},{1... | collective-permute-start | bytes 393224 | tf_op jit(solution)/shard_map/ppermute | solution.py:77
  20.1 4.6 %collective-permute-start.9 = (bf16[1,256,128]{2,1,0:T(8,128)(2,1)S(1)}, bf16[1,256,128]{2,1,0:T(8,128)(2,1)S(1)}, u32[]{:S(2)}, u32[]{:S(2)}) collective-permute-start(bf16[1,256,128]{2,1,0:T(8,128)(2,1)S(1)} %get-tuple-element.48), channel_id=1, source_target_pairs={{0,8},{4,12},{8,0},{12,4},{1,9},{5,13},{9,1},{13,5},{2,10},{6,14},... | collective-permute-start | bytes 196616 | tf_op jit(solution)/shard_map/ppermute | solution.py:77
  21.8 7.4 %collective-permute-start.8 = (bf16[2,12,32,128]{3,2,1,0:T(8,128)(2,1)S(1)}, bf16[2,12,32,128]{3,2,1,0:T(8,128)(2,1)S(1)}, u32[]{:S(2)}, u32[]{:S(2)}) collective-permute-start(bf16[2,12,32,128]{3,2,1,0:T(8,128)(2,1)S(1)} %get-tuple-element.50), channel_id=1, source_target_pairs={{0,1},{1,0},{2,3},{3,2},{4,5},{5,4},{6,7},{7,6},{8,9},{9,8},{10,11... | collective-permute-start | bytes 589832 | tf_op jit(solution)/shard_map/ppermute | solution.py:77
  24.6 7.5 %collective-permute-start.7 = (bf16[2,12,32,128]{3,2,1,0:T(8,128)(2,1)S(1)}, bf16[2,12,32,128]{3,2,1,0:T(8,128)(2,1)S(1)}, u32[]{:S(2)}, u32[]{:S(2)}) collective-permute-start(bf16[2,12,32,128]{3,2,1,0:T(8,128)(2,1)S(1)} %get-tuple-element.53), channel_id=1, source_target_pairs={{0,4},{4,0},{8,12},{12,8},{1,5},{5,1},{9,13},{13,9},{2,6},{6,2},{1... | collective-permute-start | bytes 589832 | tf_op jit(solution)/shard_map/ppermute | solution.py:77
  24.8 11.2 %collective-permute-start.12 = (bf16[256,128]{1,0:T(8,128)(2,1)S(1)}, bf16[256,128]{1,0:T(8,128)(2,1)S(1)}, u32[]{:S(2)}, u32[]{:S(2)}) collective-permute-start(bf16[256,128]{1,0:T(8,128)(2,1)S(1)} %weight_row_sum.1.refs_0_), channel_id=1, source_target_pairs={{0,3},{1,2},{2,1},{3,0},{4,7},{5,6},{6,5},{7,4},{8,11},{9,10},{10,... | collective-permute-start | bytes 196616 | tf_op jit(solution)/shard_map/ppermute | solution.py:77
  28.3 7.7 %collective-permute-start.11 = (bf16[256,128]{1,0:T(8,128)(2,1)S(1)}, bf16[256,128]{1,0:T(8,128)(2,1)S(1)}, u32[]{:S(2)}, u32[]{:S(2)}) collective-permute-start(bf16[256,128]{1,0:T(8,128)(2,1)S(1)} %weight_row_sum.1.refs_0_), channel_id=1, source_target_pairs={{0,2},{1,3},{2,0},{3,1},{4,6},{5,7},{6,4},{7,5},{8,10},{9,11},{10,... | collective-permute-start | bytes 196616 | tf_op jit(solution)/shard_map/ppermute | solution.py:77
  28.3 7.7 %collective-permute-start.10 = (bf16[256,128]{1,0:T(8,128)(2,1)S(1)}, bf16[256,128]{1,0:T(8,128)(2,1)S(1)}, u32[]{:S(2)}, u32[]{:S(2)}) collective-permute-start(bf16[256,128]{1,0:T(8,128)(2,1)S(1)} %weight_row_sum.1.refs_0_), channel_id=1, source_target_pairs={{0,1},{1,0},{2,3},{3,2},{4,5},{5,4},{6,7},{7,6},{8,9},{9,8},{10,11... | collective-permute-start | bytes 196616 | tf_op jit(solution)/shard_map/ppermute | solution.py:77
  29.3 4.5 %copy-start = (f32[128]{0:T(128)S(1)}, f32[128]{0:T(128)}, u32[]{:S(2)}) copy-start(f32[128]{0:T(128)} %param.8) | copy-start | bytes 1540
  29.3 10.2 %collective-permute-start.13 = (bf16[1,12,32,128]{3,2,1,0:T(8,128)(2,1)S(1)}, bf16[1,12,32,128]{3,2,1,0:T(8,128)(2,1)S(1)}, u32[]{:S(2)}, u32[]{:S(2)}) collective-permute-start(bf16[1,12,32,128]{3,2,1,0:T(8,128)(2,1)S(1)} %get-tuple-element.58), channel_id=1, source_target_pairs={{0,2},{1,3},{2,0},{3,1},{4,6},{5,7},{6,4},{7,5},{8,10},{9,11},{10,... | collective-permute-start | bytes 294920 | tf_op jit(solution)/shard_map/ppermute | solution.py:77
  32.2 5.7 %collective-permute-start.14 = (bf16[1,12,32,128]{3,2,1,0:T(8,128)(2,1)S(1)}, bf16[1,12,32,128]{3,2,1,0:T(8,128)(2,1)S(1)}, u32[]{:S(2)}, u32[]{:S(2)}) collective-permute-start(bf16[1,12,32,128]{3,2,1,0:T(8,128)(2,1)S(1)} %get-tuple-element.60), channel_id=1, source_target_pairs={{0,8},{4,12},{8,0},{12,4},{1,9},{5,13},{9,1},{13,5},{2,10},{6,14},... | collective-permute-start | bytes 294920 | tf_op jit(solution)/shard_map/ppermute | solution.py:77
  36.0 4.5 %collective-permute-start.17 = (bf16[256,128]{1,0:T(8,128)(2,1)S(1)}, bf16[256,128]{1,0:T(8,128)(2,1)S(1)}, u32[]{:S(2)}, u32[]{:S(2)}) collective-permute-start(bf16[256,128]{1,0:T(8,128)(2,1)S(1)} %weight_col_sum.1.refs_0_), channel_id=1, source_target_pairs={{0,12},{4,8},{8,4},{12,0},{1,13},{5,9},{9,5},{13,1},{2,14},{6,10},... | collective-permute-start | bytes 196616 | tf_op jit(solution)/shard_map/ppermute | solution.py:77
  36.3 5.4 %collective-permute-start.16 = (bf16[256,128]{1,0:T(8,128)(2,1)S(1)}, bf16[256,128]{1,0:T(8,128)(2,1)S(1)}, u32[]{:S(2)}, u32[]{:S(2)}) collective-permute-start(bf16[256,128]{1,0:T(8,128)(2,1)S(1)} %weight_col_sum.1.refs_0_), channel_id=1, source_target_pairs={{0,8},{4,12},{8,0},{12,4},{1,9},{5,13},{9,1},{13,5},{2,10},{6,14},... | collective-permute-start | bytes 196616 | tf_op jit(solution)/shard_map/ppermute | solution.py:77
  37.5 4.2 %collective-permute-start.15 = (bf16[256,128]{1,0:T(8,128)(2,1)S(1)}, bf16[256,128]{1,0:T(8,128)(2,1)S(1)}, u32[]{:S(2)}, u32[]{:S(2)}) collective-permute-start(bf16[256,128]{1,0:T(8,128)(2,1)S(1)} %weight_col_sum.1.refs_0_), channel_id=1, source_target_pairs={{0,4},{4,0},{8,12},{12,8},{1,5},{5,1},{9,13},{13,9},{2,6},{6,2},{1... | collective-permute-start | bytes 196616 | tf_op jit(solution)/shard_map/ppermute | solution.py:77

commit v4 on v3

--- a/solution.py
+++ b/solution.py
@@ -89,6 +89,19 @@
     n = lax.axis_size(axis)
     parts = {0: own}
     for bit in reversed(bits_of(n)):
+        for k in sorted(parts):
+            parts[k ^ bit] = swap(parts[k], axis, bit)
+    return [parts[k] for k in range(n)]
+
+
+def gather_far(own, axis):
+    n = lax.axis_size(axis)
+    return {0: own, n // 2: swap(own, axis, n // 2)}
+
+
+def gather_rest(parts, axis):
+    n = lax.axis_size(axis)
+    for bit in reversed(bits_of(n)[:-1]):
         for k in sorted(parts):
             parts[k ^ bit] = swap(parts[k], axis, bit)
     return [parts[k] for k in range(n)]
@@ -123,8 +136,11 @@
     weight3 = out_weight.reshape(chan, chan, width)
     grad4 = pair_grad.reshape(row4, 4, cols, width)
 
-    left_parts = gather_halves(left, "col")
+    left_parts = gather_far(left, "col")
     right_parts = gather_halves(right, "row")
+
+    def tile(q, m, h):
+        return q[m * cols : (m + 1) * cols, h * LANES : (h + 1) * LANES]
 
     def stage_kernel(grad_hbm, weight_hbm, left_hbm, right_hbm, grad, weight_e, left, right, *scr):
         weight, sems = scr
@@ -141,7 +157,7 @@
         for copy in copies[1:]:
             copy.wait()
 
-    grad_vmem, weight_e, left_parts[0], right_parts[0] = call(
+    grad_vmem, weight_e, left_vmem, right_parts[0] = call(
         stage_kernel,
         [
             struct(grad4.shape, BF),
@@ -155,50 +171,73 @@
         hbm_in=(0, 1, 2, 3),
     )
 
-    def outer_mean(a_whole, be, grad_ref, y_ref, tmp, group, masks):
+    def outer_grad_kernel(grad_ref, weight_ref, z_ref):
+        masks = lane_masks(cols, chan)
+        ws = [xor_groups(weight_ref[...], b, chan) for b in range(4)]
+        for blk in range(pairs // wide):
+            for n in range(0, row4, 4):
+                qs = [
+                    dot_nt(
+                        grad_ref[n : n + 4, b].reshape(4 * cols, width),
+                        ws[b][blk * wide : (blk + 1) * wide],
+                    ).astype(BF)
+                    for b in range(4)
+                ]
+                for m, h in [(m, h) for m in range(4) for h in range(2)]:
+                    ys = trade([tile(q, m, h) for q in qs], masks)
+                    for a in range(4):
+                        z_ref[2 * blk + h, a, :, (n + m) * LANES : (n + m + 1) * LANES] = ys[a]
+
+    (z,) = call(
+        outer_grad_kernel,
+        [struct((chan4, 4, cols, rows * chan), BF)],
+        [],
+        "outer_grad",
+        after(grad_vmem, right_parts[n_row // 2]),
+        weight_e,
+        cost=0,
+    )
+
+    left_parts[near] = after(left_parts[near], z)
+    left_parts = gather_rest(left_parts, "col")
+    left_parts[0] = left_vmem
+
+    def outer_mean(a_whole, be, grad_ref, y_ref, group, masks):
         am = a_whole[...].reshape(rows * chan // 2, samples)
+        ams = [xor_groups(am, a, chan) for a in range(4)]
         for blk in range(rows * chan // 2 // wide):
-            for a in range(4):
-                tmp[blk, a] = dot_nt(
-                    be[:, a].reshape(chan4 * cols, samples),
-                    xor_groups(am, a, chan)[blk * wide : (blk + 1) * wide],
-                ).astype(BF)
-            for e in range(chan4):
-                for h in range(2):
-                    ys = trade(
-                        [
-                            tmp[blk, a, e * cols : (e + 1) * cols, h * LANES : (h + 1) * LANES]
-                            for a in range(4)
-                        ],
-                        masks,
-                    )
+            for e in range(0, chan4, 4):
+                qs = [
+                    dot_nt(
+                        be[e : e + 4, a].reshape(4 * cols, samples),
+                        ams[a][blk * wide : (blk + 1) * wide],
+                    ).astype(BF)
+                    for a in range(4)
+                ]
+                for m, h in [(m, h) for m in range(4) for h in range(2)]:
+                    ys = trade([tile(q, m, h) for q in qs], masks)
                     for b in range(4):
-                        y_ref[2 * blk + h, b, :, e * LANES : (e + 1) * LANES] = ys[b]
+                        y_ref[2 * blk + h, b, :, (e + m) * LANES : (e + m + 1) * LANES] = ys[b]
         acc = None
         for b in range(4):
-            d = dot_tn(
-                y_ref[:, b].reshape(half4 * cols, pairs),
-                grad_ref[pl.ds(group * half4, half4), b].reshape(half4 * cols, width),
-            )
-            d = xor_groups(d, b, chan)
+            g = grad_ref[pl.ds(group * half4, half4), b].reshape(half4 * cols, width)
+            d = dot_nn(jnp.transpose(g), y_ref[:, b].reshape(half4 * cols, pairs))
+            d = xor_groups(jnp.transpose(d), b, chan)
             acc = d if acc is None else acc + d
         return acc
 
-    mean_scratch = [
-        pltpu.VMEM((rows // 2, chan, samples), BF),
-        pltpu.VMEM((rows * chan // 2 // wide, 4, chan4 * cols, wide), BF),
-    ]
+    mean_scratch = [pltpu.VMEM((rows // 2, chan, samples), BF)]
 
     def near_kernel(grad_ref, *refs):
         a_refs, b_refs = refs[:near], refs[near : near + n_row]
-        y_ref, weight_ref, be_ref, a_whole, tmp, b_whole = refs[near + n_row :]
+        y_ref, weight_ref, be_ref, a_whole, b_whole = refs[near + n_row :]
         me = lax.axis_index("col")
         assemble(a_whole, a_refs, 0, me)
         assemble(b_whole, b_refs, 0, lax.axis_index("row"))
         be = swap01(b_whole[...]).reshape(chan4, 4, cols, samples)
         be_ref[...] = be
         weight_ref[...] = outer_mean(
-            a_whole, be, grad_ref, y_ref, tmp, me // near, lane_masks(cols, chan)
+            a_whole, be, grad_ref, y_ref, me // near, lane_masks(cols, chan)
         )
 
     y_struct = struct((half4, 4, cols, pairs), BF)
@@ -214,11 +253,11 @@
 
     def far_kernel(grad_ref, be_ref, near_ref, *refs):
         a_refs, y_ref = refs[:near], refs[near]
-        keep, send, a_whole, tmp, total = refs[near + 1 :]
+        keep, send, a_whole, total = refs[near + 1 :]
         me = lax.axis_index("col")
         assemble(a_whole, a_refs, near, me)
         acc = outer_mean(
-            a_whole, be_ref, grad_ref, y_ref, tmp, 1 - me // near, lane_masks(cols, chan)
+            a_whole, be_ref, grad_ref, y_ref, 1 - me // near, lane_masks(cols, chan)
         )
         acc = (acc + near_ref[...]) * (inv_samples / (rows * n_row))
         total[...] = jnp.swapaxes(acc.reshape(chan, chan, width), 0, 1).reshape(pairs, width)
@@ -226,7 +265,7 @@
 
     y_far, weight_keep, weight_send = call(
         far_kernel,
-        [y_struct] + [struct((half, weight_piece, width), dtype) for dtype in (F32, BF)],
+        [y_struct] + [struct((half, weight_piece, width), F32)] * 2,
         mean_scratch + [pltpu.VMEM((pairs, width), F32)],
         "outer_mean_far",
         grad_vmem,
@@ -234,37 +273,6 @@
         weight_near,
         *left_parts[near:],
     )
-    def outer_grad_kernel(grad_ref, weight_ref, z_ref, tmp):
-        w = weight_ref[...]
-        masks = lane_masks(cols, chan)
-        for blk in range(pairs // wide):
-            for b in range(4):
-                tmp[blk, b] = dot_nt(
-                    grad_ref[:, b].reshape(row4 * cols, width),
-                    xor_groups(w, b, chan)[blk * wide : (blk + 1) * wide],
-                ).astype(BF)
-            for n in range(row4):
-                for h in range(2):
-                    ys = trade(
-                        [
-                            tmp[blk, b, n * cols : (n + 1) * cols, h * LANES : (h + 1) * LANES]
-                            for b in range(4)
-                        ],
-                        masks,
-                    )
-                    for a in range(4):
-                        z_ref[2 * blk + h, a, :, n * LANES : (n + 1) * LANES] = ys[a]
-
-    (z,) = call(
-        outer_grad_kernel,
-        [struct((chan4, 4, cols, rows * chan), BF)],
-        [pltpu.VMEM((pairs // wide, 4, row4 * cols, wide), BF)],
-        "outer_grad",
-        after(grad_vmem, weight_send),
-        weight_e,
-        cost=4,
-    )
-
     def halve_kernel(keep, got, next_keep, next_send):
         for k in range(keep.shape[0]):
             out = next_send if k % 2 else next_keep
@@ -276,18 +284,12 @@
             halve_kernel, [struct(shape, dtype) for dtype in (F32, BF)], [], name, keep, got
         )
 
-    for bit in bits_of(n_row)[:-1]:
-        weight_got = after(swap(weight_send, "row", bit), z)
-        weight_keep, weight_send = halve(weight_keep, weight_got, "weight_halve_%d" % bit)
-
     def left_kernel(z_ref, be_ref, keep, send, total):
         acc = None
         for a in range(4):
-            d = dot_tn(
-                z_ref[:, a].reshape(chan4 * cols, rows * chan),
-                be_ref[:, a].reshape(chan4 * cols, samples),
-            )
-            d = xor_groups(d, a, chan)
+            b = be_ref[:, a].reshape(chan4 * cols, samples)
+            d = dot_nn(jnp.transpose(b), z_ref[:, a].reshape(chan4 * cols, rows * chan))
+            d = xor_groups(jnp.transpose(d), a, chan)
             acc = d if acc is None else acc + d
         total[...] = (acc * inv_samples).reshape(rows, chan, samples)
         hand_out_halves(total, keep, send, lax.axis_index("col"))
@@ -301,6 +303,11 @@
         right_e,
         cost=3,
     )
+
+    for bit in bits_of(n_row)[:-1]:
+        weight_got = after(swap(weight_send, "row", bit), left_send)
+        weight_keep, weight_send = halve(weight_keep, weight_got, "weight_halve_%d" % bit)
+    left_send = after(left_send, weight_send)
 
     def right_kernel(z_ref, *refs):
         a_refs, (keep, send, whole, total, turned) = refs[:n_col], refs[n_col:]
@@ -321,7 +328,7 @@
             pltpu.VMEM((cols, chan, samples), F32),
         ],
         "right_grad",
-        after(z, left_send),
+        after(z, weight_send),
         *left_parts,
         cost=3,
     )
@@ -337,18 +344,6 @@
         weight_keep,
         after(swap(weight_send, "row", half), right_send),
     )
-    col_got = swap_all([weight_own] * n_col, "col")
-
-    for bit in bits_of(n_col)[:-1]:
-        left_got = after(swap(left_send, "col", bit), weight_own)
-        left_keep, left_send = halve(left_keep, left_got, "left_halve_%d" % bit)
-    left_got = swap(left_send, "col", near)
-
-    for bit in bits_of(n_row)[:-1]:
-        right_got = after(swap(right_send, "row", bit), left_send)
-        right_keep, right_send = halve(right_keep, right_got, "right_halve_%d" % bit)
-    right_got = swap(right_send, "row", half)
-
 
     def pair_kernel(near_ref, far_ref, weight_ref, bias_ref, p_hbm, p_ref, sem):
         me = lax.axis_index("col")
@@ -375,7 +370,7 @@
         [struct((row4, 4, cols, width), BF)],
         [pltpu.VMEM((2, half4, 4, cols, width), BF), pltpu.SemaphoreType.DMA((2,))],
         "pair_update",
-        after(y_near, right_send, left_send),
+        after(y_near, weight_own),
         y_far,
         weight_e,
         out_bias.reshape(1, width),
@@ -384,40 +379,56 @@
     )
 
 
-    def col_sum_kernel(*refs):
-        refs[-1][...] = tree_sum([ref[...] for ref in refs[:-1]]).astype(BF)
-
-    (weight_sum,) = call(
-        col_sum_kernel, [struct((weight_piece, width), BF)], [], "weight_col_sum", *col_got[:-1], after(col_got[-1], pair_update)
-    )
+    for bit in bits_of(n_row)[:-1]:
+        right_got = after(swap(right_send, "row", bit), pair_update)
+        right_keep, right_send = halve(right_keep, right_got, "right_halve_%d" % bit)
+    right_got = swap(right_send, "row", half)
+
+
+    def add_kernel(own, got, out):
+        out[...] = (own[...].astype(F32) + got[...].astype(F32)).astype(BF)
+
+    weight_sum, tied = weight_own, right_send
+    for bit in reversed(bits_of(n_col)):
+        weight_got = after(swap(weight_sum, "col", bit), tied)
+        (weight_sum,) = call(
+            add_kernel,
+            [struct((weight_piece, width), BF)],
+            [],
+            "weight_col_sum_%d" % bit,
+            weight_sum,
+            weight_got,
+        )
+        if tied is right_send:
+            for low in bits_of(n_col)[:-1]:
+                left_got = after(swap(left_send, "col", low), weight_sum)
+                left_keep, left_send = halve(left_keep, left_got, "left_halve_%d" % low)
+            left_got = swap(left_send, "col", near)
+            tied = left_send
     weight_rows = swap_all([weight_sum] * n_row, "row")
 
-    def totals_kernel(l_keep, l_got, r_keep, r_got, l_out, r_out):
+    def totals_kernel(l_keep, l_got, r_keep, r_got, *refs):
+        l_out, r_out, w_out = refs[n_row:]
         l_out[...] = l_keep[...] + l_got[...].astype(F32)
         r_out[...] = r_keep[...] + r_got[...].astype(F32)
-
-    grad_left, grad_right = call(
+        me = lax.axis_index("row")
+        for k in range(n_row):
+            w_out[pl.ds((me ^ k) * weight_piece, weight_piece)] = refs[k][...].astype(F32)
+
+    grad_left, grad_right, grad_weight = call(
         totals_kernel,
         [
             struct((1, left_piece, chan, samples), F32),
             struct((1, right_piece, chan, samples), F32),
+            struct((pairs, width), F32),
         ],
         [],
-        "left_right_totals",
-        after(left_keep, weight_sum),
+        "totals",
+        left_keep,
         left_got,
         right_keep,
         right_got,
-    )
-
-    def place_kernel(*refs):
-        me = lax.axis_index("row")
-        for k in range(n_row):
-            refs[-1][pl.ds((me ^ k) * weight_piece, weight_piece)] = refs[k][...].astype(F32)
-
-    weight_rows[-1] = after(weight_rows[-1], grad_right)
-    (grad_weight,) = call(
-        place_kernel, [struct((pairs, width), F32)], [], "weight_place", *weight_rows
+        *weight_rows,
     )
     return (pair_update.reshape(rows, cols, width), grad_left, grad_right, grad_weight)
 

time: 42.7 us -> 41.8 us (0.979)
  Pallas kernels: 14.8 us -> 12.6 us
  waiting for transfers between devices: 6.06 us -> 8.07 us
  starting transfers between devices: 20.9 us -> 20.2 us
    pallas_call x14, Pallas kernels: 14.8 us -> 12.6 us  [call(): pl.pallas_call(kernel, out_shape=outs, in_specs=[hbm if i in hbm_in else...]
    ppermute x18 -> x17, waiting for transfers between devices: 6.06 us -> 8.07 us  [swap(): return lax.ppermute(x, axis, [(d, d ^ k) for d in range(n)])]
    ppermute x18 -> x17, starting transfers between devices: 20.9 us -> 20.2 us  [swap(): return lax.ppermute(x, axis, [(d, d ^ k) for d in range(n)])]
  transfers between devices with their start and end apart: 18 -> 17, of which waited for: 5 -> 8; matrix products, arithmetic and copies ran while one was open for 0% -> 0% of each run, Pallas kernels for 27% -> 23%
where the time goes in v4:
time: 41.8 us; the launch traced here: 41.6 us
  starting transfers between devices  20.2 us (48%)
  Pallas kernels  12.6 us (30%)
  waiting for transfers between devices  8.07 us (19%)
  between operations  0.76 us (2%)
    ppermute x17, starting transfers between devices, swap(): return lax.ppermute(x, axis, [(d, d ^ k) for d in range(n)])  20.2 us
    pallas_call x14, Pallas kernels, call(): pl.pallas_call(kernel, out_shape=outs, in_specs=[hbm if i in hbm_in else...  12.6 us
    ppermute x17, waiting for transfers between devices, swap(): return lax.ppermute(x, axis, [(d, d ^ k) for d in range(n)])  8.07 us
  transfers between devices with their start and end apart: 17, of which 8 were waited for; matrix products, arithmetic and copies ran while one was open for 0% of the time, Pallas kernels for 23%

profile of v4, /device:TPU:0, one launch (start us, length us, event | category | flops | bytes accessed | tf_op | source)
XLA Modules:
  0.0 41.6 jit_solution(10846107035755676239)
XLA Ops:
  0.6 3.0 %collective-permute-start.2 = (bf16[12,32,128]{2,1,0:T(8,128)(2,1)}, bf16[12,32,128]{2,1,0:T(8,128)(2,1)S(1)}, u32[]{:S(2)}, u32[]{:S(2)}) collective-permute-start(bf16[12,32,128]{2,1,0:T(8,128)(2,1)} %bitcast.12), channel_id=1, source_target_pairs={{0,8},{4,12},{8,0},{12,4},{1,9},{5,13},{9,1},{13,5},{2,10},{6,14},... | collective-permute-start | bytes 294920 | tf_op jit(solution)/shard_map/ppermute | solution.py:77
  3.6 2.6 %collective-permute-start.4 = (bf16[12,32,128]{2,1,0:T(8,128)(2,1)}, bf16[12,32,128]{2,1,0:T(8,128)(2,1)S(1)}, u32[]{:S(2)}, u32[]{:S(2)}) collective-permute-start(bf16[12,32,128]{2,1,0:T(8,128)(2,1)} %bitcast.9), channel_id=1, source_target_pairs={{0,2},{1,3},{2,0},{3,1},{4,6},{5,7},{6,4},{7,5},{8,10},{9,11},{10,... | collective-permute-start | bytes 294920 | tf_op jit(solution)/shard_map/ppermute | solution.py:77
  6.2 1.6 %collective-permute-start = (bf16[12,32,128]{2,1,0:T(8,128)(2,1)}, bf16[12,32,128]{2,1,0:T(8,128)(2,1)S(1)}, u32[]{:S(2)}, u32[]{:S(2)}) collective-permute-start(bf16[12,32,128]{2,1,0:T(8,128)(2,1)} %bitcast.10), channel_id=1, source_target_pairs={{0,1},{1,0},{2,3},{3,2},{4,5},{5,4},{6,7},{7,6},{8,9},{9,8},{10,11... | collective-permute-start | bytes 294920 | tf_op jit(solution)/shard_map/ppermute | solution.py:77
  7.8 0.5 %collective-permute-start.3 = (bf16[12,32,128]{2,1,0:T(8,128)(2,1)S(1)}, bf16[12,32,128]{2,1,0:T(8,128)(2,1)S(1)}, u32[]{:S(2)}, u32[]{:S(2)}) collective-permute-start(bf16[12,32,128]{2,1,0:T(8,128)(2,1)S(1)} %collective-permute-done.2.refs_4_), channel_id=1, source_target_pairs={{0,4},{4,0},{8,12},{12,8},{1,5},{5,1},{9,13},{13,9},{2,6},{6,2},{1... | collective-permute-start | bytes 294920 | tf_op jit(solution)/shard_map/ppermute | solution.py:77
  8.3 1.3 %stage.1 = (bf16[12,4,48,128]{3,2,1,0:T(8,128)(2,1)S(1)}, bf16[1024,128]{1,0:T(8,128)(2,1)S(1)}, bf16[12,32,128]{2,1,0:T(8,128)(2,1)S(1)}, bf16[12,32,128]{2,1,0:T(8,128)(2,1)S(1)}) custom-call(bf16[12,4,48,128]{3,2,1,0:T(8,128)(2,1)} %bitcast.7, bf16[32,32,128]{2,1,0:T(8,128)(2,1)} %bitcast.8, bf16[12,32,128]{2,1,0:T(8,128)(2,1)} %bitcast.11, ...), custom_call_target="tpu_custom_call" | custom-call | flops 1073741824 | bytes 65536 | tf_op jit(solution)/shard_map/stage/pallas_call | solution.py:56
  9.6 1.4 %outer_grad.1.z_ref = bf16[8,4,48,1536]{3,2,1,0:T(8,128)(2,1)S(1)} custom-call(bf16[12,4,48,128]{3,2,1,0:T(8,128)(2,1)S(1)} %get-tuple-element.45.grad_ref, bf16[1024,128]{1,0:T(8,128)(2,1)S(1)} %get-tuple-element.46.weight_ref), custom_call_target="tpu_custom_call" | custom-call | bytes 65536 | tf_op jit(solution)/shard_map/outer_grad/pallas_call | solution.py:56
  11.1 0.8 %collective-permute-start.5 = (bf16[12,32,128]{2,1,0:T(8,128)(2,1)S(1)}, bf16[12,32,128]{2,1,0:T(8,128)(2,1)S(1)}, u32[]{:S(2)}, u32[]{:S(2)}) collective-permute-start(bf16[12,32,128]{2,1,0:T(8,128)(2,1)S(1)} %collective-permute-done.4.refs_0_.refs_2_), channel_id=1, source_target_pairs={{0,1},{1,0},{2,3},{3,2},{4,5},{5,4},{6,7},{7,6},{8,9},{9,8},{10,11... | collective-permute-start | bytes 294920 | tf_op jit(solution)/shard_map/ppermute | solution.py:77
  11.9 1.9 %outer_mean_near.1 = (bf16[6,4,48,1024]{3,2,1,0:T(8,128)(2,1)S(1)}, f32[1024,128]{1,0:T(8,128)S(1)}, bf16[8,4,48,128]{3,2,1,0:T(8,128)(2,1)S(1)}) custom-call(bf16[12,4,48,128]{3,2,1,0:T(8,128)(2,1)S(1)} %get-tuple-element.45.grad_ref, bf16[12,32,128]{2,1,0:T(8,128)(2,1)S(1)} %get-tuple-element.40.refs_0_, ...), custom_call_target="tpu_custom_call" | custom-call | flops 1073741824 | bytes 65536 | tf_op jit(solution)/shard_map/outer_mean_near/pallas_call | solution.py:56
  13.8 2.0 %collective-permute-done.5.refs_1_.refs_3_ = bf16[12,32,128]{2,1,0:T(8,128)(2,1)S(1)} collective-permute-done((bf16[12,32,128]{2,1,0:T(8,128)(2,1)S(1)}, bf16[12,32,128]{2,1,0:T(8,128)(2,1)S(1)}, u32[]{:S(2)}, u32[]{:S(2)}) %collective-permute-start.5) | collective-permute-done | bytes 98336 | tf_op jit(solution)/shard_map/ppermute | solution.py:77
  15.8 1.9 %outer_mean_far.1 = (bf16[6,4,48,1024]{3,2,1,0:T(8,128)(2,1)S(1)}, f32[2,256,128]{2,1,0:T(8,128)S(1)}, f32[2,256,128]{2,1,0:T(8,128)S(1)}) custom-call(bf16[12,4,48,128]{3,2,1,0:T(8,128)(2,1)S(1)} %get-tuple-element.45.grad_ref, bf16[8,4,48,128]{3,2,1,0:T(8,128)(2,1)S(1)} %get-tuple-element.43.be_ref, f32[1024,128]{1,0:T(8,128)S(1)} %get-tuple-element.44.near_ref, ...), custom_call_target="tpu_custom_call" | custom-call | flops 1073741824 | bytes 65536 | tf_op jit(solution)/shard_map/outer_mean_far/pallas_call | solution.py:56
  17.8 1.2 %left_grad.1 = (f32[2,12,32,128]{3,2,1,0:T(8,128)S(1)}, bf16[2,12,32,128]{3,2,1,0:T(8,128)(2,1)S(1)}) custom-call(bf16[8,4,48,1536]{3,2,1,0:T(8,128)(2,1)S(1)} %outer_grad.1.z_ref, bf16[8,4,48,128]{3,2,1,0:T(8,128)(2,1)S(1)} %get-tuple-element.43.be_ref), custom_call_target="tpu_custom_call" | custom-call | flops 3221225472 | bytes 65536 | tf_op jit(solution)/shard_map/left_grad/pallas_call | solution.py:56
  19.4 0.7 %collective-permute-start.7 = (bf16[1,256,128]{2,1,0:T(8,128)(2,1)S(1)}, bf16[1,256,128]{2,1,0:T(8,128)(2,1)S(1)}, u32[]{:S(2)}, u32[]{:S(2)}) collective-permute-start(bf16[1,256,128]{2,1,0:T(8,128)(2,1)S(1)} %get-tuple-element.54), channel_id=1, source_target_pairs={{0,8},{4,12},{8,0},{12,4},{1,9},{5,13},{9,1},{13,5},{2,10},{6,14},... | collective-permute-start | bytes 196616 | tf_op jit(solution)/shard_map/ppermute | solution.py:77
  20.1 1.5 %right_grad.1 = (f32[2,12,32,128]{3,2,1,0:T(8,128)S(1)}, bf16[2,12,32,128]{3,2,1,0:T(8,128)(2,1)S(1)}) custom-call(bf16[8,4,48,1536]{3,2,1,0:T(8,128)(2,1)S(1)} %outer_grad.1.z_ref, bf16[12,32,128]{2,1,0:T(8,128)(2,1)S(1)} %get-tuple-element.40.refs_0_, bf16[12,32,128]{2,1,0:T(8,128)(2,1)S(1)} %collective-permute-done.refs_1_, ...), custom_call_target="tpu_custom_call" | custom-call | flops 3221225472 | bytes 65536 | tf_op jit(solution)/shard_map/right_grad/pallas_call | solution.py:56
  21.7 1.7 %collective-permute-start.8 = (bf16[2,12,32,128]{3,2,1,0:T(8,128)(2,1)S(1)}, bf16[2,12,32,128]{3,2,1,0:T(8,128)(2,1)S(1)}, u32[]{:S(2)}, u32[]{:S(2)}) collective-permute-start(bf16[2,12,32,128]{3,2,1,0:T(8,128)(2,1)S(1)} %get-tuple-element.61), channel_id=1, source_target_pairs={{0,1},{1,0},{2,3},{3,2},{4,5},{5,4},{6,7},{7,6},{8,9},{9,8},{10,11... | collective-permute-start | bytes 589832 | tf_op jit(solution)/shard_map/ppermute | solution.py:77
  23.7 2.3 %collective-permute-start.9 = (bf16[256,128]{1,0:T(8,128)(2,1)S(1)}, bf16[256,128]{1,0:T(8,128)(2,1)S(1)}, u32[]{:S(2)}, u32[]{:S(2)}) collective-permute-start(bf16[256,128]{1,0:T(8,128)(2,1)S(1)} %weight_row_sum.1.own), channel_id=1, source_target_pairs={{0,2},{1,3},{2,0},{3,1},{4,6},{5,7},{6,4},{7,5},{8,10},{9,11},{10,... | collective-permute-start | bytes 196616 | tf_op jit(solution)/shard_map/ppermute | solution.py:77
  26.1 2.1 %pair_update.1 = bf16[12,4,48,128]{3,2,1,0:T(8,128)(2,1)} custom-call(bf16[6,4,48,1024]{3,2,1,0:T(8,128)(2,1)S(1)} %get-tuple-element.58.near_ref, bf16[6,4,48,1024]{3,2,1,0:T(8,128)(2,1)S(1)} %get-tuple-element.59.far_ref, bf16[1024,128]{1,0:T(8,128)(2,1)S(1)} %get-tuple-element.46.weight_ref, f32[1,128]{1,0:T(1,128)S(1)} %bitcast.6), custom_call_target="tpu_custom_call" | custom-call | flops 17179869184 | bytes 65536 | tf_op jit(solution)/shard_map/pair_update/pallas_call | solution.py:56
  28.2 1.2 %collective-permute-start.12 = (bf16[1,12,32,128]{3,2,1,0:T(8,128)(2,1)S(1)}, bf16[1,12,32,128]{3,2,1,0:T(8,128)(2,1)S(1)}, u32[]{:S(2)}, u32[]{:S(2)}) collective-permute-start(bf16[1,12,32,128]{3,2,1,0:T(8,128)(2,1)S(1)} %get-tuple-element.64), channel_id=1, source_target_pairs={{0,8},{4,12},{8,0},{12,4},{1,9},{5,13},{9,1},{13,5},{2,10},{6,14},... | collective-permute-start | bytes 294920 | tf_op jit(solution)/shard_map/ppermute | solution.py:77
  29.6 3.6 %collective-permute-start.13 = (bf16[256,128]{1,0:T(8,128)(2,1)S(1)}, bf16[256,128]{1,0:T(8,128)(2,1)S(1)}, u32[]{:S(2)}, u32[]{:S(2)}) collective-permute-start(bf16[256,128]{1,0:T(8,128)(2,1)S(1)} %weight_col_sum_2.1.own), channel_id=1, source_target_pairs={{0,1},{1,0},{2,3},{3,2},{4,5},{5,4},{6,7},{7,6},{8,9},{9,8},{10,11... | collective-permute-start | bytes 196616 | tf_op jit(solution)/shard_map/ppermute | solution.py:77
  33.4 1.9 %collective-permute-done.13.got = bf16[256,128]{1,0:T(8,128)(2,1)S(1)} collective-permute-done((bf16[256,128]{1,0:T(8,128)(2,1)S(1)}, bf16[256,128]{1,0:T(8,128)(2,1)S(1)}, u32[]{:S(2)}, u32[]{:S(2)}) %collective-permute-start.13) | collective-permute-done | bytes 65568 | tf_op jit(solution)/shard_map/ppermute | solution.py:77
  35.5 1.2 %collective-permute-start.15 = (bf16[256,128]{1,0:T(8,128)(2,1)S(1)}, bf16[256,128]{1,0:T(8,128)(2,1)S(1)}, u32[]{:S(2)}, u32[]{:S(2)}) collective-permute-start(bf16[256,128]{1,0:T(8,128)(2,1)S(1)} %weight_col_sum_1.1.refs_0_), channel_id=1, source_target_pairs={{0,8},{4,12},{8,0},{12,4},{1,9},{5,13},{9,1},{13,5},{2,10},{6,14},... | collective-permute-start | bytes 196616 | tf_op jit(solution)/shard_map/ppermute | solution.py:77
  36.7 0.6 %collective-permute-start.14 = (bf16[256,128]{1,0:T(8,128)(2,1)S(1)}, bf16[256,128]{1,0:T(8,128)(2,1)S(1)}, u32[]{:S(2)}, u32[]{:S(2)}) collective-permute-start(bf16[256,128]{1,0:T(8,128)(2,1)S(1)} %weight_col_sum_1.1.refs_0_), channel_id=1, source_target_pairs={{0,4},{4,0},{8,12},{12,8},{1,5},{5,1},{9,13},{13,9},{2,6},{6,2},{1... | collective-permute-start | bytes 196616 | tf_op jit(solution)/shard_map/ppermute | solution.py:77
  37.3 2.8 %collective-permute-done.11.l_got = bf16[1,12,32,128]{3,2,1,0:T(8,128)(2,1)S(1)} collective-permute-done((bf16[1,12,32,128]{3,2,1,0:T(8,128)(2,1)S(1)}, bf16[1,12,32,128]{3,2,1,0:T(8,128)(2,1)S(1)}, u32[]{:S(2)}, u32[]{:S(2)}) %collective-permute-start.11) | collective-permute-done | bytes 98336 | tf_op jit(solution)/shard_map/ppermute | solution.py:77
  40.1 0.5 %collective-permute-done.15.refs_2_ = bf16[256,128]{1,0:T(8,128)(2,1)S(1)} collective-permute-done((bf16[256,128]{1,0:T(8,128)(2,1)S(1)}, bf16[256,128]{1,0:T(8,128)(2,1)S(1)}, u32[]{:S(2)}, u32[]{:S(2)}) %collective-permute-start.15) | collective-permute-done | bytes 65568 | tf_op jit(solution)/shard_map/ppermute | solution.py:77
  40.7 1.0 %totals.1 = (f32[1,12,32,128]{3,2,1,0:T(8,128)}, f32[1,12,32,128]{3,2,1,0:T(8,128)}, f32[1024,128]{1,0:T(8,128)}) custom-call(f32[1,12,32,128]{3,2,1,0:T(8,128)S(1)} %get-tuple-element.67.l_keep, bf16[1,12,32,128]{3,2,1,0:T(8,128)(2,1)S(1)} %collective-permute-done.11.l_got, f32[1,12,32,128]{3,2,1,0:T(8,128)S(1)} %get-tuple-element.69.r_keep, ...), custom_call_target="tpu_custom_call" | custom-call | flops 1073741824 | bytes 65536 | tf_op jit(solution)/shard_map/totals/pallas_call | solution.py:56
  (26 shorter events, 1.4 us)
Async XLA Ops:
  0.6 7.2 %collective-permute-start.2 = (bf16[12,32,128]{2,1,0:T(8,128)(2,1)}, bf16[12,32,128]{2,1,0:T(8,128)(2,1)S(1)}, u32[]{:S(2)}, u32[]{:S(2)}) collective-permute-start(bf16[12,32,128]{2,1,0:T(8,128)(2,1)} %bitcast.12), channel_id=1, source_target_pairs={{0,8},{4,12},{8,0},{12,4},{1,9},{5,13},{9,1},{13,5},{2,10},{6,14},... | collective-permute-start | bytes 294920 | tf_op jit(solution)/shard_map/ppermute | solution.py:77
  3.6 7.5 %collective-permute-start.4 = (bf16[12,32,128]{2,1,0:T(8,128)(2,1)}, bf16[12,32,128]{2,1,0:T(8,128)(2,1)S(1)}, u32[]{:S(2)}, u32[]{:S(2)}) collective-permute-start(bf16[12,32,128]{2,1,0:T(8,128)(2,1)} %bitcast.9), channel_id=1, source_target_pairs={{0,2},{1,3},{2,0},{3,1},{4,6},{5,7},{6,4},{7,5},{8,10},{9,11},{10,... | collective-permute-start | bytes 294920 | tf_op jit(solution)/shard_map/ppermute | solution.py:77
  6.2 5.7 %collective-permute-start = (bf16[12,32,128]{2,1,0:T(8,128)(2,1)}, bf16[12,32,128]{2,1,0:T(8,128)(2,1)S(1)}, u32[]{:S(2)}, u32[]{:S(2)}) collective-permute-start(bf16[12,32,128]{2,1,0:T(8,128)(2,1)} %bitcast.10), channel_id=1, source_target_pairs={{0,1},{1,0},{2,3},{3,2},{4,5},{5,4},{6,7},{7,6},{8,9},{9,8},{10,11... | collective-permute-start | bytes 294920 | tf_op jit(solution)/shard_map/ppermute | solution.py:77
  7.8 4.1 %collective-permute-start.1 = (bf16[12,32,128]{2,1,0:T(8,128)(2,1)}, bf16[12,32,128]{2,1,0:T(8,128)(2,1)S(1)}, u32[]{:S(2)}, u32[]{:S(2)}) collective-permute-start(bf16[12,32,128]{2,1,0:T(8,128)(2,1)} %bitcast.13), channel_id=1, source_target_pairs={{0,4},{4,0},{8,12},{12,8},{1,5},{5,1},{9,13},{13,9},{2,6},{6,2},{1... | collective-permute-start | bytes 294920 | tf_op jit(solution)/shard_map/ppermute | solution.py:77
  7.8 4.1 %collective-permute-start.3 = (bf16[12,32,128]{2,1,0:T(8,128)(2,1)S(1)}, bf16[12,32,128]{2,1,0:T(8,128)(2,1)S(1)}, u32[]{:S(2)}, u32[]{:S(2)}) collective-permute-start(bf16[12,32,128]{2,1,0:T(8,128)(2,1)S(1)} %collective-permute-done.2.refs_4_), channel_id=1, source_target_pairs={{0,4},{4,0},{8,12},{12,8},{1,5},{5,1},{9,13},{13,9},{2,6},{6,2},{1... | collective-permute-start | bytes 294920 | tf_op jit(solution)/shard_map/ppermute | solution.py:77
  11.1 4.7 %collective-permute-start.5 = (bf16[12,32,128]{2,1,0:T(8,128)(2,1)S(1)}, bf16[12,32,128]{2,1,0:T(8,128)(2,1)S(1)}, u32[]{:S(2)}, u32[]{:S(2)}) collective-permute-start(bf16[12,32,128]{2,1,0:T(8,128)(2,1)S(1)} %collective-permute-done.4.refs_0_.refs_2_), channel_id=1, source_target_pairs={{0,1},{1,0},{2,3},{3,2},{4,5},{5,4},{6,7},{7,6},{8,9},{9,8},{10,11... | collective-permute-start | bytes 294920 | tf_op jit(solution)/shard_map/ppermute | solution.py:77
  17.7 1.6 %collective-permute-start.6 = (f32[2,256,128]{2,1,0:T(8,128)S(1)}, f32[2,256,128]{2,1,0:T(8,128)S(1)}, u32[]{:S(2)}, u32[]{:S(2)}) collective-permute-start(f32[2,256,128]{2,1,0:T(8,128)S(1)} %get-tuple-element.49), channel_id=1, source_target_pairs={{0,4},{4,0},{8,12},{12,8},{1,5},{5,1},{9,13},{13,9},{2,6},{6,2},{1... | collective-permute-start | bytes 786440 | tf_op jit(solution)/shard_map/ppermute | solution.py:77
  19.4 4.3 %collective-permute-start.7 = (bf16[1,256,128]{2,1,0:T(8,128)(2,1)S(1)}, bf16[1,256,128]{2,1,0:T(8,128)(2,1)S(1)}, u32[]{:S(2)}, u32[]{:S(2)}) collective-permute-start(bf16[1,256,128]{2,1,0:T(8,128)(2,1)S(1)} %get-tuple-element.54), channel_id=1, source_target_pairs={{0,8},{4,12},{8,0},{12,4},{1,9},{5,13},{9,1},{13,5},{2,10},{6,14},... | collective-permute-start | bytes 196616 | tf_op jit(solution)/shard_map/ppermute | solution.py:77
  21.6 4.4 %copy-start = (f32[128]{0:T(128)S(1)}, f32[128]{0:T(128)}, u32[]{:S(2)}) copy-start(f32[128]{0:T(128)} %param.8) | copy-start | bytes 1540
  21.7 6.5 %collective-permute-start.10 = (bf16[2,12,32,128]{3,2,1,0:T(8,128)(2,1)S(1)}, bf16[2,12,32,128]{3,2,1,0:T(8,128)(2,1)S(1)}, u32[]{:S(2)}, u32[]{:S(2)}) collective-permute-start(bf16[2,12,32,128]{3,2,1,0:T(8,128)(2,1)S(1)} %get-tuple-element.56), channel_id=1, source_target_pairs={{0,4},{4,0},{8,12},{12,8},{1,5},{5,1},{9,13},{13,9},{2,6},{6,2},{1... | collective-permute-start | bytes 589832 | tf_op jit(solution)/shard_map/ppermute | solution.py:77
  21.7 11.4 %collective-permute-start.8 = (bf16[2,12,32,128]{3,2,1,0:T(8,128)(2,1)S(1)}, bf16[2,12,32,128]{3,2,1,0:T(8,128)(2,1)S(1)}, u32[]{:S(2)}, u32[]{:S(2)}) collective-permute-start(bf16[2,12,32,128]{3,2,1,0:T(8,128)(2,1)S(1)} %get-tuple-element.61), channel_id=1, source_target_pairs={{0,1},{1,0},{2,3},{3,2},{4,5},{5,4},{6,7},{7,6},{8,9},{9,8},{10,11... | collective-permute-start | bytes 589832 | tf_op jit(solution)/shard_map/ppermute | solution.py:77
  23.7 5.8 %collective-permute-start.9 = (bf16[256,128]{1,0:T(8,128)(2,1)S(1)}, bf16[256,128]{1,0:T(8,128)(2,1)S(1)}, u32[]{:S(2)}, u32[]{:S(2)}) collective-permute-start(bf16[256,128]{1,0:T(8,128)(2,1)S(1)} %weight_row_sum.1.own), channel_id=1, source_target_pairs={{0,2},{1,3},{2,0},{3,1},{4,6},{5,7},{6,4},{7,5},{8,10},{9,11},{10,... | collective-permute-start | bytes 196616 | tf_op jit(solution)/shard_map/ppermute | solution.py:77
  28.2 9.1 %collective-permute-start.12 = (bf16[1,12,32,128]{3,2,1,0:T(8,128)(2,1)S(1)}, bf16[1,12,32,128]{3,2,1,0:T(8,128)(2,1)S(1)}, u32[]{:S(2)}, u32[]{:S(2)}) collective-permute-start(bf16[1,12,32,128]{3,2,1,0:T(8,128)(2,1)S(1)} %get-tuple-element.64), channel_id=1, source_target_pairs={{0,8},{4,12},{8,0},{12,4},{1,9},{5,13},{9,1},{13,5},{2,10},{6,14},... | collective-permute-start | bytes 294920 | tf_op jit(solution)/shard_map/ppermute | solution.py:77
  29.6 5.8 %collective-permute-start.13 = (bf16[256,128]{1,0:T(8,128)(2,1)S(1)}, bf16[256,128]{1,0:T(8,128)(2,1)S(1)}, u32[]{:S(2)}, u32[]{:S(2)}) collective-permute-start(bf16[256,128]{1,0:T(8,128)(2,1)S(1)} %weight_col_sum_2.1.own), channel_id=1, source_target_pairs={{0,1},{1,0},{2,3},{3,2},{4,5},{5,4},{6,7},{7,6},{8,9},{9,8},{10,11... | collective-permute-start | bytes 196616 | tf_op jit(solution)/shard_map/ppermute | solution.py:77
  33.2 6.9 %collective-permute-start.11 = (bf16[1,12,32,128]{3,2,1,0:T(8,128)(2,1)S(1)}, bf16[1,12,32,128]{3,2,1,0:T(8,128)(2,1)S(1)}, u32[]{:S(2)}, u32[]{:S(2)}) collective-permute-start(bf16[1,12,32,128]{3,2,1,0:T(8,128)(2,1)S(1)} %get-tuple-element.68), channel_id=1, source_target_pairs={{0,2},{1,3},{2,0},{3,1},{4,6},{5,7},{6,4},{7,5},{8,10},{9,11},{10,... | collective-permute-start | bytes 294920 | tf_op jit(solution)/shard_map/ppermute | solution.py:77
  35.4 4.7 %collective-permute-start.16 = (bf16[256,128]{1,0:T(8,128)(2,1)S(1)}, bf16[256,128]{1,0:T(8,128)(2,1)S(1)}, u32[]{:S(2)}, u32[]{:S(2)}) collective-permute-start(bf16[256,128]{1,0:T(8,128)(2,1)S(1)} %weight_col_sum_1.1.refs_0_), channel_id=1, source_target_pairs={{0,12},{4,8},{8,4},{12,0},{1,13},{5,9},{9,5},{13,1},{2,14},{6,10},... | collective-permute-start | bytes 196616 | tf_op jit(solution)/shard_map/ppermute | solution.py:77
  35.5 5.2 %collective-permute-start.15 = (bf16[256,128]{1,0:T(8,128)(2,1)S(1)}, bf16[256,128]{1,0:T(8,128)(2,1)S(1)}, u32[]{:S(2)}, u32[]{:S(2)}) collective-permute-start(bf16[256,128]{1,0:T(8,128)(2,1)S(1)} %weight_col_sum_1.1.refs_0_), channel_id=1, source_target_pairs={{0,8},{4,12},{8,0},{12,4},{1,9},{5,13},{9,1},{13,5},{2,10},{6,14},... | collective-permute-start | bytes 196616 | tf_op jit(solution)/shard_map/ppermute | solution.py:77
  36.7 4.0 %collective-permute-start.14 = (bf16[256,128]{1,0:T(8,128)(2,1)S(1)}, bf16[256,128]{1,0:T(8,128)(2,1)S(1)}, u32[]{:S(2)}, u32[]{:S(2)}) collective-permute-start(bf16[256,128]{1,0:T(8,128)(2,1)S(1)} %weight_col_sum_1.1.refs_0_), channel_id=1, source_target_pairs={{0,4},{4,0},{8,12},{12,8},{1,5},{5,1},{9,13},{13,9},{2,6},{6,2},{1... | collective-permute-start | bytes 196616 | tf_op jit(solution)/shard_map/ppermute | solution.py:77

commit v5 on v4

--- a/solution.py
+++ b/solution.py
@@ -137,7 +137,7 @@
     grad4 = pair_grad.reshape(row4, 4, cols, width)
 
     left_parts = gather_far(left, "col")
-    right_parts = gather_halves(right, "row")
+    right_parts = swap_all([right] * n_row, "row")
 
     def tile(q, m, h):
         return q[m * cols : (m + 1) * cols, h * LANES : (h + 1) * LANES]
@@ -193,7 +193,7 @@
         [struct((chan4, 4, cols, rows * chan), BF)],
         [],
         "outer_grad",
-        after(grad_vmem, right_parts[n_row // 2]),
+        grad_vmem,
         weight_e,
         cost=0,
     )
@@ -307,7 +307,6 @@
     for bit in bits_of(n_row)[:-1]:
         weight_got = after(swap(weight_send, "row", bit), left_send)
         weight_keep, weight_send = halve(weight_keep, weight_got, "weight_halve_%d" % bit)
-    left_send = after(left_send, weight_send)
 
     def right_kernel(z_ref, *refs):
         a_refs, (keep, send, whole, total, turned) = refs[:n_col], refs[n_col:]

time: 41.8 us -> 40.7 us (0.974)
  starting transfers between devices: 20.2 us -> 18.1 us
  waiting for transfers between devices: 8.07 us -> 9.1 us
    ppermute x17, starting transfers between devices: 20.2 us -> 18.1 us  [swap(): return lax.ppermute(x, axis, [(d, d ^ k) for d in range(n)])]
    ppermute x17, waiting for transfers between devices: 8.07 us -> 9.1 us  [swap(): return lax.ppermute(x, axis, [(d, d ^ k) for d in range(n)])]
  transfers between devices with their start and end apart: 17 -> 17, of which waited for: 8 -> 8; matrix products, arithmetic and copies ran while one was open for 0% -> 0% of each run, Pallas kernels for 23% -> 24%
where the time goes in v5:
time: 40.7 us; the launch traced here: 40.5 us
  starting transfers between devices  18.1 us (44%)
  Pallas kernels  12.6 us (31%)
  waiting for transfers between devices  9.1 us (22%)
  between operations  0.77 us (2%)
    ppermute x17, starting transfers between devices, swap(): return lax.ppermute(x, axis, [(d, d ^ k) for d in range(n)])  18.1 us
    pallas_call x14, Pallas kernels, call(): pl.pallas_call(kernel, out_shape=outs, in_specs=[hbm if i in hbm_in else...  12.6 us
    ppermute x17, waiting for transfers between devices, swap(): return lax.ppermute(x, axis, [(d, d ^ k) for d in range(n)])  9.1 us
  transfers between devices with their start and end apart: 17, of which 8 were waited for; matrix products, arithmetic and copies ran while one was open for 0% of the time, Pallas kernels for 24%

profile of v5, /device:TPU:0, one launch (start us, length us, event | category | flops | bytes accessed | tf_op | source)
XLA Modules:
  0.0 40.5 jit_solution(6048594797255642971)
XLA Ops:
  0.6 4.1 %collective-permute-start.4 = (bf16[12,32,128]{2,1,0:T(8,128)(2,1)}, bf16[12,32,128]{2,1,0:T(8,128)(2,1)S(1)}, u32[]{:S(2)}, u32[]{:S(2)}) collective-permute-start(bf16[12,32,128]{2,1,0:T(8,128)(2,1)} %bitcast.9), channel_id=1, source_target_pairs={{0,2},{1,3},{2,0},{3,1},{4,6},{5,7},{6,4},{7,5},{8,10},{9,11},{10,... | collective-permute-start | bytes 294920 | tf_op jit(solution)/shard_map/ppermute | solution.py:77
  4.7 1.6 %collective-permute-start = (bf16[12,32,128]{2,1,0:T(8,128)(2,1)}, bf16[12,32,128]{2,1,0:T(8,128)(2,1)S(1)}, u32[]{:S(2)}, u32[]{:S(2)}) collective-permute-start(bf16[12,32,128]{2,1,0:T(8,128)(2,1)} %bitcast.10), channel_id=1, source_target_pairs={{0,1},{1,0},{2,3},{3,2},{4,5},{5,4},{6,7},{7,6},{8,9},{9,8},{10,11... | collective-permute-start | bytes 294920 | tf_op jit(solution)/shard_map/ppermute | solution.py:77
  6.7 1.2 %collective-permute-start.2 = (bf16[12,32,128]{2,1,0:T(8,128)(2,1)}, bf16[12,32,128]{2,1,0:T(8,128)(2,1)S(1)}, u32[]{:S(2)}, u32[]{:S(2)}) collective-permute-start(bf16[12,32,128]{2,1,0:T(8,128)(2,1)} %bitcast.13), channel_id=1, source_target_pairs={{0,8},{4,12},{8,0},{12,4},{1,9},{5,13},{9,1},{13,5},{2,10},{6,14},... | collective-permute-start | bytes 294920 | tf_op jit(solution)/shard_map/ppermute | solution.py:77
  8.2 1.3 %stage.1 = (bf16[12,4,48,128]{3,2,1,0:T(8,128)(2,1)S(1)}, bf16[1024,128]{1,0:T(8,128)(2,1)S(1)}, bf16[12,32,128]{2,1,0:T(8,128)(2,1)S(1)}, bf16[12,32,128]{2,1,0:T(8,128)(2,1)S(1)}) custom-call(bf16[12,4,48,128]{3,2,1,0:T(8,128)(2,1)} %bitcast.7, bf16[32,32,128]{2,1,0:T(8,128)(2,1)} %bitcast.8, bf16[12,32,128]{2,1,0:T(8,128)(2,1)} %bitcast.11, ...), custom_call_target="tpu_custom_call" | custom-call | flops 1073741824 | bytes 65536 | tf_op jit(solution)/shard_map/stage/pallas_call | solution.py:56
  9.5 1.4 %outer_grad.1.z_ref = bf16[8,4,48,1536]{3,2,1,0:T(8,128)(2,1)S(1)} custom-call(bf16[12,4,48,128]{3,2,1,0:T(8,128)(2,1)S(1)} %get-tuple-element.37.grad_ref, bf16[1024,128]{1,0:T(8,128)(2,1)S(1)} %get-tuple-element.43.weight_ref), custom_call_target="tpu_custom_call" | custom-call | bytes 65536 | tf_op jit(solution)/shard_map/outer_grad/pallas_call | solution.py:56
  11.6 2.1 %collective-permute-done.2.refs_4_ = bf16[12,32,128]{2,1,0:T(8,128)(2,1)S(1)} collective-permute-done((bf16[12,32,128]{2,1,0:T(8,128)(2,1)}, bf16[12,32,128]{2,1,0:T(8,128)(2,1)S(1)}, u32[]{:S(2)}, u32[]{:S(2)}) %collective-permute-start.2) | collective-permute-done | bytes 98336 | tf_op jit(solution)/shard_map/ppermute | solution.py:77
  13.7 1.9 %outer_mean_near.1 = (bf16[6,4,48,1024]{3,2,1,0:T(8,128)(2,1)S(1)}, f32[1024,128]{1,0:T(8,128)S(1)}, bf16[8,4,48,128]{3,2,1,0:T(8,128)(2,1)S(1)}) custom-call(bf16[12,4,48,128]{3,2,1,0:T(8,128)(2,1)S(1)} %get-tuple-element.37.grad_ref, bf16[12,32,128]{2,1,0:T(8,128)(2,1)S(1)} %get-tuple-element.38.refs_0_, ...), custom_call_target="tpu_custom_call" | custom-call | flops 1073741824 | bytes 65536 | tf_op jit(solution)/shard_map/outer_mean_near/pallas_call | solution.py:56
  15.9 1.9 %outer_mean_far.1 = (bf16[6,4,48,1024]{3,2,1,0:T(8,128)(2,1)S(1)}, f32[2,256,128]{2,1,0:T(8,128)S(1)}, f32[2,256,128]{2,1,0:T(8,128)S(1)}) custom-call(bf16[12,4,48,128]{3,2,1,0:T(8,128)(2,1)S(1)} %get-tuple-element.37.grad_ref, bf16[8,4,48,128]{3,2,1,0:T(8,128)(2,1)S(1)} %get-tuple-element.41.be_ref, f32[1024,128]{1,0:T(8,128)S(1)} %get-tuple-element.42.near_ref, ...), custom_call_target="tpu_custom_call" | custom-call | flops 1073741824 | bytes 65536 | tf_op jit(solution)/shard_map/outer_mean_far/pallas_call | solution.py:56
  17.8 1.2 %left_grad.1 = (f32[2,12,32,128]{3,2,1,0:T(8,128)S(1)}, bf16[2,12,32,128]{3,2,1,0:T(8,128)(2,1)S(1)}) custom-call(bf16[8,4,48,1536]{3,2,1,0:T(8,128)(2,1)S(1)} %outer_grad.1.z_ref, bf16[8,4,48,128]{3,2,1,0:T(8,128)(2,1)S(1)} %get-tuple-element.41.be_ref), custom_call_target="tpu_custom_call" | custom-call | flops 3221225472 | bytes 65536 | tf_op jit(solution)/shard_map/left_grad/pallas_call | solution.py:56
  19.6 1.4 %collective-permute-start.7 = (bf16[1,256,128]{2,1,0:T(8,128)(2,1)S(1)}, bf16[1,256,128]{2,1,0:T(8,128)(2,1)S(1)}, u32[]{:S(2)}, u32[]{:S(2)}) collective-permute-start(bf16[1,256,128]{2,1,0:T(8,128)(2,1)S(1)} %get-tuple-element.51), channel_id=1, source_target_pairs={{0,8},{4,12},{8,0},{12,4},{1,9},{5,13},{9,1},{13,5},{2,10},{6,14},... | collective-permute-start | bytes 196616 | tf_op jit(solution)/shard_map/ppermute | solution.py:77
  21.0 1.5 %right_grad.1 = (f32[2,12,32,128]{3,2,1,0:T(8,128)S(1)}, bf16[2,12,32,128]{3,2,1,0:T(8,128)(2,1)S(1)}) custom-call(bf16[8,4,48,1536]{3,2,1,0:T(8,128)(2,1)S(1)} %outer_grad.1.z_ref, bf16[12,32,128]{2,1,0:T(8,128)(2,1)S(1)} %get-tuple-element.38.refs_0_, bf16[12,32,128]{2,1,0:T(8,128)(2,1)S(1)} %collective-permute-done.refs_1_, ...), custom_call_target="tpu_custom_call" | custom-call | flops 3221225472 | bytes 65536 | tf_op jit(solution)/shard_map/right_grad/pallas_call | solution.py:56
  22.6 1.3 %collective-permute-done.7.got = bf16[1,256,128]{2,1,0:T(8,128)(2,1)S(1)} collective-permute-done((bf16[1,256,128]{2,1,0:T(8,128)(2,1)S(1)}, bf16[1,256,128]{2,1,0:T(8,128)(2,1)S(1)}, u32[]{:S(2)}, u32[]{:S(2)}) %collective-permute-start.7) | collective-permute-done | bytes 65568 | tf_op jit(solution)/shard_map/ppermute | solution.py:77
  24.0 2.4 %collective-permute-start.9 = (bf16[256,128]{1,0:T(8,128)(2,1)S(1)}, bf16[256,128]{1,0:T(8,128)(2,1)S(1)}, u32[]{:S(2)}, u32[]{:S(2)}) collective-permute-start(bf16[256,128]{1,0:T(8,128)(2,1)S(1)} %weight_row_sum.1.own), channel_id=1, source_target_pairs={{0,2},{1,3},{2,0},{3,1},{4,6},{5,7},{6,4},{7,5},{8,10},{9,11},{10,... | collective-permute-start | bytes 196616 | tf_op jit(solution)/shard_map/ppermute | solution.py:77
  26.4 2.1 %pair_update.1 = bf16[12,4,48,128]{3,2,1,0:T(8,128)(2,1)} custom-call(bf16[6,4,48,1024]{3,2,1,0:T(8,128)(2,1)S(1)} %get-tuple-element.55.near_ref, bf16[6,4,48,1024]{3,2,1,0:T(8,128)(2,1)S(1)} %get-tuple-element.56.far_ref, bf16[1024,128]{1,0:T(8,128)(2,1)S(1)} %get-tuple-element.43.weight_ref, f32[1,128]{1,0:T(1,128)S(1)} %bitcast.6), custom_call_target="tpu_custom_call" | custom-call | flops 17179869184 | bytes 65536 | tf_op jit(solution)/shard_map/pair_update/pallas_call | solution.py:56
  28.6 1.5 %collective-permute-start.12 = (bf16[1,12,32,128]{3,2,1,0:T(8,128)(2,1)S(1)}, bf16[1,12,32,128]{3,2,1,0:T(8,128)(2,1)S(1)}, u32[]{:S(2)}, u32[]{:S(2)}) collective-permute-start(bf16[1,12,32,128]{3,2,1,0:T(8,128)(2,1)S(1)} %get-tuple-element.60), channel_id=1, source_target_pairs={{0,8},{4,12},{8,0},{12,4},{1,9},{5,13},{9,1},{13,5},{2,10},{6,14},... | collective-permute-start | bytes 294920 | tf_op jit(solution)/shard_map/ppermute | solution.py:77
  30.2 0.7 %collective-permute-start.13 = (bf16[256,128]{1,0:T(8,128)(2,1)S(1)}, bf16[256,128]{1,0:T(8,128)(2,1)S(1)}, u32[]{:S(2)}, u32[]{:S(2)}) collective-permute-start(bf16[256,128]{1,0:T(8,128)(2,1)S(1)} %weight_col_sum_2.1.own), channel_id=1, source_target_pairs={{0,1},{1,0},{2,3},{3,2},{4,5},{5,4},{6,7},{7,6},{8,9},{9,8},{10,11... | collective-permute-start | bytes 196616 | tf_op jit(solution)/shard_map/ppermute | solution.py:77
  30.9 1.4 %collective-permute-start.11 = (bf16[1,12,32,128]{3,2,1,0:T(8,128)(2,1)S(1)}, bf16[1,12,32,128]{3,2,1,0:T(8,128)(2,1)S(1)}, u32[]{:S(2)}, u32[]{:S(2)}) collective-permute-start(bf16[1,12,32,128]{3,2,1,0:T(8,128)(2,1)S(1)} %get-tuple-element.64), channel_id=1, source_target_pairs={{0,2},{1,3},{2,0},{3,1},{4,6},{5,7},{6,4},{7,5},{8,10},{9,11},{10,... | collective-permute-start | bytes 294920 | tf_op jit(solution)/shard_map/ppermute | solution.py:77
  32.3 2.2 %collective-permute-done.13.got = bf16[256,128]{1,0:T(8,128)(2,1)S(1)} collective-permute-done((bf16[256,128]{1,0:T(8,128)(2,1)S(1)}, bf16[256,128]{1,0:T(8,128)(2,1)S(1)}, u32[]{:S(2)}, u32[]{:S(2)}) %collective-permute-start.13) | collective-permute-done | bytes 65568 | tf_op jit(solution)/shard_map/ppermute | solution.py:77
  34.6 0.7 %collective-permute-start.15 = (bf16[256,128]{1,0:T(8,128)(2,1)S(1)}, bf16[256,128]{1,0:T(8,128)(2,1)S(1)}, u32[]{:S(2)}, u32[]{:S(2)}) collective-permute-start(bf16[256,128]{1,0:T(8,128)(2,1)S(1)} %weight_col_sum_1.1.refs_0_), channel_id=1, source_target_pairs={{0,8},{4,12},{8,0},{12,4},{1,9},{5,13},{9,1},{13,5},{2,10},{6,14},... | collective-permute-start | bytes 196616 | tf_op jit(solution)/shard_map/ppermute | solution.py:77
  35.3 1.1 %collective-permute-start.14 = (bf16[256,128]{1,0:T(8,128)(2,1)S(1)}, bf16[256,128]{1,0:T(8,128)(2,1)S(1)}, u32[]{:S(2)}, u32[]{:S(2)}) collective-permute-start(bf16[256,128]{1,0:T(8,128)(2,1)S(1)} %weight_col_sum_1.1.refs_0_), channel_id=1, source_target_pairs={{0,4},{4,0},{8,12},{12,8},{1,5},{5,1},{9,13},{13,9},{2,6},{6,2},{1... | collective-permute-start | bytes 196616 | tf_op jit(solution)/shard_map/ppermute | solution.py:77
  36.4 1.1 %collective-permute-done.11.l_got = bf16[1,12,32,128]{3,2,1,0:T(8,128)(2,1)S(1)} collective-permute-done((bf16[1,12,32,128]{3,2,1,0:T(8,128)(2,1)S(1)}, bf16[1,12,32,128]{3,2,1,0:T(8,128)(2,1)S(1)}, u32[]{:S(2)}, u32[]{:S(2)}) %collective-permute-start.11) | collective-permute-done | bytes 98336 | tf_op jit(solution)/shard_map/ppermute | solution.py:77
  37.5 0.8 %collective-permute-done.16.refs_3_ = bf16[256,128]{1,0:T(8,128)(2,1)S(1)} collective-permute-done((bf16[256,128]{1,0:T(8,128)(2,1)S(1)}, bf16[256,128]{1,0:T(8,128)(2,1)S(1)}, u32[]{:S(2)}, u32[]{:S(2)}) %collective-permute-start.16) | collective-permute-done | bytes 65568 | tf_op jit(solution)/shard_map/ppermute | solution.py:77
  38.4 1.2 %collective-permute-done.15.refs_2_ = bf16[256,128]{1,0:T(8,128)(2,1)S(1)} collective-permute-done((bf16[256,128]{1,0:T(8,128)(2,1)S(1)}, bf16[256,128]{1,0:T(8,128)(2,1)S(1)}, u32[]{:S(2)}, u32[]{:S(2)}) %collective-permute-start.15) | collective-permute-done | bytes 65568 | tf_op jit(solution)/shard_map/ppermute | solution.py:77
  39.6 1.0 %totals.1 = (f32[1,12,32,128]{3,2,1,0:T(8,128)}, f32[1,12,32,128]{3,2,1,0:T(8,128)}, f32[1024,128]{1,0:T(8,128)}) custom-call(f32[1,12,32,128]{3,2,1,0:T(8,128)S(1)} %get-tuple-element.63.l_keep, bf16[1,12,32,128]{3,2,1,0:T(8,128)(2,1)S(1)} %collective-permute-done.11.l_got, f32[1,12,32,128]{3,2,1,0:T(8,128)S(1)} %get-tuple-element.65.r_keep, ...), custom_call_target="tpu_custom_call" | custom-call | flops 1073741824 | bytes 65536 | tf_op jit(solution)/shard_map/totals/pallas_call | solution.py:56
  (26 shorter events, 2.5 us)
Async XLA Ops:
  0.6 10.3 %collective-permute-start.4 = (bf16[12,32,128]{2,1,0:T(8,128)(2,1)}, bf16[12,32,128]{2,1,0:T(8,128)(2,1)S(1)}, u32[]{:S(2)}, u32[]{:S(2)}) collective-permute-start(bf16[12,32,128]{2,1,0:T(8,128)(2,1)} %bitcast.9), channel_id=1, source_target_pairs={{0,2},{1,3},{2,0},{3,1},{4,6},{5,7},{6,4},{7,5},{8,10},{9,11},{10,... | collective-permute-start | bytes 294920 | tf_op jit(solution)/shard_map/ppermute | solution.py:77
  4.7 6.7 %collective-permute-start = (bf16[12,32,128]{2,1,0:T(8,128)(2,1)}, bf16[12,32,128]{2,1,0:T(8,128)(2,1)S(1)}, u32[]{:S(2)}, u32[]{:S(2)}) collective-permute-start(bf16[12,32,128]{2,1,0:T(8,128)(2,1)} %bitcast.10), channel_id=1, source_target_pairs={{0,1},{1,0},{2,3},{3,2},{4,5},{5,4},{6,7},{7,6},{8,9},{9,8},{10,11... | collective-permute-start | bytes 294920 | tf_op jit(solution)/shard_map/ppermute | solution.py:77
  6.3 5.3 %collective-permute-start.3 = (bf16[12,32,128]{2,1,0:T(8,128)(2,1)}, bf16[12,32,128]{2,1,0:T(8,128)(2,1)S(1)}, u32[]{:S(2)}, u32[]{:S(2)}) collective-permute-start(bf16[12,32,128]{2,1,0:T(8,128)(2,1)} %bitcast.12), channel_id=1, source_target_pairs={{0,12},{4,8},{8,4},{12,0},{1,13},{5,9},{9,5},{13,1},{2,14},{6,10},... | collective-permute-start | bytes 294920 | tf_op jit(solution)/shard_map/ppermute | solution.py:77
  6.7 7.0 %collective-permute-start.2 = (bf16[12,32,128]{2,1,0:T(8,128)(2,1)}, bf16[12,32,128]{2,1,0:T(8,128)(2,1)S(1)}, u32[]{:S(2)}, u32[]{:S(2)}) collective-permute-start(bf16[12,32,128]{2,1,0:T(8,128)(2,1)} %bitcast.13), channel_id=1, source_target_pairs={{0,8},{4,12},{8,0},{12,4},{1,9},{5,13},{9,1},{13,5},{2,10},{6,14},... | collective-permute-start | bytes 294920 | tf_op jit(solution)/shard_map/ppermute | solution.py:77
  7.8 5.9 %collective-permute-start.1 = (bf16[12,32,128]{2,1,0:T(8,128)(2,1)}, bf16[12,32,128]{2,1,0:T(8,128)(2,1)S(1)}, u32[]{:S(2)}, u32[]{:S(2)}) collective-permute-start(bf16[12,32,128]{2,1,0:T(8,128)(2,1)} %bitcast.14), channel_id=1, source_target_pairs={{0,4},{4,0},{8,12},{12,8},{1,5},{5,1},{9,13},{13,9},{2,6},{6,2},{1... | collective-permute-start | bytes 294920 | tf_op jit(solution)/shard_map/ppermute | solution.py:77
  10.9 4.9 %collective-permute-start.5 = (bf16[12,32,128]{2,1,0:T(8,128)(2,1)S(1)}, bf16[12,32,128]{2,1,0:T(8,128)(2,1)S(1)}, u32[]{:S(2)}, u32[]{:S(2)}) collective-permute-start(bf16[12,32,128]{2,1,0:T(8,128)(2,1)S(1)} %collective-permute-done.4.refs_0_.refs_2_), channel_id=1, source_target_pairs={{0,1},{1,0},{2,3},{3,2},{4,5},{5,4},{6,7},{7,6},{8,9},{9,8},{10,11... | collective-permute-start | bytes 294920 | tf_op jit(solution)/shard_map/ppermute | solution.py:77
  17.8 1.8 %collective-permute-start.6 = (f32[2,256,128]{2,1,0:T(8,128)S(1)}, f32[2,256,128]{2,1,0:T(8,128)S(1)}, u32[]{:S(2)}, u32[]{:S(2)}) collective-permute-start(f32[2,256,128]{2,1,0:T(8,128)S(1)} %get-tuple-element.46), channel_id=1, source_target_pairs={{0,4},{4,0},{8,12},{12,8},{1,5},{5,1},{9,13},{13,9},{2,6},{6,2},{1... | collective-permute-start | bytes 786440 | tf_op jit(solution)/shard_map/ppermute | solution.py:77
  19.1 11.8 %collective-permute-start.8 = (bf16[2,12,32,128]{3,2,1,0:T(8,128)(2,1)S(1)}, bf16[2,12,32,128]{3,2,1,0:T(8,128)(2,1)S(1)}, u32[]{:S(2)}, u32[]{:S(2)}) collective-permute-start(bf16[2,12,32,128]{3,2,1,0:T(8,128)(2,1)S(1)} %get-tuple-element.48), channel_id=1, source_target_pairs={{0,1},{1,0},{2,3},{3,2},{4,5},{5,4},{6,7},{7,6},{8,9},{9,8},{10,11... | collective-permute-start | bytes 589832 | tf_op jit(solution)/shard_map/ppermute | solution.py:77
  19.6 4.3 %collective-permute-start.7 = (bf16[1,256,128]{2,1,0:T(8,128)(2,1)S(1)}, bf16[1,256,128]{2,1,0:T(8,128)(2,1)S(1)}, u32[]{:S(2)}, u32[]{:S(2)}) collective-permute-start(bf16[1,256,128]{2,1,0:T(8,128)(2,1)S(1)} %get-tuple-element.51), channel_id=1, source_target_pairs={{0,8},{4,12},{8,0},{12,4},{1,9},{5,13},{9,1},{13,5},{2,10},{6,14},... | collective-permute-start | bytes 196616 | tf_op jit(solution)/shard_map/ppermute | solution.py:77
  22.6 3.8 %copy-start = (f32[128]{0:T(128)S(1)}, f32[128]{0:T(128)}, u32[]{:S(2)}) copy-start(f32[128]{0:T(128)} %param.8) | copy-start | bytes 1540
  22.6 6.0 %collective-permute-start.10 = (bf16[2,12,32,128]{3,2,1,0:T(8,128)(2,1)S(1)}, bf16[2,12,32,128]{3,2,1,0:T(8,128)(2,1)S(1)}, u32[]{:S(2)}, u32[]{:S(2)}) collective-permute-start(bf16[2,12,32,128]{3,2,1,0:T(8,128)(2,1)S(1)} %get-tuple-element.53), channel_id=1, source_target_pairs={{0,4},{4,0},{8,12},{12,8},{1,5},{5,1},{9,13},{13,9},{2,6},{6,2},{1... | collective-permute-start | bytes 589832 | tf_op jit(solution)/shard_map/ppermute | solution.py:77
  24.0 6.2 %collective-permute-start.9 = (bf16[256,128]{1,0:T(8,128)(2,1)S(1)}, bf16[256,128]{1,0:T(8,128)(2,1)S(1)}, u32[]{:S(2)}, u32[]{:S(2)}) collective-permute-start(bf16[256,128]{1,0:T(8,128)(2,1)S(1)} %weight_row_sum.1.own), channel_id=1, source_target_pairs={{0,2},{1,3},{2,0},{3,1},{4,6},{5,7},{6,4},{7,5},{8,10},{9,11},{10,... | collective-permute-start | bytes 196616 | tf_op jit(solution)/shard_map/ppermute | solution.py:77
  28.6 9.0 %collective-permute-start.12 = (bf16[1,12,32,128]{3,2,1,0:T(8,128)(2,1)S(1)}, bf16[1,12,32,128]{3,2,1,0:T(8,128)(2,1)S(1)}, u32[]{:S(2)}, u32[]{:S(2)}) collective-permute-start(bf16[1,12,32,128]{3,2,1,0:T(8,128)(2,1)S(1)} %get-tuple-element.60), channel_id=1, source_target_pairs={{0,8},{4,12},{8,0},{12,4},{1,9},{5,13},{9,1},{13,5},{2,10},{6,14},... | collective-permute-start | bytes 294920 | tf_op jit(solution)/shard_map/ppermute | solution.py:77
  30.2 4.3 %collective-permute-start.13 = (bf16[256,128]{1,0:T(8,128)(2,1)S(1)}, bf16[256,128]{1,0:T(8,128)(2,1)S(1)}, u32[]{:S(2)}, u32[]{:S(2)}) collective-permute-start(bf16[256,128]{1,0:T(8,128)(2,1)S(1)} %weight_col_sum_2.1.own), channel_id=1, source_target_pairs={{0,1},{1,0},{2,3},{3,2},{4,5},{5,4},{6,7},{7,6},{8,9},{9,8},{10,11... | collective-permute-start | bytes 196616 | tf_op jit(solution)/shard_map/ppermute | solution.py:77
  30.9 6.6 %collective-permute-start.11 = (bf16[1,12,32,128]{3,2,1,0:T(8,128)(2,1)S(1)}, bf16[1,12,32,128]{3,2,1,0:T(8,128)(2,1)S(1)}, u32[]{:S(2)}, u32[]{:S(2)}) collective-permute-start(bf16[1,12,32,128]{3,2,1,0:T(8,128)(2,1)S(1)} %get-tuple-element.64), channel_id=1, source_target_pairs={{0,2},{1,3},{2,0},{3,1},{4,6},{5,7},{6,4},{7,5},{8,10},{9,11},{10,... | collective-permute-start | bytes 294920 | tf_op jit(solution)/shard_map/ppermute | solution.py:77
  34.5 3.8 %collective-permute-start.16 = (bf16[256,128]{1,0:T(8,128)(2,1)S(1)}, bf16[256,128]{1,0:T(8,128)(2,1)S(1)}, u32[]{:S(2)}, u32[]{:S(2)}) collective-permute-start(bf16[256,128]{1,0:T(8,128)(2,1)S(1)} %weight_col_sum_1.1.refs_0_), channel_id=1, source_target_pairs={{0,12},{4,8},{8,4},{12,0},{1,13},{5,9},{9,5},{13,1},{2,14},{6,10},... | collective-permute-start | bytes 196616 | tf_op jit(solution)/shard_map/ppermute | solution.py:77
  34.6 5.0 %collective-permute-start.15 = (bf16[256,128]{1,0:T(8,128)(2,1)S(1)}, bf16[256,128]{1,0:T(8,128)(2,1)S(1)}, u32[]{:S(2)}, u32[]{:S(2)}) collective-permute-start(bf16[256,128]{1,0:T(8,128)(2,1)S(1)} %weight_col_sum_1.1.refs_0_), channel_id=1, source_target_pairs={{0,8},{4,12},{8,0},{12,4},{1,9},{5,13},{9,1},{13,5},{2,10},{6,14},... | collective-permute-start | bytes 196616 | tf_op jit(solution)/shard_map/ppermute | solution.py:77
  35.3 4.3 %collective-permute-start.14 = (bf16[256,128]{1,0:T(8,128)(2,1)S(1)}, bf16[256,128]{1,0:T(8,128)(2,1)S(1)}, u32[]{:S(2)}, u32[]{:S(2)}) collective-permute-start(bf16[256,128]{1,0:T(8,128)(2,1)S(1)} %weight_col_sum_1.1.refs_0_), channel_id=1, source_target_pairs={{0,4},{4,0},{8,12},{12,8},{1,5},{5,1},{9,13},{13,9},{2,6},{6,2},{1... | collective-permute-start | bytes 196616 | tf_op jit(solution)/shard_map/ppermute | solution.py:77

commit v6 on v5

--- a/solution.py
+++ b/solution.py
@@ -13,10 +13,6 @@
 
 def dot_nt(x, y):
     return lax.dot_general(x, y, (((1,), (1,)), ((), ())), preferred_element_type=F32)
-
-
-def dot_tn(x, y):
-    return lax.dot_general(x, y, (((0,), (0,)), ((), ())), preferred_element_type=F32)
 
 
 def dot_nn(x, y):
@@ -85,15 +81,6 @@
     return [1 << s for s in range(n.bit_length() - 1)]
 
 
-def gather_halves(own, axis):
-    n = lax.axis_size(axis)
-    parts = {0: own}
-    for bit in reversed(bits_of(n)):
-        for k in sorted(parts):
-            parts[k ^ bit] = swap(parts[k], axis, bit)
-    return [parts[k] for k in range(n)]
-
-
 def gather_far(own, axis):
     n = lax.axis_size(axis)
     return {0: own, n // 2: swap(own, axis, n // 2)}
@@ -109,13 +96,6 @@
 
 def after(x, *earlier):
     return lax.optimization_barrier((x, earlier))[0]
-
-
-def tree_sum(parts):
-    parts = [part.astype(F32) for part in parts]
-    while len(parts) > 1:
-        parts = [parts[i] + parts[i + 1] for i in range(0, len(parts), 2)]
-    return parts[0]
 
 
 def on_device(left_factors, right_factors, out_weight, out_bias, pair_grad):
@@ -127,7 +107,6 @@
     rows, cols, width = pair_grad.shape
     pairs = chan * chan
     row4, chan4 = rows // 4, chan // 4
-    half4 = row4 // 2
     near, half = n_col // 2, n_row // 2
     inv_samples = 1.0 / samples
     wide = 2 * LANES
@@ -202,77 +181,98 @@
     left_parts = gather_rest(left_parts, "col")
     left_parts[0] = left_vmem
 
-    def outer_mean(a_whole, be, grad_ref, y_ref, group, masks):
-        am = a_whole[...].reshape(rows * chan // 2, samples)
-        ams = [xor_groups(am, a, chan) for a in range(4)]
-        for blk in range(rows * chan // 2 // wide):
+    def outer_mean(a_refs, first, be, grad_ref, y_ref, a_whole):
+        me = lax.axis_index("col")
+        count = a_whole.shape[0]
+        assemble(a_whole, a_refs, first, me)
+        group = (me ^ first) // len(a_refs)
+        masks = lane_masks(cols, chan)
+        ams = [xor_groups(a_whole[...].reshape(count * chan, samples), a, chan) for a in range(4)]
+        for at in range(0, count * chan, wide):
+            size = min(wide, count * chan - at)
             for e in range(0, chan4, 4):
                 qs = [
-                    dot_nt(
-                        be[e : e + 4, a].reshape(4 * cols, samples),
-                        ams[a][blk * wide : (blk + 1) * wide],
-                    ).astype(BF)
+                    dot_nt(be[e : e + 4, a].reshape(4 * cols, samples), ams[a][at : at + size])
                     for a in range(4)
                 ]
-                for m, h in [(m, h) for m in range(4) for h in range(2)]:
+                qs = [q.astype(BF) for q in qs]
+                for m, h in [(m, h) for m in range(4) for h in range(size // LANES)]:
                     ys = trade([tile(q, m, h) for q in qs], masks)
                     for b in range(4):
-                        y_ref[2 * blk + h, b, :, (e + m) * LANES : (e + m + 1) * LANES] = ys[b]
+                        lanes = slice((e + m) * LANES, (e + m + 1) * LANES)
+                        y_ref[at // LANES + h, b, :, lanes] = ys[b]
         acc = None
         for b in range(4):
-            g = grad_ref[pl.ds(group * half4, half4), b].reshape(half4 * cols, width)
-            d = dot_nn(jnp.transpose(g), y_ref[:, b].reshape(half4 * cols, pairs))
+            g = grad_ref[pl.ds(group * (count // 4), count // 4), b]
+            d = dot_nn(
+                jnp.transpose(g.reshape(count // 4 * cols, width)),
+                y_ref[:, b].reshape(count // 4 * cols, pairs),
+            )
             d = xor_groups(jnp.transpose(d), b, chan)
             acc = d if acc is None else acc + d
         return acc
 
-    mean_scratch = [pltpu.VMEM((rows // 2, chan, samples), BF)]
+    bounds = [0, near, near + near // 2, n_col]
+
+    def mean_outs(step):
+        count = (bounds[step + 1] - bounds[step]) * left_piece
+        y = struct((count // 4, 4, cols, pairs), BF)
+        return y, pltpu.VMEM((count, chan, samples), BF)
 
     def near_kernel(grad_ref, *refs):
         a_refs, b_refs = refs[:near], refs[near : near + n_row]
-        y_ref, weight_ref, be_ref, a_whole, b_whole = refs[near + n_row :]
-        me = lax.axis_index("col")
-        assemble(a_whole, a_refs, 0, me)
+        y_ref, acc_ref, be_ref, a_whole, b_whole = refs[near + n_row :]
         assemble(b_whole, b_refs, 0, lax.axis_index("row"))
-        be = swap01(b_whole[...]).reshape(chan4, 4, cols, samples)
-        be_ref[...] = be
-        weight_ref[...] = outer_mean(
-            a_whole, be, grad_ref, y_ref, me // near, lane_masks(cols, chan)
-        )
-
-    y_struct = struct((half4, 4, cols, pairs), BF)
+        be_ref[...] = swap01(b_whole[...]).reshape(chan4, 4, cols, samples)
+        acc_ref[...] = outer_mean(a_refs, 0, be_ref, grad_ref, y_ref, a_whole)
+
+    y_struct, whole = mean_outs(0)
     y_near, weight_near, right_e = call(
         near_kernel,
         [y_struct, struct((pairs, width), F32), struct((chan4, 4, cols, samples), BF)],
-        mean_scratch + [pltpu.VMEM((cols, chan, samples), BF)],
+        [whole, pltpu.VMEM((cols, chan, samples), BF)],
         "outer_mean_near",
-        grad_vmem,
+        after(grad_vmem, z),
         *left_parts[:near],
         *right_parts,
     )
 
-    def far_kernel(grad_ref, be_ref, near_ref, *refs):
-        a_refs, y_ref = refs[:near], refs[near]
-        keep, send, a_whole, total = refs[near + 1 :]
-        me = lax.axis_index("col")
-        assemble(a_whole, a_refs, near, me)
-        acc = outer_mean(
-            a_whole, be_ref, grad_ref, y_ref, 1 - me // near, lane_masks(cols, chan)
-        )
-        acc = (acc + near_ref[...]) * (inv_samples / (rows * n_row))
+    def middle_kernel(grad_ref, be_ref, before_ref, *refs):
+        a_refs, (y_ref, acc_ref, a_whole) = refs[:-3], refs[-3:]
+        acc = outer_mean(a_refs, bounds[1], be_ref, grad_ref, y_ref, a_whole)
+        acc_ref[...] = acc + before_ref[...]
+
+    y_struct, whole = mean_outs(1)
+    y_middle, weight_middle = call(
+        middle_kernel,
+        [y_struct, struct((pairs, width), F32)],
+        [whole],
+        "outer_mean_middle",
+        grad_vmem,
+        right_e,
+        weight_near,
+        *left_parts[bounds[1] : bounds[2]],
+    )
+
+    def far_kernel(grad_ref, be_ref, before_ref, *refs):
+        a_refs, (y_ref, keep, send, a_whole, total) = refs[:-5], refs[-5:]
+        acc = outer_mean(a_refs, bounds[2], be_ref, grad_ref, y_ref, a_whole)
+        acc = (acc + before_ref[...]) * (inv_samples / (rows * n_row))
         total[...] = jnp.swapaxes(acc.reshape(chan, chan, width), 0, 1).reshape(pairs, width)
         hand_out_halves(total, keep, send, lax.axis_index("row"))
 
+    y_struct, whole = mean_outs(2)
     y_far, weight_keep, weight_send = call(
         far_kernel,
         [y_struct] + [struct((half, weight_piece, width), F32)] * 2,
-        mean_scratch + [pltpu.VMEM((pairs, width), F32)],
+        [whole, pltpu.VMEM((pairs, width), F32)],
         "outer_mean_far",
         grad_vmem,
         right_e,
-        weight_near,
-        *left_parts[near:],
-    )
+        weight_middle,
+        *left_parts[bounds[2] :],
+    )
+
     def halve_kernel(keep, got, next_keep, next_send):
         for k in range(keep.shape[0]):
             out = next_send if k % 2 else next_keep
@@ -344,33 +344,39 @@
         after(swap(weight_send, "row", half), right_send),
     )
 
-    def pair_kernel(near_ref, far_ref, weight_ref, bias_ref, p_hbm, p_ref, sem):
+    ys = [y_near, y_middle, y_far]
+
+    def pair_kernel(*refs):
+        y_refs, (weight_ref, bias_ref, p_hbm, p_ref, sem) = refs[:3], refs[3:]
         me = lax.axis_index("col")
         copies = []
-        for part, y_ref in enumerate((near_ref, far_ref)):
-            group = part ^ (me // near)
+        at = 0
+        for step, y_ref in enumerate(y_refs):
+            count = y_ref.shape[0]
+            group = (me ^ bounds[step]) // (bounds[step + 1] - bounds[step])
             for b in range(4):
                 d = dot_nn(
-                    y_ref[:, b].reshape(half4 * cols, pairs), xor_groups(weight_ref[...], b, chan)
+                    y_ref[:, b].reshape(count * cols, pairs), xor_groups(weight_ref[...], b, chan)
                 )
                 d = d * inv_samples + bias_ref[...]
-                p_ref[part, :, b] = d.reshape(half4, cols, width).astype(BF)
+                p_ref[at : at + count, b] = d.reshape(count, cols, width).astype(BF)
             copies.append(
                 pltpu.make_async_copy(
-                    p_ref.at[part], p_hbm.at[pl.ds(group * half4, half4)], sem.at[part]
+                    p_ref.at[pl.ds(at, count)], p_hbm.at[pl.ds(group * count, count)], sem.at[step]
                 )
             )
             copies[-1].start()
+            at += count
         for copy in copies:
             copy.wait()
 
     (pair_update,) = call(
         pair_kernel,
         [struct((row4, 4, cols, width), BF)],
-        [pltpu.VMEM((2, half4, 4, cols, width), BF), pltpu.SemaphoreType.DMA((2,))],
+        [pltpu.VMEM((row4, 4, cols, width), BF), pltpu.SemaphoreType.DMA((3,))],
         "pair_update",
-        after(y_near, weight_own),
-        y_far,
+        after(ys[0], weight_own),
+        *ys[1:],
         weight_e,
         out_bias.reshape(1, width),
         cost=16,
@@ -406,28 +412,47 @@
             tied = left_send
     weight_rows = swap_all([weight_sum] * n_row, "row")
 
-    def totals_kernel(l_keep, l_got, r_keep, r_got, *refs):
-        l_out, r_out, w_out = refs[n_row:]
+    def totals_kernel(l_keep, l_got, r_keep, r_got, l_out, r_out):
         l_out[...] = l_keep[...] + l_got[...].astype(F32)
         r_out[...] = r_keep[...] + r_got[...].astype(F32)
-        me = lax.axis_index("row")
-        for k in range(n_row):
-            w_out[pl.ds((me ^ k) * weight_piece, weight_piece)] = refs[k][...].astype(F32)
-
-    grad_left, grad_right, grad_weight = call(
+
+    grad_left, grad_right = call(
         totals_kernel,
         [
             struct((1, left_piece, chan, samples), F32),
             struct((1, right_piece, chan, samples), F32),
-            struct((pairs, width), F32),
         ],
         [],
-        "totals",
-        left_keep,
+        "left_right_totals",
+        after(left_keep, weight_sum),
         left_got,
         right_keep,
         right_got,
+    )
+
+    def place_kernel(*refs):
+        w_hbm, wide_ref, sems = refs[n_row:]
+        me = lax.axis_index("row")
+        copies = []
+        for k in range(n_row):
+            wide_ref[k] = refs[k][...].astype(F32)
+            target = w_hbm.at[pl.ds((me ^ k) * weight_piece, weight_piece)]
+            copies.append(pltpu.make_async_copy(wide_ref.at[k], target, sems.at[k]))
+            copies[-1].start()
+        for copy in copies:
+            copy.wait()
+
+    weight_rows[-1] = after(weight_rows[-1], grad_right)
+    (grad_weight,) = call(
+        place_kernel,
+        [struct((pairs, width), F32)],
+        [
+            pltpu.VMEM((n_row, weight_piece, width), F32),
+            pltpu.SemaphoreType.DMA((n_row,)),
+        ],
+        "weight_place",
         *weight_rows,
+        hbm_out=(0,),
     )
     return (pair_update.reshape(rows, cols, width), grad_left, grad_right, grad_weight)
 

time: 40.7 us -> 40.3 us (level)
  starting transfers between devices: 18.1 us -> 16.6 us
  Pallas kernels: 12.6 us -> 13.9 us
    ppermute x17, starting transfers between devices: 18.1 us -> 16.6 us  [swap(): return lax.ppermute(x, axis, [(d, d ^ k) for d in range(n)])]
    pallas_call x14 -> x16, Pallas kernels: 12.6 us -> 13.9 us  [call(): pl.pallas_call(kernel, out_shape=outs, in_specs=[hbm if i in hbm_in else...]
  transfers between devices with their start and end apart: 17 -> 17, of which waited for: 8 -> 7; matrix products, arithmetic and copies ran while one was open for 0% -> 0% of each run, Pallas kernels for 24% -> 29%
where the time goes in v6:
time: 40.3 us; the launch traced here: 40.2 us
  starting transfers between devices  16.6 us (41%)
  Pallas kernels  13.9 us (34%)
  waiting for transfers between devices  8.85 us (22%)
  between operations  0.77 us (2%)
    ppermute x17, starting transfers between devices, swap(): return lax.ppermute(x, axis, [(d, d ^ k) for d in range(n)])  16.6 us
    pallas_call x16, Pallas kernels, call(): pl.pallas_call(kernel, out_shape=outs, in_specs=[hbm if i in hbm_in else...  13.9 us
    ppermute x17, waiting for transfers between devices, swap(): return lax.ppermute(x, axis, [(d, d ^ k) for d in range(n)])  8.85 us
  transfers between devices with their start and end apart: 17, of which 7 were waited for; matrix products, arithmetic and copies ran while one was open for 0% of the time, Pallas kernels for 29%

profile of v6, /device:TPU:0, one launch (start us, length us, event | category | flops | bytes accessed | tf_op | source)
XLA Modules:
  0.0 40.2 jit_solution(9082592506497723667)
XLA Ops:
  0.6 4.1 %collective-permute-start.4 = (bf16[12,32,128]{2,1,0:T(8,128)(2,1)}, bf16[12,32,128]{2,1,0:T(8,128)(2,1)S(1)}, u32[]{:S(2)}, u32[]{:S(2)}) collective-permute-start(bf16[12,32,128]{2,1,0:T(8,128)(2,1)} %bitcast.9), channel_id=1, source_target_pairs={{0,2},{1,3},{2,0},{3,1},{4,6},{5,7},{6,4},{7,5},{8,10},{9,11},{10,... | collective-permute-start | bytes 294920 | tf_op jit(solution)/shard_map/ppermute | solution.py:73
  4.7 1.6 %collective-permute-start = (bf16[12,32,128]{2,1,0:T(8,128)(2,1)}, bf16[12,32,128]{2,1,0:T(8,128)(2,1)S(1)}, u32[]{:S(2)}, u32[]{:S(2)}) collective-permute-start(bf16[12,32,128]{2,1,0:T(8,128)(2,1)} %bitcast.10), channel_id=1, source_target_pairs={{0,1},{1,0},{2,3},{3,2},{4,5},{5,4},{6,7},{7,6},{8,9},{9,8},{10,11... | collective-permute-start | bytes 294920 | tf_op jit(solution)/shard_map/ppermute | solution.py:73
  6.7 1.2 %collective-permute-start.2 = (bf16[12,32,128]{2,1,0:T(8,128)(2,1)}, bf16[12,32,128]{2,1,0:T(8,128)(2,1)S(1)}, u32[]{:S(2)}, u32[]{:S(2)}) collective-permute-start(bf16[12,32,128]{2,1,0:T(8,128)(2,1)} %bitcast.13), channel_id=1, source_target_pairs={{0,8},{4,12},{8,0},{12,4},{1,9},{5,13},{9,1},{13,5},{2,10},{6,14},... | collective-permute-start | bytes 294920 | tf_op jit(solution)/shard_map/ppermute | solution.py:73
  8.2 1.3 %stage.1 = (bf16[12,4,48,128]{3,2,1,0:T(8,128)(2,1)S(1)}, bf16[1024,128]{1,0:T(8,128)(2,1)S(1)}, bf16[12,32,128]{2,1,0:T(8,128)(2,1)S(1)}, bf16[12,32,128]{2,1,0:T(8,128)(2,1)S(1)}) custom-call(bf16[12,4,48,128]{3,2,1,0:T(8,128)(2,1)} %bitcast.7, bf16[32,32,128]{2,1,0:T(8,128)(2,1)} %bitcast.8, bf16[12,32,128]{2,1,0:T(8,128)(2,1)} %bitcast.11, ...), custom_call_target="tpu_custom_call" | custom-call | flops 1073741824 | bytes 65536 | tf_op jit(solution)/shard_map/stage/pallas_call | solution.py:52
  9.5 1.4 %outer_grad.1.z_ref = bf16[8,4,48,1536]{3,2,1,0:T(8,128)(2,1)S(1)} custom-call(bf16[12,4,48,128]{3,2,1,0:T(8,128)(2,1)S(1)} %get-tuple-element.43.grad_ref, bf16[1024,128]{1,0:T(8,128)(2,1)S(1)} %get-tuple-element.42.weight_ref.refs_3_), custom_call_target="tpu_custom_call" | custom-call | bytes 65536 | tf_op jit(solution)/shard_map/outer_grad/pallas_call | solution.py:52
  11.6 2.1 %collective-permute-done.2.refs_4_ = bf16[12,32,128]{2,1,0:T(8,128)(2,1)S(1)} collective-permute-done((bf16[12,32,128]{2,1,0:T(8,128)(2,1)}, bf16[12,32,128]{2,1,0:T(8,128)(2,1)S(1)}, u32[]{:S(2)}, u32[]{:S(2)}) %collective-permute-start.2) | collective-permute-done | bytes 98336 | tf_op jit(solution)/shard_map/ppermute | solution.py:73
  13.7 1.9 %outer_mean_near.1 = (bf16[6,4,48,1024]{3,2,1,0:T(8,128)(2,1)S(1)}, f32[1024,128]{1,0:T(8,128)S(1)}, bf16[8,4,48,128]{3,2,1,0:T(8,128)(2,1)S(1)}) custom-call(bf16[12,4,48,128]{3,2,1,0:T(8,128)(2,1)S(1)} %get-tuple-element.43.grad_ref, bf16[12,32,128]{2,1,0:T(8,128)(2,1)S(1)} %get-tuple-element.44.refs_0_, ...), custom_call_target="tpu_custom_call" | custom-call | flops 1073741824 | bytes 65536 | tf_op jit(solution)/shard_map/outer_mean_near/pallas_call | solution.py:52
  15.7 1.3 %outer_mean_middle.1 = (bf16[3,4,48,1024]{3,2,1,0:T(8,128)(2,1)S(1)}, f32[1024,128]{1,0:T(8,128)S(1)}) custom-call(bf16[12,4,48,128]{3,2,1,0:T(8,128)(2,1)S(1)} %get-tuple-element.43.grad_ref, bf16[8,4,48,128]{3,2,1,0:T(8,128)(2,1)S(1)} %get-tuple-element.47.be_ref, f32[1024,128]{1,0:T(8,128)S(1)} %get-tuple-element.48.before_ref, ...), custom_call_target="tpu_custom_call" | custom-call | flops 1073741824 | bytes 65536 | tf_op jit(solution)/shard_map/outer_mean_middle/pallas_call | solution.py:52
  17.0 1.4 %outer_mean_far.1 = (bf16[3,4,48,1024]{3,2,1,0:T(8,128)(2,1)S(1)}, f32[2,256,128]{2,1,0:T(8,128)S(1)}, f32[2,256,128]{2,1,0:T(8,128)S(1)}) custom-call(bf16[12,4,48,128]{3,2,1,0:T(8,128)(2,1)S(1)} %get-tuple-element.43.grad_ref, bf16[8,4,48,128]{3,2,1,0:T(8,128)(2,1)S(1)} %get-tuple-element.47.be_ref, f32[1024,128]{1,0:T(8,128)S(1)} %get-tuple-element.50.before_ref, ...), custom_call_target="tpu_custom_call" | custom-call | flops 1073741824 | bytes 65536 | tf_op jit(solution)/shard_map/outer_mean_far/pallas_call | solution.py:52
  18.5 1.2 %left_grad.1 = (f32[2,12,32,128]{3,2,1,0:T(8,128)S(1)}, bf16[2,12,32,128]{3,2,1,0:T(8,128)(2,1)S(1)}) custom-call(bf16[8,4,48,1536]{3,2,1,0:T(8,128)(2,1)S(1)} %outer_grad.1.z_ref, bf16[8,4,48,128]{3,2,1,0:T(8,128)(2,1)S(1)} %get-tuple-element.47.be_ref), custom_call_target="tpu_custom_call" | custom-call | flops 3221225472 | bytes 65536 | tf_op jit(solution)/shard_map/left_grad/pallas_call | solution.py:52
  20.3 0.8 %collective-permute-start.7 = (bf16[1,256,128]{2,1,0:T(8,128)(2,1)S(1)}, bf16[1,256,128]{2,1,0:T(8,128)(2,1)S(1)}, u32[]{:S(2)}, u32[]{:S(2)}) collective-permute-start(bf16[1,256,128]{2,1,0:T(8,128)(2,1)S(1)} %get-tuple-element.57), channel_id=1, source_target_pairs={{0,8},{4,12},{8,0},{12,4},{1,9},{5,13},{9,1},{13,5},{2,10},{6,14},... | collective-permute-start | bytes 196616 | tf_op jit(solution)/shard_map/ppermute | solution.py:73
  21.1 1.5 %right_grad.1 = (f32[2,12,32,128]{3,2,1,0:T(8,128)S(1)}, bf16[2,12,32,128]{3,2,1,0:T(8,128)(2,1)S(1)}) custom-call(bf16[8,4,48,1536]{3,2,1,0:T(8,128)(2,1)S(1)} %outer_grad.1.z_ref, bf16[12,32,128]{2,1,0:T(8,128)(2,1)S(1)} %get-tuple-element.44.refs_0_, bf16[12,32,128]{2,1,0:T(8,128)(2,1)S(1)} %collective-permute-done.refs_1_, ...), custom_call_target="tpu_custom_call" | custom-call | flops 3221225472 | bytes 65536 | tf_op jit(solution)/shard_map/right_grad/pallas_call | solution.py:52
  22.7 1.9 %collective-permute-done.7.got = bf16[1,256,128]{2,1,0:T(8,128)(2,1)S(1)} collective-permute-done((bf16[1,256,128]{2,1,0:T(8,128)(2,1)S(1)}, bf16[1,256,128]{2,1,0:T(8,128)(2,1)S(1)}, u32[]{:S(2)}, u32[]{:S(2)}) %collective-permute-start.7) | collective-permute-done | bytes 65568 | tf_op jit(solution)/shard_map/ppermute | solution.py:73
  24.6 1.2 %collective-permute-start.9 = (bf16[256,128]{1,0:T(8,128)(2,1)S(1)}, bf16[256,128]{1,0:T(8,128)(2,1)S(1)}, u32[]{:S(2)}, u32[]{:S(2)}) collective-permute-start(bf16[256,128]{1,0:T(8,128)(2,1)S(1)} %weight_row_sum.1.own), channel_id=1, source_target_pairs={{0,2},{1,3},{2,0},{3,1},{4,6},{5,7},{6,4},{7,5},{8,10},{9,11},{10,... | collective-permute-start | bytes 196616 | tf_op jit(solution)/shard_map/ppermute | solution.py:73
  25.9 2.1 %pair_update.1 = bf16[12,4,48,128]{3,2,1,0:T(8,128)(2,1)} custom-call(bf16[6,4,48,1024]{3,2,1,0:T(8,128)(2,1)S(1)} %get-tuple-element.61.refs_0_, bf16[3,4,48,1024]{3,2,1,0:T(8,128)(2,1)S(1)} %get-tuple-element.62.refs_1_, bf16[3,4,48,1024]{3,2,1,0:T(8,128)(2,1)S(1)} %get-tuple-element.63.refs_2_, ...), custom_call_target="tpu_custom_call" | custom-call | flops 17179869184 | bytes 65536 | tf_op jit(solution)/shard_map/pair_update/pallas_call | solution.py:52
  28.0 1.6 %collective-permute-start.13 = (bf16[1,12,32,128]{3,2,1,0:T(8,128)(2,1)S(1)}, bf16[1,12,32,128]{3,2,1,0:T(8,128)(2,1)S(1)}, u32[]{:S(2)}, u32[]{:S(2)}) collective-permute-start(bf16[1,12,32,128]{3,2,1,0:T(8,128)(2,1)S(1)} %get-tuple-element.67), channel_id=1, source_target_pairs={{0,8},{4,12},{8,0},{12,4},{1,9},{5,13},{9,1},{13,5},{2,10},{6,14},... | collective-permute-start | bytes 294920 | tf_op jit(solution)/shard_map/ppermute | solution.py:73
  29.9 1.6 %collective-permute-start.11 = (bf16[256,128]{1,0:T(8,128)(2,1)S(1)}, bf16[256,128]{1,0:T(8,128)(2,1)S(1)}, u32[]{:S(2)}, u32[]{:S(2)}) collective-permute-start(bf16[256,128]{1,0:T(8,128)(2,1)S(1)} %weight_col_sum_2.1.own), channel_id=1, source_target_pairs={{0,1},{1,0},{2,3},{3,2},{4,5},{5,4},{6,7},{7,6},{8,9},{9,8},{10,11... | collective-permute-start | bytes 196616 | tf_op jit(solution)/shard_map/ppermute | solution.py:73
  31.6 0.8 %collective-permute-start.12 = (bf16[1,12,32,128]{3,2,1,0:T(8,128)(2,1)S(1)}, bf16[1,12,32,128]{3,2,1,0:T(8,128)(2,1)S(1)}, u32[]{:S(2)}, u32[]{:S(2)}) collective-permute-start(bf16[1,12,32,128]{3,2,1,0:T(8,128)(2,1)S(1)} %get-tuple-element.71), channel_id=1, source_target_pairs={{0,2},{1,3},{2,0},{3,1},{4,6},{5,7},{6,4},{7,5},{8,10},{9,11},{10,... | collective-permute-start | bytes 294920 | tf_op jit(solution)/shard_map/ppermute | solution.py:73
  32.3 1.9 %collective-permute-done.11.got = bf16[256,128]{1,0:T(8,128)(2,1)S(1)} collective-permute-done((bf16[256,128]{1,0:T(8,128)(2,1)S(1)}, bf16[256,128]{1,0:T(8,128)(2,1)S(1)}, u32[]{:S(2)}, u32[]{:S(2)}) %collective-permute-start.11) | collective-permute-done | bytes 65568 | tf_op jit(solution)/shard_map/ppermute | solution.py:73
  34.4 0.7 %collective-permute-start.15 = (bf16[256,128]{1,0:T(8,128)(2,1)S(1)}, bf16[256,128]{1,0:T(8,128)(2,1)S(1)}, u32[]{:S(2)}, u32[]{:S(2)}) collective-permute-start(bf16[256,128]{1,0:T(8,128)(2,1)S(1)} %weight_col_sum_1.1.refs_0_), channel_id=1, source_target_pairs={{0,8},{4,12},{8,0},{12,4},{1,9},{5,13},{9,1},{13,5},{2,10},{6,14},... | collective-permute-start | bytes 196616 | tf_op jit(solution)/shard_map/ppermute | solution.py:73
  35.1 1.1 %collective-permute-start.14 = (bf16[256,128]{1,0:T(8,128)(2,1)S(1)}, bf16[256,128]{1,0:T(8,128)(2,1)S(1)}, u32[]{:S(2)}, u32[]{:S(2)}) collective-permute-start(bf16[256,128]{1,0:T(8,128)(2,1)S(1)} %weight_col_sum_1.1.refs_0_), channel_id=1, source_target_pairs={{0,4},{4,0},{8,12},{12,8},{1,5},{5,1},{9,13},{13,9},{2,6},{6,2},{1... | collective-permute-start | bytes 196616 | tf_op jit(solution)/shard_map/ppermute | solution.py:73
  36.2 1.9 %collective-permute-done.12.l_got = bf16[1,12,32,128]{3,2,1,0:T(8,128)(2,1)S(1)} collective-permute-done((bf16[1,12,32,128]{3,2,1,0:T(8,128)(2,1)S(1)}, bf16[1,12,32,128]{3,2,1,0:T(8,128)(2,1)S(1)}, u32[]{:S(2)}, u32[]{:S(2)}) %collective-permute-start.12) | collective-permute-done | bytes 98336 | tf_op jit(solution)/shard_map/ppermute | solution.py:73
  38.1 0.8 %left_right_totals.1 = (f32[1,12,32,128]{3,2,1,0:T(8,128)}, f32[1,12,32,128]{3,2,1,0:T(8,128)}) custom-call(f32[1,12,32,128]{3,2,1,0:T(8,128)S(1)} %get-tuple-element.73.l_keep, bf16[1,12,32,128]{3,2,1,0:T(8,128)(2,1)S(1)} %collective-permute-done.12.l_got, f32[1,12,32,128]{3,2,1,0:T(8,128)S(1)} %get-tuple-element.74.r_keep, ...), custom_call_target="tpu_custom_call" | custom-call | flops 1073741824 | bytes 65536 | tf_op jit(solution)/shard_map/left_right_totals/pallas_call | solution.py:52
  39.3 0.8 %weight_place.1 = f32[1024,128]{1,0:T(8,128)} custom-call(bf16[256,128]{1,0:T(8,128)(2,1)S(1)} %weight_col_sum_1.1.refs_0_, bf16[256,128]{1,0:T(8,128)(2,1)S(1)} %collective-permute-done.14.refs_1_, bf16[256,128]{1,0:T(8,128)(2,1)S(1)} %collective-permute-done.15.refs_2_, bf16[256,128]{1,0:T(8,128)(2,1)S(1)} %collective-permute-done.16.refs_3_), custom_call_target="tpu_custom_call" | custom-call | flops 1073741824 | bytes 65536 | tf_op jit(solution)/shard_map/weight_place/pallas_call | solution.py:52
  (28 shorter events, 3.1 us)
Async XLA Ops:
  0.6 10.3 %collective-permute-start.4 = (bf16[12,32,128]{2,1,0:T(8,128)(2,1)}, bf16[12,32,128]{2,1,0:T(8,128)(2,1)S(1)}, u32[]{:S(2)}, u32[]{:S(2)}) collective-permute-start(bf16[12,32,128]{2,1,0:T(8,128)(2,1)} %bitcast.9), channel_id=1, source_target_pairs={{0,2},{1,3},{2,0},{3,1},{4,6},{5,7},{6,4},{7,5},{8,10},{9,11},{10,... | collective-permute-start | bytes 294920 | tf_op jit(solution)/shard_map/ppermute | solution.py:73
  4.7 6.7 %collective-permute-start = (bf16[12,32,128]{2,1,0:T(8,128)(2,1)}, bf16[12,32,128]{2,1,0:T(8,128)(2,1)S(1)}, u32[]{:S(2)}, u32[]{:S(2)}) collective-permute-start(bf16[12,32,128]{2,1,0:T(8,128)(2,1)} %bitcast.10), channel_id=1, source_target_pairs={{0,1},{1,0},{2,3},{3,2},{4,5},{5,4},{6,7},{7,6},{8,9},{9,8},{10,11... | collective-permute-start | bytes 294920 | tf_op jit(solution)/shard_map/ppermute | solution.py:73
  6.3 5.3 %collective-permute-start.3 = (bf16[12,32,128]{2,1,0:T(8,128)(2,1)}, bf16[12,32,128]{2,1,0:T(8,128)(2,1)S(1)}, u32[]{:S(2)}, u32[]{:S(2)}) collective-permute-start(bf16[12,32,128]{2,1,0:T(8,128)(2,1)} %bitcast.12), channel_id=1, source_target_pairs={{0,12},{4,8},{8,4},{12,0},{1,13},{5,9},{9,5},{13,1},{2,14},{6,10},... | collective-permute-start | bytes 294920 | tf_op jit(solution)/shard_map/ppermute | solution.py:73
  6.7 7.0 %collective-permute-start.2 = (bf16[12,32,128]{2,1,0:T(8,128)(2,1)}, bf16[12,32,128]{2,1,0:T(8,128)(2,1)S(1)}, u32[]{:S(2)}, u32[]{:S(2)}) collective-permute-start(bf16[12,32,128]{2,1,0:T(8,128)(2,1)} %bitcast.13), channel_id=1, source_target_pairs={{0,8},{4,12},{8,0},{12,4},{1,9},{5,13},{9,1},{13,5},{2,10},{6,14},... | collective-permute-start | bytes 294920 | tf_op jit(solution)/shard_map/ppermute | solution.py:73
  7.8 5.9 %collective-permute-start.1 = (bf16[12,32,128]{2,1,0:T(8,128)(2,1)}, bf16[12,32,128]{2,1,0:T(8,128)(2,1)S(1)}, u32[]{:S(2)}, u32[]{:S(2)}) collective-permute-start(bf16[12,32,128]{2,1,0:T(8,128)(2,1)} %bitcast.14), channel_id=1, source_target_pairs={{0,4},{4,0},{8,12},{12,8},{1,5},{5,1},{9,13},{13,9},{2,6},{6,2},{1... | collective-permute-start | bytes 294920 | tf_op jit(solution)/shard_map/ppermute | solution.py:73
  10.9 6.1 %collective-permute-start.5 = (bf16[12,32,128]{2,1,0:T(8,128)(2,1)S(1)}, bf16[12,32,128]{2,1,0:T(8,128)(2,1)S(1)}, u32[]{:S(2)}, u32[]{:S(2)}) collective-permute-start(bf16[12,32,128]{2,1,0:T(8,128)(2,1)S(1)} %collective-permute-done.4.refs_0_.refs_2_), channel_id=1, source_target_pairs={{0,1},{1,0},{2,3},{3,2},{4,5},{5,4},{6,7},{7,6},{8,9},{9,8},{10,11... | collective-permute-start | bytes 294920 | tf_op jit(solution)/shard_map/ppermute | solution.py:73
  18.4 1.9 %collective-permute-start.6 = (f32[2,256,128]{2,1,0:T(8,128)S(1)}, f32[2,256,128]{2,1,0:T(8,128)S(1)}, u32[]{:S(2)}, u32[]{:S(2)}) collective-permute-start(f32[2,256,128]{2,1,0:T(8,128)S(1)} %get-tuple-element.52), channel_id=1, source_target_pairs={{0,4},{4,0},{8,12},{12,8},{1,5},{5,1},{9,13},{13,9},{2,6},{6,2},{1... | collective-permute-start | bytes 786440 | tf_op jit(solution)/shard_map/ppermute | solution.py:73
  19.7 11.8 %collective-permute-start.8 = (bf16[2,12,32,128]{3,2,1,0:T(8,128)(2,1)S(1)}, bf16[2,12,32,128]{3,2,1,0:T(8,128)(2,1)S(1)}, u32[]{:S(2)}, u32[]{:S(2)}) collective-permute-start(bf16[2,12,32,128]{3,2,1,0:T(8,128)(2,1)S(1)} %get-tuple-element.54), channel_id=1, source_target_pairs={{0,1},{1,0},{2,3},{3,2},{4,5},{5,4},{6,7},{7,6},{8,9},{9,8},{10,11... | collective-permute-start | bytes 589832 | tf_op jit(solution)/shard_map/ppermute | solution.py:73
  20.3 4.3 %collective-permute-start.7 = (bf16[1,256,128]{2,1,0:T(8,128)(2,1)S(1)}, bf16[1,256,128]{2,1,0:T(8,128)(2,1)S(1)}, u32[]{:S(2)}, u32[]{:S(2)}) collective-permute-start(bf16[1,256,128]{2,1,0:T(8,128)(2,1)S(1)} %get-tuple-element.57), channel_id=1, source_target_pairs={{0,8},{4,12},{8,0},{12,4},{1,9},{5,13},{9,1},{13,5},{2,10},{6,14},... | collective-permute-start | bytes 196616 | tf_op jit(solution)/shard_map/ppermute | solution.py:73
  22.6 3.3 %copy-start = (f32[128]{0:T(128)S(1)}, f32[128]{0:T(128)}, u32[]{:S(2)}) copy-start(f32[128]{0:T(128)} %param.8) | copy-start | bytes 1540
  22.6 5.3 %collective-permute-start.10 = (bf16[2,12,32,128]{3,2,1,0:T(8,128)(2,1)S(1)}, bf16[2,12,32,128]{3,2,1,0:T(8,128)(2,1)S(1)}, u32[]{:S(2)}, u32[]{:S(2)}) collective-permute-start(bf16[2,12,32,128]{3,2,1,0:T(8,128)(2,1)S(1)} %get-tuple-element.59), channel_id=1, source_target_pairs={{0,4},{4,0},{8,12},{12,8},{1,5},{5,1},{9,13},{13,9},{2,6},{6,2},{1... | collective-permute-start | bytes 589832 | tf_op jit(solution)/shard_map/ppermute | solution.py:73
  24.6 5.3 %collective-permute-start.9 = (bf16[256,128]{1,0:T(8,128)(2,1)S(1)}, bf16[256,128]{1,0:T(8,128)(2,1)S(1)}, u32[]{:S(2)}, u32[]{:S(2)}) collective-permute-start(bf16[256,128]{1,0:T(8,128)(2,1)S(1)} %weight_row_sum.1.own), channel_id=1, source_target_pairs={{0,2},{1,3},{2,0},{3,1},{4,6},{5,7},{6,4},{7,5},{8,10},{9,11},{10,... | collective-permute-start | bytes 196616 | tf_op jit(solution)/shard_map/ppermute | solution.py:73
  28.0 10.1 %collective-permute-start.13 = (bf16[1,12,32,128]{3,2,1,0:T(8,128)(2,1)S(1)}, bf16[1,12,32,128]{3,2,1,0:T(8,128)(2,1)S(1)}, u32[]{:S(2)}, u32[]{:S(2)}) collective-permute-start(bf16[1,12,32,128]{3,2,1,0:T(8,128)(2,1)S(1)} %get-tuple-element.67), channel_id=1, source_target_pairs={{0,8},{4,12},{8,0},{12,4},{1,9},{5,13},{9,1},{13,5},{2,10},{6,14},... | collective-permute-start | bytes 294920 | tf_op jit(solution)/shard_map/ppermute | solution.py:73
  29.9 4.3 %collective-permute-start.11 = (bf16[256,128]{1,0:T(8,128)(2,1)S(1)}, bf16[256,128]{1,0:T(8,128)(2,1)S(1)}, u32[]{:S(2)}, u32[]{:S(2)}) collective-permute-start(bf16[256,128]{1,0:T(8,128)(2,1)S(1)} %weight_col_sum_2.1.own), channel_id=1, source_target_pairs={{0,1},{1,0},{2,3},{3,2},{4,5},{5,4},{6,7},{7,6},{8,9},{9,8},{10,11... | collective-permute-start | bytes 196616 | tf_op jit(solution)/shard_map/ppermute | solution.py:73
  31.6 6.6 %collective-permute-start.12 = (bf16[1,12,32,128]{3,2,1,0:T(8,128)(2,1)S(1)}, bf16[1,12,32,128]{3,2,1,0:T(8,128)(2,1)S(1)}, u32[]{:S(2)}, u32[]{:S(2)}) collective-permute-start(bf16[1,12,32,128]{3,2,1,0:T(8,128)(2,1)S(1)} %get-tuple-element.71), channel_id=1, source_target_pairs={{0,2},{1,3},{2,0},{3,1},{4,6},{5,7},{6,4},{7,5},{8,10},{9,11},{10,... | collective-permute-start | bytes 294920 | tf_op jit(solution)/shard_map/ppermute | solution.py:73
  34.3 4.6 %collective-permute-start.16 = (bf16[256,128]{1,0:T(8,128)(2,1)S(1)}, bf16[256,128]{1,0:T(8,128)(2,1)S(1)}, u32[]{:S(2)}, u32[]{:S(2)}) collective-permute-start(bf16[256,128]{1,0:T(8,128)(2,1)S(1)} %weight_col_sum_1.1.refs_0_), channel_id=1, source_target_pairs={{0,12},{4,8},{8,4},{12,0},{1,13},{5,9},{9,5},{13,1},{2,14},{6,10},... | collective-permute-start | bytes 196616 | tf_op jit(solution)/shard_map/ppermute | solution.py:73
  34.4 5.0 %collective-permute-start.15 = (bf16[256,128]{1,0:T(8,128)(2,1)S(1)}, bf16[256,128]{1,0:T(8,128)(2,1)S(1)}, u32[]{:S(2)}, u32[]{:S(2)}) collective-permute-start(bf16[256,128]{1,0:T(8,128)(2,1)S(1)} %weight_col_sum_1.1.refs_0_), channel_id=1, source_target_pairs={{0,8},{4,12},{8,0},{12,4},{1,9},{5,13},{9,1},{13,5},{2,10},{6,14},... | collective-permute-start | bytes 196616 | tf_op jit(solution)/shard_map/ppermute | solution.py:73
  35.1 4.3 %collective-permute-start.14 = (bf16[256,128]{1,0:T(8,128)(2,1)S(1)}, bf16[256,128]{1,0:T(8,128)(2,1)S(1)}, u32[]{:S(2)}, u32[]{:S(2)}) collective-permute-start(bf16[256,128]{1,0:T(8,128)(2,1)S(1)} %weight_col_sum_1.1.refs_0_), channel_id=1, source_target_pairs={{0,4},{4,0},{8,12},{12,8},{1,5},{5,1},{9,13},{13,9},{2,6},{6,2},{1... | collective-permute-start | bytes 196616 | tf_op jit(solution)/shard_map/ppermute | solution.py:73
